TPU v7x, 32 devices: a whole 2x2x4 slice. The times are simulated.
32 devices in a mesh: gx: 8 (over z, x), gy: 4 (over y, core).
Axes of the slice: x: 2, y: 2, z: 4, core: 2. Of those that a mesh axis runs over, the one named last changes fastest.
Arguments:
- checkpoint: float32 [27, 8, 32, 512], P(None, None, 'gx', 'gy'), may hold values from 0.0027 to 0.415, as said below
- rates: float32 [27], replicated, may hold values from 0.8 to 1.7
- wall_mask: int32 [8, 32, 512], P(None, 'gx', 'gy'), may hold values 0 or 1
- cotangent: float32 [27, 8, 32, 512], P(None, None, 'gx', 'gy'), may hold values from -6 to 6
Outputs:
- grad_checkpoint: float32 [27, 8, 32, 512], P(None, None, 'gx', 'gy')
Inputs may be any that keep to these rules, and one draw needn't show every extreme that they name: `checkpoint`: each population lies between 0.6 and 1.4 times its lattice weight.
All inputs are finite; a program needn't handle non-finite values. No bound on the sum of `wall_mask` on one device may be relied on, other than what follows from the above.
Results may differ from a plain program's by a relative error of at most 0.00009.
Values sent between devices are 32-bit elements; how exact they have to be, the bound alone decides.
No kernel may reach another device: no remote copies, remote signals or barrier semaphores. Data moves between devices by JAX's collectives and lax.ppermute only.
A program may use at most 64 MiB of HBM per device.

v0:
```python
import jax
import jax.numpy as jnp
import numpy as np
from jax import lax
from jax.sharding import PartitionSpec as P


def from_behind(block, axis, distance):
    devices = range(lax.axis_size(axis))
    route = [((i - distance) % len(devices), i) for i in devices]
    return lax.ppermute(block, axis, route)


def lattice_tables():
    signs = (-1, 0, 1)
    velocity = [[a, b, c] for a in signs for b in signs for c in signs]
    table = [8.0 / 27.0, 2.0 / 27.0, 1.0 / 54.0, 1.0 / 216.0]
    weights = [table[abs(a) + abs(b) + abs(c)] for a in signs for b in signs for c in signs]
    powers = [[1.0, 1.0, 1.0], [-1.0, 0.0, 1.0], [1.0, 0.0, 1.0]]
    undo = [[0.0, -0.5, 0.5], [1.0, 0.0, -1.0], [0.0, 0.5, 0.5]]
    moment = np.kron(np.kron(powers, powers), powers)
    inverse = np.kron(np.kron(undo, undo), undo)
    return (velocity, weights, moment, inverse)


def collide(incoming, rates, wall_cells):
    velocity, weights, moment, inverse = lattice_tables()
    velocity = jnp.asarray(velocity, jnp.float32)
    weights = jnp.asarray(weights, jnp.float32)
    moment = jnp.asarray(moment, jnp.float32)
    inverse = jnp.asarray(inverse, jnp.float32)
    high = lax.Precision.HIGHEST
    populations = incoming.reshape(27, -1)
    density = jnp.sum(populations, axis=0)
    momentum = jnp.dot(velocity.T, populations, precision=high)
    speeds = momentum / density
    projected = jnp.dot(velocity, speeds, precision=high)
    speed_sq = jnp.sum(speeds * speeds, axis=0)
    equilibrium = (
        weights[:, None]
        * density
        * (1.0 + 3.0 * projected + 4.5 * projected * projected - 1.5 * speed_sq)
    )
    relaxation = jnp.dot(inverse, rates[:, None] * moment, precision=high)
    collided = populations - jnp.dot(relaxation, populations - equilibrium, precision=high)
    reflected = populations[::-1]
    solid = wall_cells.reshape(1, -1)
    return (collided + solid * (reflected - collided)).reshape(incoming.shape)


def wall_field(wall_mask):
    height = lax.broadcasted_iota(jnp.int32, wall_mask.shape, 0)
    boundary = (height == 0) | (height == wall_mask.shape[0] - 1)
    return jnp.where(boundary, 1, wall_mask).astype(jnp.float32)


def stream(field, direction):
    planes, width_x, width_y = (field.shape[1], field.shape[2], field.shape[3])
    upper = 2 if direction > 0 else 0
    lower = 2 - upper
    lattice = field.reshape(3, 3, 3, planes, width_x, width_y)
    forward = lattice[upper]
    backward = lattice[lower]
    from_below = from_behind(forward[:, :, :, -1:, :], "gx", 1)
    from_above = from_behind(backward[:, :, :, :1, :], "gx", -1)
    forward = jnp.concatenate([from_below, forward[:, :, :, :-1, :]], axis=3)
    backward = jnp.concatenate([backward[:, :, :, 1:, :], from_above], axis=3)
    layers = [None, lattice[1], None]
    layers[upper] = forward
    layers[lower] = backward
    lattice = jnp.stack(layers)
    forward = lattice[:, upper]
    backward = lattice[:, lower]
    from_below = from_behind(forward[..., -1:], "gy", 1)
    from_above = from_behind(backward[..., :1], "gy", -1)
    forward = jnp.concatenate([from_below, forward[..., :-1]], axis=4)
    backward = jnp.concatenate([backward[..., 1:], from_above], axis=4)
    layers = [None, lattice[:, 1], None]
    layers[upper] = forward
    layers[lower] = backward
    lattice = jnp.stack(layers, axis=1)
    pieces = []
    for index_z in range(3):
        pieces.append(jnp.roll(lattice[:, :, index_z], direction * (index_z - 1), axis=2))
    return jnp.stack(pieces, axis=2).reshape(field.shape)


def shards(checkpoint, rates, wall_mask, cotangent):
    wall_cells = wall_field(wall_mask)
    back_one = stream(cotangent, -1)
    collided = collide(checkpoint, rates, wall_cells)
    next_state = stream(collided, 1)
    _, pullback = jax.vjp(lambda value: collide(value, rates, wall_cells), next_state)
    grad_next = pullback(back_one)[0]
    back_two = stream(grad_next, -1)
    _, pullback_first = jax.vjp(lambda value: collide(value, rates, wall_cells), checkpoint)
    return pullback_first(back_two)[0]


def solution(mesh):
    in_specs = (P(None, None, "gx", "gy"), P(), P(None, "gx", "gy"), P(None, None, "gx", "gy"))
    out_specs = P(None, None, "gx", "gy")
    return jax.shard_map(shards, mesh=mesh, in_specs=in_specs, out_specs=out_specs, check_vma=False)
```

profile of v0, /device:TPU:0, one launch (start us, length us, event | category | flops | bytes accessed | tf_op | source)
XLA Modules:
  0.0 53.8 jit_solution(3617700966414562182)
XLA Ops:
  0.0 1.1 %fusion.68 = (f32[9,8,4,128]{3,2,1,0:T(4,128)S(1)}, f32[9,8,4,128]{3,2,1,0:T(4,128)S(1)}, f32[9,8,4,128]{3,2,1,0:T(4,128)S(1)}) fusion(f32[27,8,4,128]{3,2,1,0:T(4,128)} %param.19), kind=kLoop, calls=%fused_computation.143 | loop fusion | bytes 884736 | tf_op jit(solution)/shard_map/slice | solution.py:62
  1.2 6.0 %collective-permute-start.1 = (f32[3,3,8,1,128]{4,3,2,1,0:T(1,128)S(1)}, f32[3,3,8,1,128]{4,3,2,1,0:T(1,128)S(1)}, u32[]{:S(2)}, u32[]{:S(2)}) collective-permute-start(f32[3,3,8,1,128]{4,3,2,1,0:T(1,128)S(1)} %slice.277), channel_id=1, source_target_pairs={{4,0},{8,4},{12,8},{16,12},{20,16},{24,20},{28,24},{0,28},{5,1},{9... | collective-permute-start | bytes 110600 | tf_op jit(solution)/shard_map/ppermute | solution.py:11
  7.6 0.9 %rev.10 = f32[27,4096]{1,0:T(8,128)S(1)} reverse(f32[27,4096]{1,0:T(8,128)S(1)} %reshape.97), dimensions={0} | reverse | bytes 884736 | tf_op jit(solution)/shard_map/rev | solution.py:46
  9.5 0.7 %copy-done.2 = s32[8,4,128]{2,1,0:T(4,128)S(1)} copy-done((s32[8,4,128]{2,1,0:T(4,128)S(1)}, s32[8,4,128]{2,1,0:T(4,128)}, u32[]{:S(2)}) %copy-start.2) | copy-done | bytes 16408
  11.2 0.7 %copy-done.3 = f32[27]{0:T(128)S(1)} copy-done((f32[27]{0:T(128)S(1)}, f32[27]{0:T(128)}, u32[]{:S(2)}) %copy-start.3) | copy-done | bytes 132
  11.9 0.8 %multiply_add_fusion = f32[27,4096]{1,0:T(8,128)S(1)} fusion(f32[27,4096]{1,0:T(8,128)S(1)} %rev.10, f32[27,4096]{1,0:T(8,128)S(1)} %reshape.97, f32[27,27]{1,0:T(8,128)S(1)} %fusion.54, f32[27,4096]{1,0:T(8,128)S(1)} %fusion.64, f32[4096]{0:T(1024)S(1)} %broadcast_multiply_fusion.3, f32[4096]{0:T(1024)S(1)} %bitcast.139, f32[27]{0:T(128)S(1)} %copy-done.3, ...), kind=kOutput, calls=%fused_computation.36 | convolution fusion | flops 37269504 | bytes 1821648 | tf_op jit(solution)/shard_map/dot_general | solution.py:45
  12.9 4.8 %collective-permute-start.4 = (f32[3,3,8,1,128]{4,3,2,1,0:T(1,128)S(1)}, f32[3,3,8,1,128]{4,3,2,1,0:T(1,128)S(1)}, u32[]{:S(2)}, u32[]{:S(2)}) collective-permute-start(f32[3,3,8,1,128]{4,3,2,1,0:T(1,128)S(1)} %slice.294), channel_id=1, source_target_pairs={{4,0},{8,4},{12,8},{16,12},{20,16},{24,20},{28,24},{0,28},{5,1},{9... | collective-permute-start | bytes 110600 | tf_op jit(solution)/shard_map/ppermute | solution.py:11
  18.8 1.8 %collective-permute-start.3 = (f32[3,3,8,4,1]{4,3,2,0,1:T(4,128)S(1)}, f32[3,3,8,4,1]{4,3,2,0,1:T(4,128)S(1)}, u32[]{:S(2)}, u32[]{:S(2)}) collective-permute-start(f32[3,3,8,4,1]{4,3,2,0,1:T(4,128)S(1)} %bitcast.147), channel_id=1, source_target_pairs={{1,0},{2,1},{3,2},{0,3},{5,4},{6,5},{7,6},{4,7},{9,8},{10,9},{11,1... | collective-permute-start | bytes 3464 | tf_op jit(solution)/shard_map/ppermute | solution.py:11
  20.6 3.9 %collective-permute-done.5 = f32[3,3,8,1,128]{4,3,2,1,0:T(1,128)S(1)} collective-permute-done((f32[3,3,8,1,128]{4,3,2,1,0:T(1,128)S(1)}, f32[3,3,8,1,128]{4,3,2,1,0:T(1,128)S(1)}, u32[]{:S(2)}, u32[]{:S(2)}) %collective-permute-start.5) | collective-permute-done | bytes 36896 | tf_op jit(solution)/shard_map/ppermute | solution.py:11
  26.1 1.9 %collective-permute-done.6 = f32[3,3,8,4,1]{4,3,2,0,1:T(4,128)S(1)} collective-permute-done((f32[3,3,8,4,1]{4,3,2,0,1:T(4,128)S(1)}, f32[3,3,8,4,1]{4,3,2,0,1:T(4,128)S(1)}, u32[]{:S(2)}, u32[]{:S(2)}) %collective-permute-start.6) | collective-permute-done | bytes 1184 | tf_op jit(solution)/shard_map/ppermute | solution.py:11
  28.2 2.9 %collective-permute-done.7 = f32[3,3,8,4,1]{4,3,2,0,1:T(4,128)S(1)} collective-permute-done((f32[3,3,8,4,1]{4,3,2,0,1:T(4,128)S(1)}, f32[3,3,8,4,1]{4,3,2,0,1:T(4,128)S(1)}, u32[]{:S(2)}, u32[]{:S(2)}) %collective-permute-start.7) | collective-permute-done | bytes 1184 | tf_op jit(solution)/shard_map/ppermute | solution.py:11
  33.4 0.8 %fusion.29 = (f32[4096]{0:T(1024)S(1)}, f32[4096]{0:T(1024)S(1)}, f32[27,4096]{1,0:T(8,128)S(1)}) fusion(f32[4096]{0:T(1024)S(1)} %bitcast.153, f32[27]{0:T(128)S(1)} %copy-done.3, f32[4096]{0:T(1024)S(1)} %broadcast_multiply_fusion.2, f32[27,4096]{1,0:T(8,128)S(1)} %fusion.65, f32[27,27]{1,0:T(8,128)S(1)} %fusion.54, f32[27,4096]{1,0:T(8,128)S(1)} %reshape_reshape.10, ...), kind=kOutput, calls=%fused_computation.49 | convolution fusion | flops 37703680 | bytes 1412048 | tf_op jit(solution)/shard_map/transpose(jvp())/dot_general | solution.py:45
  34.3 0.9 %rev.9 = f32[27,4096]{1,0:T(8,128)S(1)} reverse(f32[27,4096]{1,0:T(8,128)S(1)} %broadcast_multiply_fusion.1), dimensions={0} | reverse | bytes 884736 | tf_op jit(solution)/shard_map/transpose(jvp())/rev | solution.py:46
  35.1 0.6 %multiply_reduce_fusion.2 = (f32[4096]{0:T(1024)S(1)}, f32[3,4096]{1,0:T(4,128)S(1)}) fusion(f32[3,4096]{1,0:T(4,128)S(1)} %get-tuple-element.44, f32[4096]{0:T(1024)S(1)} %multiply_divide_fusion.1, f32[27,3]{1,0:T(8,128)S(1)} %copy-done.1, f32[27,4096]{1,0:T(8,128)S(1)} %fusion.65, f32[27,4096]{1,0:T(8,128)S(1)} %get-tuple-element.45, ...), kind=kOutput, calls=%fused_computation.111 | convolution fusion | flops 5169152 | bytes 1049008 | tf_op jit(solution)/shard_map/transpose(jvp())/dot_general | solution.py:37
  35.8 0.6 %fusion.1 = f32[27,4096]{1,0:T(8,128)S(1)} fusion(f32[27,3]{1,0:T(8,128)S(1)} %copy-done.1, f32[27,4096]{1,0:T(8,128)S(1)} %get-tuple-element.45, f32[27,4096]{1,0:T(8,128)S(1)} %rev.9, f32[4096]{0:T(1024)S(1)} %negate_add_fusion.5, f32[27,4096]{1,0:T(8,128)S(1)} %reshape_reshape.10, f32[4096]{0:T(1024)S(1)} %bitcast.133, ...), kind=kOutput, calls=%fused_computation.4 | convolution fusion | flops 4767744 | bytes 1868100 | tf_op jit(solution)/shard_map/transpose(jvp())/dot_general | solution.py:35
  36.9 4.8 %collective-permute-start.9 = (f32[3,3,8,1,128]{4,3,2,1,0:T(1,128)S(1)}, f32[3,3,8,1,128]{4,3,2,1,0:T(1,128)S(1)}, u32[]{:S(2)}, u32[]{:S(2)}) collective-permute-start(f32[3,3,8,1,128]{4,3,2,1,0:T(1,128)S(1)} %slice.319), channel_id=1, source_target_pairs={{4,0},{8,4},{12,8},{16,12},{20,16},{24,20},{28,24},{0,28},{5,1},{9... | collective-permute-start | bytes 110600 | tf_op jit(solution)/shard_map/ppermute | solution.py:11
  41.8 1.6 %collective-permute-done.8 = f32[3,3,8,1,128]{4,3,2,1,0:T(1,128)S(1)} collective-permute-done((f32[3,3,8,1,128]{4,3,2,1,0:T(1,128)S(1)}, f32[3,3,8,1,128]{4,3,2,1,0:T(1,128)S(1)}, u32[]{:S(2)}, u32[]{:S(2)}) %collective-permute-start.8) | collective-permute-done | bytes 36896 | tf_op jit(solution)/shard_map/ppermute | solution.py:11
  44.0 2.0 %collective-permute-start.11 = (f32[3,3,8,4,1]{4,3,2,0,1:T(4,128)S(1)}, f32[3,3,8,4,1]{4,3,2,0,1:T(4,128)S(1)}, u32[]{:S(2)}, u32[]{:S(2)}) collective-permute-start(f32[3,3,8,4,1]{4,3,2,0,1:T(4,128)S(1)} %bitcast.149), channel_id=1, source_target_pairs={{1,0},{2,1},{3,2},{0,3},{5,4},{6,5},{7,6},{4,7},{9,8},{10,9},{11,1... | collective-permute-start | bytes 3464 | tf_op jit(solution)/shard_map/ppermute | solution.py:11
  46.0 2.8 %collective-permute-done.10 = f32[3,3,8,4,1]{4,3,2,0,1:T(4,128)S(1)} collective-permute-done((f32[3,3,8,4,1]{4,3,2,0,1:T(4,128)S(1)}, f32[3,3,8,4,1]{4,3,2,0,1:T(4,128)S(1)}, u32[]{:S(2)}, u32[]{:S(2)}) %collective-permute-start.10) | collective-permute-done | bytes 1184 | tf_op jit(solution)/shard_map/ppermute | solution.py:11
  49.7 0.8 %fusion.30 = (f32[4096]{0:T(1024)S(1)}, f32[4096]{0:T(1024)S(1)}, f32[27,4096]{1,0:T(8,128)S(1)}) fusion(f32[4096]{0:T(1024)S(1)} %bitcast.141, f32[27]{0:T(128)S(1)} %copy-done.3, f32[4096]{0:T(1024)S(1)} %broadcast_multiply_fusion.3, f32[27,4096]{1,0:T(8,128)S(1)} %fusion.64, f32[27,27]{1,0:T(8,128)S(1)} %fusion.54, f32[27,4096]{1,0:T(8,128)S(1)} %reshape_reshape.12, ...), kind=kOutput, calls=%fused_computation.50 | convolution fusion | flops 37703680 | bytes 1412048 | tf_op jit(solution)/shard_map/transpose(jvp())/dot_general | solution.py:45
  50.6 0.9 %rev.11 = f32[27,4096]{1,0:T(8,128)S(1)} reverse(f32[27,4096]{1,0:T(8,128)S(1)} %broadcast_multiply_fusion), dimensions={0} | reverse | bytes 884736 | tf_op jit(solution)/shard_map/transpose(jvp())/rev | solution.py:46
  51.5 0.6 %multiply_reduce_fusion.1 = (f32[4096]{0:T(1024)S(1)}, f32[3,4096]{1,0:T(4,128)S(1)}) fusion(f32[3,4096]{1,0:T(4,128)S(1)} %get-tuple-element.42, f32[4096]{0:T(1024)S(1)} %multiply_divide_fusion, f32[27,3]{1,0:T(8,128)S(1)} %copy-done.1, f32[27,4096]{1,0:T(8,128)S(1)} %fusion.64, f32[27,4096]{1,0:T(8,128)S(1)} %get-tuple-element.48, ...), kind=kOutput, calls=%fused_computation.110 | convolution fusion | flops 5169152 | bytes 1049008 | tf_op jit(solution)/shard_map/transpose(jvp())/dot_general | solution.py:37
  52.1 0.6 %fusion = f32[27,4096]{1,0:T(8,128)S(1)} fusion(f32[27,3]{1,0:T(8,128)S(1)} %copy-done.1, f32[27,4096]{1,0:T(8,128)S(1)} %get-tuple-element.48, f32[27,4096]{1,0:T(8,128)S(1)} %rev.11, f32[4096]{0:T(1024)S(1)} %negate_add_fusion.4, f32[27,4096]{1,0:T(8,128)S(1)} %reshape_reshape.12, f32[4096]{0:T(1024)S(1)} %bitcast.136, ...), kind=kOutput, calls=%fused_computation.2 | convolution fusion | flops 4767744 | bytes 1868100 | tf_op jit(solution)/shard_map/transpose(jvp())/dot_general | solution.py:35
  52.8 1.1 %reshape.98 = f32[27,8,4,128]{3,2,1,0:T(4,128)} reshape(f32[27,4096]{1,0:T(8,128)S(1)} %fusion) | data formatting | bytes 884736 | tf_op jit(solution)/shard_map/transpose(jvp())/reshape | solution.py:33
  (115 shorter events, 9.6 us)
Async XLA Ops:
  0.0 7.3 %copy-start = (f32[27,8,4,128]{3,2,1,0:T(4,128)S(1)}, f32[27,8,4,128]{3,2,1,0:T(4,128)}, u32[]{:S(2)}) copy-start(f32[27,8,4,128]{3,2,1,0:T(4,128)} %param.16) | copy-start | bytes 1327108
  1.2 16.9 %collective-permute-start.1 = (f32[3,3,8,1,128]{4,3,2,1,0:T(1,128)S(1)}, f32[3,3,8,1,128]{4,3,2,1,0:T(1,128)S(1)}, u32[]{:S(2)}, u32[]{:S(2)}) collective-permute-start(f32[3,3,8,1,128]{4,3,2,1,0:T(1,128)S(1)} %slice.277), channel_id=1, source_target_pairs={{4,0},{8,4},{12,8},{16,12},{20,16},{24,20},{28,24},{0,28},{5,1},{9... | collective-permute-start | bytes 110600 | tf_op jit(solution)/shard_map/ppermute | solution.py:11
  7.3 10.9 %collective-permute-start = (f32[3,3,8,1,128]{4,3,2,1,0:T(1,128)S(1)}, f32[3,3,8,1,128]{4,3,2,1,0:T(1,128)S(1)}, u32[]{:S(2)}, u32[]{:S(2)}) collective-permute-start(f32[3,3,8,1,128]{4,3,2,1,0:T(1,128)S(1)} %slice.274), channel_id=1, source_target_pairs={{28,0},{0,4},{4,8},{8,12},{12,16},{16,20},{20,24},{24,28},{29,1},{... | collective-permute-start | bytes 110600 | tf_op jit(solution)/shard_map/ppermute | solution.py:11
  7.6 0.9 %copy-start.1 = (f32[27,3]{1,0:T(8,128)S(1)}, f32[27,3]{1,0:T(8,128)}, u32[]{:S(2)}) copy-start(f32[27,3]{1,0:T(8,128)} %constant.11.clone) | copy-start | bytes 976
  9.5 0.7 %copy-start.2 = (s32[8,4,128]{2,1,0:T(4,128)S(1)}, s32[8,4,128]{2,1,0:T(4,128)}, u32[]{:S(2)}) copy-start(s32[8,4,128]{2,1,0:T(4,128)} %param.18) | copy-start | bytes 49156
  10.2 0.7 %copy-start.4 = (f32[27]{0:T(128)S(1)}, f32[27]{0:T(128)}, u32[]{:S(2)}) copy-start(f32[27]{0:T(128)} %param.17) | copy-start | bytes 328
  10.2 0.7 %copy-start.5 = (f32[27,27]{1,0:T(8,128)S(1)}, f32[27,27]{1,0:T(8,128)}, u32[]{:S(2)}) copy-start(f32[27,27]{1,0:T(8,128)} %constant.27.clone) | copy-start | bytes 8752
  10.2 0.7 %copy-start.6 = (f32[27,27]{1,0:T(8,128)S(1)}, f32[27,27]{1,0:T(8,128)}, u32[]{:S(2)}) copy-start(f32[27,27]{1,0:T(8,128)} %constant.28.clone) | copy-start | bytes 8752
  11.2 0.7 %copy-start.3 = (f32[27]{0:T(128)S(1)}, f32[27]{0:T(128)}, u32[]{:S(2)}) copy-start(f32[27]{0:T(128)} %constant.26.clone) | copy-start | bytes 328
  12.9 7.7 %collective-permute-start.4 = (f32[3,3,8,1,128]{4,3,2,1,0:T(1,128)S(1)}, f32[3,3,8,1,128]{4,3,2,1,0:T(1,128)S(1)}, u32[]{:S(2)}, u32[]{:S(2)}) collective-permute-start(f32[3,3,8,1,128]{4,3,2,1,0:T(1,128)S(1)} %slice.294), channel_id=1, source_target_pairs={{4,0},{8,4},{12,8},{16,12},{20,16},{24,20},{28,24},{0,28},{5,1},{9... | collective-permute-start | bytes 110600 | tf_op jit(solution)/shard_map/ppermute | solution.py:11
  17.8 6.7 %collective-permute-start.5 = (f32[3,3,8,1,128]{4,3,2,1,0:T(1,128)S(1)}, f32[3,3,8,1,128]{4,3,2,1,0:T(1,128)S(1)}, u32[]{:S(2)}, u32[]{:S(2)}) collective-permute-start(f32[3,3,8,1,128]{4,3,2,1,0:T(1,128)S(1)} %slice.297), channel_id=1, source_target_pairs={{28,0},{0,4},{4,8},{8,12},{12,16},{16,20},{20,24},{24,28},{29,1},{... | collective-permute-start | bytes 110600 | tf_op jit(solution)/shard_map/ppermute | solution.py:11
  18.5 7.1 %collective-permute-start.2 = (f32[3,3,8,4,1]{4,3,2,0,1:T(4,128)S(1)}, f32[3,3,8,4,1]{4,3,2,0,1:T(4,128)S(1)}, u32[]{:S(2)}, u32[]{:S(2)}) collective-permute-start(f32[3,3,8,4,1]{4,3,2,0,1:T(4,128)S(1)} %slice.279), channel_id=1, source_target_pairs={{3,0},{0,1},{1,2},{2,3},{7,4},{4,5},{5,6},{6,7},{11,8},{8,9},{9,10... | collective-permute-start | bytes 3464 | tf_op jit(solution)/shard_map/ppermute | solution.py:11
  18.8 7.0 %collective-permute-start.3 = (f32[3,3,8,4,1]{4,3,2,0,1:T(4,128)S(1)}, f32[3,3,8,4,1]{4,3,2,0,1:T(4,128)S(1)}, u32[]{:S(2)}, u32[]{:S(2)}) collective-permute-start(f32[3,3,8,4,1]{4,3,2,0,1:T(4,128)S(1)} %bitcast.147), channel_id=1, source_target_pairs={{1,0},{2,1},{3,2},{0,3},{5,4},{6,5},{7,6},{4,7},{9,8},{10,9},{11,1... | collective-permute-start | bytes 3464 | tf_op jit(solution)/shard_map/ppermute | solution.py:11
  24.9 3.1 %collective-permute-start.6 = (f32[3,3,8,4,1]{4,3,2,0,1:T(4,128)S(1)}, f32[3,3,8,4,1]{4,3,2,0,1:T(4,128)S(1)}, u32[]{:S(2)}, u32[]{:S(2)}) collective-permute-start(f32[3,3,8,4,1]{4,3,2,0,1:T(4,128)S(1)} %bitcast.148), channel_id=1, source_target_pairs={{1,0},{2,1},{3,2},{0,3},{5,4},{6,5},{7,6},{4,7},{9,8},{10,9},{11,1... | collective-permute-start | bytes 3464 | tf_op jit(solution)/shard_map/ppermute | solution.py:11
  25.1 6.1 %collective-permute-start.7 = (f32[3,3,8,4,1]{4,3,2,0,1:T(4,128)S(1)}, f32[3,3,8,4,1]{4,3,2,0,1:T(4,128)S(1)}, u32[]{:S(2)}, u32[]{:S(2)}) collective-permute-start(f32[3,3,8,4,1]{4,3,2,0,1:T(4,128)S(1)} %slice.304), channel_id=1, source_target_pairs={{3,0},{0,1},{1,2},{2,3},{7,4},{4,5},{5,6},{6,7},{11,8},{8,9},{9,10... | collective-permute-start | bytes 3464 | tf_op jit(solution)/shard_map/ppermute | solution.py:11
  36.6 6.7 %collective-permute-start.8 = (f32[3,3,8,1,128]{4,3,2,1,0:T(1,128)S(1)}, f32[3,3,8,1,128]{4,3,2,1,0:T(1,128)S(1)}, u32[]{:S(2)}, u32[]{:S(2)}) collective-permute-start(f32[3,3,8,1,128]{4,3,2,1,0:T(1,128)S(1)} %slice.314), channel_id=1, source_target_pairs={{28,0},{0,4},{4,8},{8,12},{12,16},{16,20},{20,24},{24,28},{29,1},{... | collective-permute-start | bytes 110600 | tf_op jit(solution)/shard_map/ppermute | solution.py:11
  36.9 6.5 %collective-permute-start.9 = (f32[3,3,8,1,128]{4,3,2,1,0:T(1,128)S(1)}, f32[3,3,8,1,128]{4,3,2,1,0:T(1,128)S(1)}, u32[]{:S(2)}, u32[]{:S(2)}) collective-permute-start(f32[3,3,8,1,128]{4,3,2,1,0:T(1,128)S(1)} %slice.319), channel_id=1, source_target_pairs={{4,0},{8,4},{12,8},{16,12},{20,16},{24,20},{28,24},{0,28},{5,1},{9... | collective-permute-start | bytes 110600 | tf_op jit(solution)/shard_map/ppermute | solution.py:11
  43.8 5.0 %collective-permute-start.10 = (f32[3,3,8,4,1]{4,3,2,0,1:T(4,128)S(1)}, f32[3,3,8,4,1]{4,3,2,0,1:T(4,128)S(1)}, u32[]{:S(2)}, u32[]{:S(2)}) collective-permute-start(f32[3,3,8,4,1]{4,3,2,0,1:T(4,128)S(1)} %slice.321), channel_id=1, source_target_pairs={{3,0},{0,1},{1,2},{2,3},{7,4},{4,5},{5,6},{6,7},{11,8},{8,9},{9,10... | collective-permute-start | bytes 3464 | tf_op jit(solution)/shard_map/ppermute | solution.py:11
  44.0 4.9 %collective-permute-start.11 = (f32[3,3,8,4,1]{4,3,2,0,1:T(4,128)S(1)}, f32[3,3,8,4,1]{4,3,2,0,1:T(4,128)S(1)}, u32[]{:S(2)}, u32[]{:S(2)}) collective-permute-start(f32[3,3,8,4,1]{4,3,2,0,1:T(4,128)S(1)} %bitcast.149), channel_id=1, source_target_pairs={{1,0},{2,1},{3,2},{0,3},{5,4},{6,5},{7,6},{4,7},{9,8},{10,9},{11,1... | collective-permute-start | bytes 3464 | tf_op jit(solution)/shard_map/ppermute | solution.py:11
where the time goes:
time: 54.6 us; the launch traced here: 53.8 us
  starting transfers between devices  20.2 us (37%)
  waiting for transfers between devices  13.1 us (24%)
  local copies, waits for them, and re-layouts  9.71 us (18%)
  matrix products  7.04 us (13%)
  other arithmetic  2.96 us (5%)
  between operations  0.84 us (2%)
    ppermute x12, starting transfers between devices, from_behind(): return lax.ppermute(block, axis, route)  20.2 us
    ppermute x12, waiting for transfers between devices, from_behind(): return lax.ppermute(block, axis, route)  13.1 us
    rev x3, local copies, waits for them, and re-layouts, collide(): reflected = populations[::-1]  2.58 us
    dot_general x3, matrix products, collide(): jnp.dot(relaxation, populations - equilibrium, precision=high)  2.39 us
    dot_general x4, matrix products, collide(): projected = jnp.dot(velocity, speeds, precision=high)  2.36 us
    unnamed x14, local copies, waits for them, and re-layouts  2.05 us
    dot_general x4, matrix products, collide(): momentum = jnp.dot(velocity.T, populations, precision=high)  2.03 us
    reshape x2, local copies, waits for them, and re-layouts, collide(): populations = incoming.reshape(27, -1)  1.23 us
  transfers between devices with their start and end apart: 12, of which 5 were waited for; matrix products, arithmetic and copies ran while one was open for 11% of the time, Pallas kernels for 0%

commit v1 on v0

v1 whole, which is shorter than its diff:
```python
import functools
import jax
import jax.numpy as jnp
from jax import lax
from jax.experimental import pallas as pl
from jax.experimental.pallas import tpu as pltpu
from jax.sharding import PartitionSpec as P

F32 = jnp.float32
SIGNS = (-1, 0, 1)
Q = [(a, b, c) for a in SIGNS for b in SIGNS for c in SIGNS]


def qi(a, b, c):
    return 9 * (a + 1) + 3 * (b + 1) + (c + 1)


def mi(i, j, k):
    return 9 * i + 3 * j + k


NNZ = [(i > 0) + (j > 0) + (k > 0) for i in range(3) for j in range(3) for k in range(3)]


def slots(rows):
    first, second, sums = [], [], []
    for q, (a, b, c) in enumerate(Q):
        for x in range(rows):
            left = (a >= 0 and x == 0) or (a == 1 and x == 1)
            right = (a <= 0 and x == rows - 1) or (a == -1 and x == rows - 2)
            (first if left or right else second).append((("v", q, x), b))
    for x in range(rows):
        second.append((("w", x), 0))
    for a in SIGNS:
        for b in SIGNS:
            for s in range(2):
                for x in range(rows):
                    sums.append((("s", a, b, s, x), -b))
    table = {}
    groups = [first + sums[64:], second, sums[:64]]
    for g, group in enumerate(groups):
        for i, (key, kind) in enumerate(group):
            table[key] = (g, 2 * i, kind)
    return table, 2 * len(first)


def turn(v, shift, axis):
    shift = shift % v.shape[axis]
    return v if shift == 0 else pltpu.roll(v, shift, axis)


def lanes():
    return lax.broadcasted_iota(jnp.int32, (8, 128), 1)


def outgoing(block, lane, kind):
    return turn(block, {0: lane + 1, 1: lane, -1: lane + 2}[kind], 1)


def incoming(packed, lane, kind):
    return turn(packed, {0: 127, 1: 0, -1: 126}[kind] - lane, 1)


def shift_y(main, outer, b, lane):
    if b == 0:
        return main, outer
    edge = lane == (127 if b == 1 else 0)
    rm, ro = turn(main, -b, 1), turn(outer, -b, 1)
    return jnp.where(edge, ro, rm), jnp.where(edge, rm, ro)


def along(values, pass_):
    values = list(values)
    for step in (1, 3, 9):
        for start in range(27):
            if (start // step) % 3 == 0:
                at = (start, start + step, start + 2 * step)
                for i, new in zip(at, pass_(*[values[j] for j in at])):
                    values[i] = new
    return values


def moments(values):
    def pass_(lo, mid, hi):
        both = lo + hi
        return both + mid, hi - lo, both
    return along(values, pass_)


def dual_moments(values):
    return along(values, lambda lo, mid, hi: (mid, hi - lo, (hi - mid) + (lo - mid)))


def from_moments(values):
    return along(values, lambda m0, m1, m2: (m2 - m1, m0 - (m2 + m2), m2 + m1))


def from_dual(values):
    def pass_(z0, z1, z2):
        both = z0 + z2
        return both - z1, z0, both + z1
    return along(values, pass_)


def collide(f, solid, scale):
    m = moments(f)
    rho = m[0]
    inverse = 1.0 / rho
    jx, jy, jz = m[mi(1, 0, 0)], m[mi(0, 1, 0)], m[mi(0, 0, 1)]
    ux, uy, uz = jx * inverse, jy * inverse, jz * inverse
    xx, yy, zz = jx * ux, jy * uy, jz * uz
    third = rho * (1.0 / 3.0)
    ninth = rho * (1.0 / 9.0)
    e = [None] * 27
    e[mi(2, 0, 0)], e[mi(0, 2, 0)], e[mi(0, 0, 2)] = third + xx, third + yy, third + zz
    e[mi(1, 1, 0)], e[mi(1, 0, 1)], e[mi(0, 1, 1)] = jx * uy, jx * uz, jy * uz
    jx3, jy3, jz3 = jx * (1.0 / 3.0), jy * (1.0 / 3.0), jz * (1.0 / 3.0)
    e[mi(1, 2, 0)] = e[mi(1, 0, 2)] = jx3
    e[mi(2, 1, 0)] = e[mi(0, 1, 2)] = jy3
    e[mi(2, 0, 1)] = e[mi(0, 2, 1)] = jz3
    e[mi(2, 2, 0)] = ninth + (xx + yy) * (1.0 / 3.0)
    e[mi(2, 0, 2)] = ninth + (xx + zz) * (1.0 / 3.0)
    e[mi(0, 2, 2)] = ninth + (yy + zz) * (1.0 / 3.0)
    e[mi(2, 1, 1)] = e[mi(0, 1, 1)] * (1.0 / 3.0)
    e[mi(1, 2, 1)] = e[mi(1, 0, 1)] * (1.0 / 3.0)
    e[mi(1, 1, 2)] = e[mi(1, 1, 0)] * (1.0 / 3.0)
    e[mi(1, 2, 2)], e[mi(2, 1, 2)], e[mi(2, 2, 1)] = jx * (1.0 / 9.0), jy * (1.0 / 9.0), jz * (1.0 / 9.0)
    e[mi(2, 2, 2)] = (third + (xx + yy + zz)) * (1.0 / 9.0)
    z = []
    for i in range(27):
        if i in (0, 1, 3, 9):
            z.append(jnp.zeros_like(rho))
        else:
            z.append((m[i] if e[i] is None else m[i] - e[i]) * scale[i])
    h = from_moments(z)
    out = [jnp.where(solid, f[26 - q], f[q] - h[q]) for q in range(27)]
    return out, (ux, uy, uz)


def pull_back(v, u, solid, scale):
    ux, uy, uz = u
    z = [y * s for y, s in zip(dual_moments(v), scale)]

    def at(i, j, k):
        return z[mi(i, j, k)]

    third = 1.0 / 3.0
    top = at(2, 2, 2) * third
    d_xy, d_xz, d_yz = at(2, 2, 0) + top, at(2, 0, 2) + top, at(0, 2, 2) + top
    q_xx = at(2, 0, 0) + (at(2, 2, 0) + d_xz) * third
    q_yy = at(0, 2, 0) + (at(0, 2, 2) + d_xy) * third
    q_zz = at(0, 0, 2) + (at(2, 0, 2) + d_yz) * third
    base = at(0, 0, 0) + (q_xx + (at(0, 2, 0) + at(0, 0, 2) + at(0, 2, 2) * third)) * third
    b_x = at(1, 0, 0) + (at(1, 2, 0) + at(1, 0, 2) + at(1, 2, 2) * third) * third
    b_y = at(0, 1, 0) + (at(2, 1, 0) + at(0, 1, 2) + at(2, 1, 2) * third) * third
    b_z = at(0, 0, 1) + (at(2, 0, 1) + at(0, 2, 1) + at(2, 2, 1) * third) * third
    q_xy = at(1, 1, 0) + at(1, 1, 2) * third
    q_xz = at(1, 0, 1) + at(1, 2, 1) * third
    q_yz = at(0, 1, 1) + at(2, 1, 1) * third
    p_x = (q_xx + q_xx) * ux + q_xy * uy + q_xz * uz
    p_y = q_xy * ux + (q_yy + q_yy) * uy + q_yz * uz
    p_z = q_xz * ux + q_yz * uy + (q_zz + q_zz) * uz
    quad = (p_x * ux + p_y * uy + p_z * uz) * 0.5
    z[0] = z[0] - (base - quad)
    z[mi(1, 0, 0)] = z[mi(1, 0, 0)] - (b_x + p_x)
    z[mi(0, 1, 0)] = z[mi(0, 1, 0)] - (b_y + p_y)
    z[mi(0, 0, 1)] = z[mi(0, 0, 1)] - (b_z + p_z)
    h = from_dual(z)
    return [jnp.where(solid, v[26 - q], v[q] - h[q]) for q in range(27)]


def scales(rates_ref):
    return [rates_ref[i] * (0.5 ** NNZ[i]) for i in range(27)]


def first_kernel(rows, rates, f, wall, cot, sums, speed, solid_out, packed):
    scale = scales(rates)
    plane = lax.broadcasted_iota(jnp.int32, (8, 128), 0)
    boundary = (plane == 0) | (plane == 7)
    lane = lanes()
    table, _ = slots(rows)
    for x in range(rows):
        at = pl.ds(x, 8, stride=rows)
        solid = boundary | (wall[at, :] == 1)
        solid_out[x] = jnp.where(solid, 1.0, 0.0)
        out, u = collide([f[q, at, :] for q in range(27)], solid, scale)
        for k in range(3):
            speed[k, x] = u[k]
        for a in SIGNS:
            for b in SIGNS:
                low = turn(out[qi(a, b, -1)], -1, 0)
                high = turn(out[qi(a, b, 1)], 1, 0)
                i = 2 * (3 * (a + 1) + b + 1)
                sums[i, x] = out[qi(a, b, 0)] + (low + high)
                sums[i + 1, x] = high - low
    pieces = [jnp.zeros((8, 128), F32) for _ in range(3)]
    for key, (g, i, kind) in table.items():
        if key[0] == "v":
            block = cot[key[1], pl.ds(key[2], 8, stride=rows), :]
        elif key[0] == "w":
            block = solid_out[key[1]]
        else:
            block = sums[2 * (3 * (key[1] + 1) + key[2] + 1) + key[3], key[4]]
        mine = (lane == i) | (lane == i + 1)
        pieces[g] = jnp.where(mine, outgoing(block, i, kind), pieces[g])
    for g in range(3):
        packed[g] = pieces[g]


def edge_rows(rows, side):
    near, far = (0, 1) if side == 1 else (rows - 1, rows - 2)
    keys = [(q, near) for q, c in enumerate(Q) if c[0] == 0]
    keys += [(q, near) for q, c in enumerate(Q) if c[0] == side]
    return keys + [(q, far) for q, c in enumerate(Q) if c[0] == side]


def second_kernel(rows, cot, sums, solid_in, from_left, from_right, to_left, to_right, own, merged):
    lane = lanes()
    table, used = slots(rows)
    halo = []
    for g in range(3):
        takes_left = jnp.zeros((8, 128), jnp.bool_)
        for key, (h, i, kind) in table.items():
            if h == g and kind <= 0:
                takes_left = takes_left | (lane == i)
            if h == g and kind == -1:
                takes_left = takes_left | (lane == i + 1)
        halo.append(jnp.where(takes_left, from_left[g], from_right[g]))
        merged[g] = halo[g]

    def outer(key):
        g, i, kind = table[key]
        return incoming(halo[g], i, kind)

    def both(a, x):
        parts = {}
        for b in SIGNS:
            for s in range(2):
                i = 2 * (3 * (a + 1) + b + 1) + s
                parts[b, s] = shift_y(sums[i, x], outer(("s", a, b, s, x)), -b, lane)
        result = []
        for n in range(2):
            result.append((
                parts[0, 0][n] + (parts[-1, 0][n] + parts[1, 0][n]),
                parts[1, 0][n] - parts[-1, 0][n],
                parts[0, 1][n] + (parts[-1, 1][n] + parts[1, 1][n]),
            ))
        return result

    t = {(a, x): both(a, x) for a in SIGNS for x in range(rows)}

    def total(x, n):
        terms = [(a, t[a, x - a][n]) for a in SIGNS if 0 <= x - a < rows]
        density = functools.reduce(jnp.add, [v[0] for _, v in terms])
        along_y = functools.reduce(jnp.add, [v[1] for _, v in terms])
        along_z = functools.reduce(jnp.add, [v[2] for _, v in terms])
        moving = [(a, v[0]) for a, v in terms if a]
        along_x = jnp.zeros((8, 128), F32)
        for a, v in moving:
            along_x = along_x + v if a == 1 else along_x - v
        return density, along_x, along_y, along_z

    for x in range(-1, rows + 1):
        for n in range(2):
            for k, v in enumerate(total(x, n)):
                own[k, 2 * (x + 1) + n] = v

    for side, message in ((1, to_left), (-1, to_right)):
        near, far = (0, 1) if side == 1 else (rows - 1, rows - 2)
        for k, (q, x) in enumerate(edge_rows(rows, side)):
            message[k] = cot[q, pl.ds(x, 8, stride=rows), :]
        extra = []
        for n in range(2):
            row = list(t[-side, near][n])
            still, moved = t[0, near][n], t[-side, far][n]
            row += [still[0] + moved[0], moved[0] if side == -1 else -moved[0]]
            row += [still[1] + moved[1], still[2] + moved[2]]
            row.append(solid_in[near] if n == 0 else outer(("w", near)))
            extra.append(row)
        columns = halo[0]
        for k in range(8):
            message[27 + k] = extra[0][k]
            i = used + 2 * k
            columns = jnp.where((lane == i) | (lane == i + 1), turn(extra[1][k], i + 1, 1), columns)
        message[35] = columns


def third_kernel(rows, rates, cot, speed, solid_in, own, merged, from_low, from_high, out, v1, g1, extra):
    scale = scales(rates)
    lane = lanes()
    table, used = slots(rows)
    ring = rows + 2
    remote = {}
    for side, message in ((1, from_high), (-1, from_low)):
        for k, (q, x) in enumerate(edge_rows(rows, side)):
            g, i, kind = table["v", q, x]
            remote[q, x + side * rows] = (message, k, i, kind)
    for q, (a, b, c) in enumerate(Q):
        for x in range(-1, rows + 1):
            source = x + a
            if 0 <= source < rows:
                main = cot[q, pl.ds(source, 8, stride=rows), :]
                g, i, kind = table["v", q, source]
                outer = incoming(merged[g], i, kind)
            else:
                message, k, i, kind = remote[q, source]
                main = message[k]
                outer = incoming(message[35], i, kind)
            main, outer = turn(main, -c, 0), turn(outer, -c, 0)
            main, outer = shift_y(main, outer, b, lane)
            v1[q, 2 * (x + 1)] = main
            v1[q, 2 * (x + 1) + 1] = outer
    for x in range(-1, rows + 1):
        for n in range(2):
            total = [own[k, 2 * (x + 1) + n] for k in range(4)]
            for side, message in ((1, from_high), (-1, from_low)):
                near = rows - 1 if side == 1 else 0

                def got(k):
                    if n == 0:
                        return message[27 + k]
                    return incoming(message[35], used + 2 * k, 0)

                if x == near:
                    total = [total[0] + got(0), total[1] - got(0) if side == 1 else total[1] + got(0),
                             total[2] + got(1), total[3] + got(2)]
                if x == near + side:
                    total = [total[k] + got(3 + k) for k in range(4)]
                    wall = got(7)
            if 0 <= x < rows:
                if n == 0:
                    wall = solid_in[x]
                else:
                    g, i, kind = table["w", x]
                    wall = incoming(merged[g], i, kind)
            inverse = 1.0 / total[0]
            for k in range(3):
                extra[k, 2 * (x + 1) + n] = total[k + 1] * inverse
            extra[3, 2 * (x + 1) + n] = wall

    def one(r, _):
        v = [v1[q, r] for q in range(27)]
        u = [extra[k, r] for k in range(3)]
        g = pull_back(v, u, extra[3, r] > 0.5, scale)
        for q in range(27):
            g1[q, r] = g[q]
        return 0

    lax.fori_loop(0, 2 * ring, one, 0)
    for x in range(rows):
        v = []
        for q, (a, b, c) in enumerate(Q):
            r = 2 * (x + a + 1)
            main = g1[q, r]
            if b:
                main = shift_y(main, g1[q, r + 1], b, lane)[0]
            v.append(turn(main, -c, 0))
        result = pull_back(v, [speed[k, x] for k in range(3)], solid_in[x] > 0.5, scale)
        for q in range(27):
            out[q, pl.ds(x, 8, stride=rows), :] = result[q]


def call(kernel, name, out_shapes, scratch, operands, smem_first):
    vmem = pl.BlockSpec(memory_space=pltpu.VMEM)
    specs = [vmem] * len(operands)
    if smem_first:
        specs[0] = pl.BlockSpec(memory_space=pltpu.SMEM)
    return pl.pallas_call(
        kernel,
        out_shape=[jax.ShapeDtypeStruct(s, F32) for s in out_shapes],
        in_specs=specs,
        out_specs=[vmem] * len(out_shapes),
        scratch_shapes=[pltpu.VMEM(s, F32) for s in scratch],
        compiler_params=pltpu.CompilerParams(vmem_limit_bytes=32 * 1024 * 1024),
        name=name,
    )(*operands)


def ring(block, axis, step):
    size = lax.axis_size(axis)
    return lax.ppermute(block, axis, [(i, (i + step) % size) for i in range(size)])


def shards(checkpoint, rates, wall_mask, cotangent):
    planes, rows, width = checkpoint.shape[1:]
    f = checkpoint.reshape(27, planes * rows, width)
    cot = cotangent.reshape(27, planes * rows, width)
    wall = wall_mask.reshape(planes * rows, width)
    tile = (planes, width)
    sums, speed, solid, packed = call(
        functools.partial(first_kernel, rows), "collide",
        [(18, rows) + tile, (3, rows) + tile, (rows,) + tile, (3,) + tile], [],
        (rates, f, wall, cot), True)
    from_right = ring(packed, "gy", -1)
    from_left = ring(packed, "gy", 1)
    to_left, to_right, own, merged = call(
        functools.partial(second_kernel, rows), "pack",
        [(36,) + tile, (36,) + tile, (4, 2 * rows + 4) + tile, (3,) + tile], [],
        (cot, sums, solid, from_left, from_right), False)
    from_high = ring(to_left, "gx", -1)
    from_low = ring(to_right, "gx", 1)
    (out,) = call(
        functools.partial(third_kernel, rows), "gradient",
        [(27, planes * rows, width)],
        [(27, 2 * rows + 4) + tile, (27, 2 * rows + 4) + tile, (4, 2 * rows + 4) + tile],
        (rates, cot, speed, solid, own, merged, from_low, from_high), True)
    return out.reshape(checkpoint.shape)


def solution(mesh):
    in_specs = (P(None, None, "gx", "gy"), P(), P(None, "gx", "gy"), P(None, None, "gx", "gy"))
    out_specs = P(None, None, "gx", "gy")
    return jax.shard_map(shards, mesh=mesh, in_specs=in_specs, out_specs=out_specs, check_vma=False)
```

time: 54.6 us -> 25.2 us (0.46)
  starting transfers between devices: 20.2 us -> 7.24 us
  matrix products: 7.04 us -> 0 us
  Pallas kernels: 0 us -> 6.83 us
  local copies, waits for them, and re-layouts: 9.71 us -> 3.4 us
  waiting for transfers between devices: 13.1 us -> 7.46 us
  other arithmetic: 2.96 us -> 0 us
  between operations: 0.84 us -> 0.02 us
    ppermute x12 -> x4, starting transfers between devices: 20.2 us -> 7.24 us  [ring(): lax.ppermute(block, axis, [(i, (i + step) % size) for i in range(size)])]
    dot_general x12 -> x0, matrix products: 7.04 us -> none  [the longest x3 2.39 us: collide(): jnp.dot(relaxation, populations - equilibrium, precision=high)]
    pallas_call x0 -> x3, Pallas kernels: none -> 6.83 us  [call(): pl.pallas_call(kernel, out_shape=[jax.ShapeDtypeStruct(s, F32) for s in o...]
    ppermute x12 -> x4, waiting for transfers between devices: 13.1 us -> 7.46 us  [ring(): lax.ppermute(block, axis, [(i, (i + step) % size) for i in range(size)])]
    slice x32 -> x0, local copies, waits for them, and re-layouts: 2.7 us -> none  [the longest x2 1.19 us: stream(): forward = lattice[upper]]
    another operation x25 -> x0, other arithmetic: 2.59 us -> none  [the longest x9 1.21 us: stream(): lattice = jnp.stack(layers, axis=1)]
    rev x3 -> x0, local copies, waits for them, and re-layouts: 2.58 us -> none  [collide(): reflected = populations[::-1]]
    unnamed x14 -> x10, local copies, waits for them, and re-layouts: 2.05 us -> 3.4 us
  transfers between devices with their start and end apart: 12 -> 4, of which waited for: 5 -> 4; matrix products, arithmetic and copies ran while one was open for 11% -> 0% of each run, Pallas kernels for 0% -> 0%
where the time goes in v1:
time: 25.2 us; the launch traced here: 24.9 us
  waiting for transfers between devices  7.46 us (30%)
  starting transfers between devices  7.24 us (29%)
  Pallas kernels  6.83 us (27%)
  local copies, waits for them, and re-layouts  3.4 us (13%)
    ppermute x4, waiting for transfers between devices, ring(): lax.ppermute(block, axis, [(i, (i + step) % size) for i in range(size)])  7.46 us
    ppermute x4, starting transfers between devices, ring(): lax.ppermute(block, axis, [(i, (i + step) % size) for i in range(size)])  7.24 us
    pallas_call x3, Pallas kernels, call(): pl.pallas_call(kernel, out_shape=[jax.ShapeDtypeStruct(s, F32) for s in o...  6.83 us
    unnamed x10, local copies, waits for them, and re-layouts  3.4 us
  transfers between devices with their start and end apart: 4, of which 4 were waited for; matrix products, arithmetic and copies ran while one was open for 0% of the time, Pallas kernels for 0%

profile of v1, /device:TPU:0, one launch (start us, length us, event | category | flops | bytes accessed | tf_op | source)
XLA Modules:
  0.0 24.9 jit_solution(4806697078545028316)
XLA Ops:
  0.0 0.0 copy-start.4
  0.0 0.7 %copy-done.4 = f32[27]{0:T(128)S(1)} copy-done((f32[27]{0:T(128)S(1)}, f32[27]{0:T(128)}, u32[]{:S(2)}) %copy-start.4) | copy-done | bytes 132
  0.7 0.0 copy-start
  0.7 1.0 %copy-done = f32[27,8,4,128]{3,2,1,0:T(4,128)S(1)} copy-done((f32[27,8,4,128]{3,2,1,0:T(4,128)S(1)}, f32[27,8,4,128]{3,2,1,0:T(4,128)}, u32[]{:S(2)}) %copy-start) | copy-done | bytes 442392
  1.7 0.0 copy-start.2
  1.7 1.0 %copy-done.2 = f32[27,8,4,128]{3,2,1,0:T(4,128)S(1)} copy-done((f32[27,8,4,128]{3,2,1,0:T(4,128)S(1)}, f32[27,8,4,128]{3,2,1,0:T(4,128)}, u32[]{:S(2)}) %copy-start.2) | copy-done | bytes 442392
  2.7 0.0 copy-start.3
  2.7 0.7 %copy-done.3 = s32[8,4,128]{2,1,0:T(4,128)S(1)} copy-done((s32[8,4,128]{2,1,0:T(4,128)S(1)}, s32[8,4,128]{2,1,0:T(4,128)}, u32[]{:S(2)}) %copy-start.3) | copy-done | bytes 16408
  3.4 0.0 copy-start.1
  3.4 0.9 %collide.1 = (f32[18,4,8,128]{3,2,1,0:T(8,128)S(1)}, f32[3,4,8,128]{3,2,1,0:T(8,128)S(1)}, f32[4,8,128]{2,1,0:T(8,128)S(1)}, f32[3,8,128]{2,1,0:T(8,128)S(1)}) custom-call(f32[27]{0:T(128)S(1)} %copy-done.4, f32[27,32,128]{2,1,0:T(8,128)S(1)} %bitcast.7, s32[32,128]{1,0:T(8,128)S(1)} %bitcast.8, f32[27,32,128]{2,1,0:T(8,128)S(1)} %bitcast.4), custom_call_target="tpu_custom_call" | custom-call | tf_op jit(solution)/shard_map/collide/pallas_call | solution.py:368
  4.3 2.5 %collective-permute-start.1 = (f32[3,8,128]{2,1,0:T(8,128)S(1)}, f32[3,8,128]{2,1,0:T(8,128)S(1)}, u32[]{:S(2)}, u32[]{:S(2)}) collective-permute-start(f32[3,8,128]{2,1,0:T(8,128)S(1)} %get-tuple-element.16), channel_id=1, source_target_pairs={{0,3},{1,0},{2,1},{3,2},{4,7},{5,4},{6,5},{7,6},{8,11},{9,8},{10,9... | collective-permute-start | bytes 36872 | tf_op jit(solution)/shard_map/ppermute | solution.py:381
  6.8 0.0 collective-permute-start
  6.8 1.4 %collective-permute-done.1.from_right = f32[3,8,128]{2,1,0:T(8,128)S(1)} collective-permute-done((f32[3,8,128]{2,1,0:T(8,128)S(1)}, f32[3,8,128]{2,1,0:T(8,128)S(1)}, u32[]{:S(2)}, u32[]{:S(2)}) %collective-permute-start.1) | collective-permute-done | bytes 12320 | tf_op jit(solution)/shard_map/ppermute | solution.py:381
  8.2 1.7 %collective-permute-done.from_left = f32[3,8,128]{2,1,0:T(8,128)S(1)} collective-permute-done((f32[3,8,128]{2,1,0:T(8,128)S(1)}, f32[3,8,128]{2,1,0:T(8,128)S(1)}, u32[]{:S(2)}, u32[]{:S(2)}) %collective-permute-start) | collective-permute-done | bytes 12320 | tf_op jit(solution)/shard_map/ppermute | solution.py:381
  9.9 0.0 copy-done.1
  9.9 0.5 %pack.1 = (f32[36,8,128]{2,1,0:T(8,128)S(1)}, f32[36,8,128]{2,1,0:T(8,128)S(1)}, f32[4,12,8,128]{3,2,1,0:T(8,128)S(1)}, f32[3,8,128]{2,1,0:T(8,128)S(1)}) custom-call(f32[27,32,128]{2,1,0:T(8,128)S(1)} %bitcast.5, f32[18,4,8,128]{3,2,1,0:T(8,128)S(1)} %get-tuple-element.15.sums, f32[4,8,128]{2,1,0:T(8,128)S(1)} %get-tuple-element.14.solid_in, ...), custom_call_target="tpu_custom_call" | custom-call | tf_op jit(solution)/shard_map/pack/pallas_call | solution.py:368
  10.4 1.5 %collective-permute-start.2 = (f32[36,8,128]{2,1,0:T(8,128)S(1)}, f32[36,8,128]{2,1,0:T(8,128)S(1)}, u32[]{:S(2)}, u32[]{:S(2)}) collective-permute-start(f32[36,8,128]{2,1,0:T(8,128)S(1)} %get-tuple-element.19), channel_id=1, source_target_pairs={{0,4},{4,8},{8,12},{12,16},{16,20},{20,24},{24,28},{28,0},{1,5},{5... | collective-permute-start | bytes 442376 | tf_op jit(solution)/shard_map/ppermute | solution.py:381
  12.0 3.2 %collective-permute-start.3 = (f32[36,8,128]{2,1,0:T(8,128)S(1)}, f32[36,8,128]{2,1,0:T(8,128)S(1)}, u32[]{:S(2)}, u32[]{:S(2)}) collective-permute-start(f32[36,8,128]{2,1,0:T(8,128)S(1)} %get-tuple-element.20), channel_id=1, source_target_pairs={{0,28},{4,0},{8,4},{12,8},{16,12},{20,16},{24,20},{28,24},{1,29},{... | collective-permute-start | bytes 442376 | tf_op jit(solution)/shard_map/ppermute | solution.py:381
  15.2 3.2 %collective-permute-done.2.from_low = f32[36,8,128]{2,1,0:T(8,128)S(1)} collective-permute-done((f32[36,8,128]{2,1,0:T(8,128)S(1)}, f32[36,8,128]{2,1,0:T(8,128)S(1)}, u32[]{:S(2)}, u32[]{:S(2)}) %collective-permute-start.2) | collective-permute-done | bytes 147488 | tf_op jit(solution)/shard_map/ppermute | solution.py:381
  18.4 1.2 %collective-permute-done.3.from_high = f32[36,8,128]{2,1,0:T(8,128)S(1)} collective-permute-done((f32[36,8,128]{2,1,0:T(8,128)S(1)}, f32[36,8,128]{2,1,0:T(8,128)S(1)}, u32[]{:S(2)}, u32[]{:S(2)}) %collective-permute-start.3) | collective-permute-done | bytes 147488 | tf_op jit(solution)/shard_map/ppermute | solution.py:381
  19.5 5.4 %gradient.1 = f32[27,32,128]{2,1,0:T(8,128)} custom-call(f32[27]{0:T(128)S(1)} %copy-done.4, f32[27,32,128]{2,1,0:T(8,128)S(1)} %bitcast.6, f32[3,4,8,128]{3,2,1,0:T(8,128)S(1)} %get-tuple-element.13.speed, f32[4,8,128]{2,1,0:T(8,128)S(1)} %get-tuple-element.14.solid_in, f32[4,12,8,128]{3,2,1,0:T(8,128)S(1)} %get-tuple-element.17.own, ...), custom_call_target="tpu_custom_call" | custom-call | tf_op jit(solution)/shard_map/gradient/pallas_call | solution.py:368
Async XLA Ops:
  0.0 0.7 %copy-start.4 = (f32[27]{0:T(128)S(1)}, f32[27]{0:T(128)}, u32[]{:S(2)}) copy-start(f32[27]{0:T(128)} %rates.3) | copy-start | bytes 328
  0.7 1.0 %copy-start = (f32[27,8,4,128]{3,2,1,0:T(4,128)S(1)}, f32[27,8,4,128]{3,2,1,0:T(4,128)}, u32[]{:S(2)}) copy-start(f32[27,8,4,128]{3,2,1,0:T(4,128)} %param.7) | copy-start | bytes 1327108
  1.7 1.0 %copy-start.2 = (f32[27,8,4,128]{3,2,1,0:T(4,128)S(1)}, f32[27,8,4,128]{3,2,1,0:T(4,128)}, u32[]{:S(2)}) copy-start(f32[27,8,4,128]{3,2,1,0:T(4,128)} %param.4) | copy-start | bytes 1327108
  2.7 0.7 %copy-start.3 = (s32[8,4,128]{2,1,0:T(4,128)S(1)}, s32[8,4,128]{2,1,0:T(4,128)}, u32[]{:S(2)}) copy-start(s32[8,4,128]{2,1,0:T(4,128)} %param.6) | copy-start | bytes 49156
  3.4 6.5 %copy-start.1 = (f32[27,8,4,128]{3,2,1,0:T(4,128)S(1)}, f32[27,8,4,128]{3,2,1,0:T(4,128)}, u32[]{:S(2)}) copy-start(f32[27,8,4,128]{3,2,1,0:T(4,128)} %param.7) | copy-start | bytes 1327108
  4.3 3.9 %collective-permute-start.1 = (f32[3,8,128]{2,1,0:T(8,128)S(1)}, f32[3,8,128]{2,1,0:T(8,128)S(1)}, u32[]{:S(2)}, u32[]{:S(2)}) collective-permute-start(f32[3,8,128]{2,1,0:T(8,128)S(1)} %get-tuple-element.16), channel_id=1, source_target_pairs={{0,3},{1,0},{2,1},{3,2},{4,7},{5,4},{6,5},{7,6},{8,11},{9,8},{10,9... | collective-permute-start | bytes 36872 | tf_op jit(solution)/shard_map/ppermute | solution.py:381
  6.8 3.1 %collective-permute-start = (f32[3,8,128]{2,1,0:T(8,128)S(1)}, f32[3,8,128]{2,1,0:T(8,128)S(1)}, u32[]{:S(2)}, u32[]{:S(2)}) collective-permute-start(f32[3,8,128]{2,1,0:T(8,128)S(1)} %get-tuple-element.16), channel_id=1, source_target_pairs={{0,1},{1,2},{2,3},{3,0},{4,5},{5,6},{6,7},{7,4},{8,9},{9,10},{10,1... | collective-permute-start | bytes 36872 | tf_op jit(solution)/shard_map/ppermute | solution.py:381
  10.4 7.9 %collective-permute-start.2 = (f32[36,8,128]{2,1,0:T(8,128)S(1)}, f32[36,8,128]{2,1,0:T(8,128)S(1)}, u32[]{:S(2)}, u32[]{:S(2)}) collective-permute-start(f32[36,8,128]{2,1,0:T(8,128)S(1)} %get-tuple-element.19), channel_id=1, source_target_pairs={{0,4},{4,8},{8,12},{12,16},{16,20},{20,24},{24,28},{28,0},{1,5},{5... | collective-permute-start | bytes 442376 | tf_op jit(solution)/shard_map/ppermute | solution.py:381
  12.0 7.6 %collective-permute-start.3 = (f32[36,8,128]{2,1,0:T(8,128)S(1)}, f32[36,8,128]{2,1,0:T(8,128)S(1)}, u32[]{:S(2)}, u32[]{:S(2)}) collective-permute-start(f32[36,8,128]{2,1,0:T(8,128)S(1)} %get-tuple-element.20), channel_id=1, source_target_pairs={{0,28},{4,0},{8,4},{12,8},{16,12},{20,16},{24,20},{28,24},{1,29},{... | collective-permute-start | bytes 442376 | tf_op jit(solution)/shard_map/ppermute | solution.py:381

commit v2 on v1

--- a/solution.py
+++ b/solution.py
@@ -57,16 +57,16 @@
     return turn(block, {0: lane + 1, 1: lane, -1: lane + 2}[kind], 1)
 
 
-def incoming(packed, lane, kind):
-    return turn(packed, {0: 127, 1: 0, -1: 126}[kind] - lane, 1)
-
-
-def shift_y(main, outer, b, lane):
+def incoming(packed, lane, kind, b=0):
+    return turn(packed, {0: 127, 1: 0, -1: 126}[kind] - lane - b, 1)
+
+
+def shift_y(main, rolled_outer, b, lane):
     if b == 0:
-        return main, outer
+        return main, rolled_outer
     edge = lane == (127 if b == 1 else 0)
-    rm, ro = turn(main, -b, 1), turn(outer, -b, 1)
-    return jnp.where(edge, ro, rm), jnp.where(edge, rm, ro)
+    rolled = turn(main, -b, 1)
+    return jnp.where(edge, rolled_outer, rolled), jnp.where(edge, rolled, rolled_outer)
 
 
 def along(values, pass_):
@@ -169,12 +169,24 @@
     return [jnp.where(solid, v[26 - q], v[q] - h[q]) for q in range(27)]
 
 
-def scales(rates_ref):
-    return [rates_ref[i] * (0.5 ** NNZ[i]) for i in range(27)]
-
-
-def first_kernel(rows, rates, f, wall, cot, sums, speed, solid_out, packed):
-    scale = scales(rates)
+PIECES = 3
+
+
+def first_kernel(rows, rates_in, f_in, wall_in, cot_in, cot, scale_out, sums, speed, solid_out, packed,
+                 rates, f, wall, sems):
+    copies = [pltpu.make_async_copy(rates_in, rates, sems.at[0]), pltpu.make_async_copy(wall_in, wall, sems.at[1])]
+    for array, (source, target) in enumerate(((f_in, f), (cot_in, cot))):
+        for piece in range(PIECES):
+            part = pl.ds(27 // PIECES * piece, 27 // PIECES)
+            copies.append(pltpu.make_async_copy(
+                source.at[part], target.at[part], sems.at[2 + PIECES * array + piece]))
+    for copy in copies:
+        copy.start()
+    for copy in copies[:2 + PIECES]:
+        copy.wait()
+    for i in range(27):
+        scale_out[i] = jnp.full((8, 128), rates[i] * (0.5 ** NNZ[i]), F32)
+    scale = [rates[i] * (0.5 ** NNZ[i]) for i in range(27)]
     plane = lax.broadcasted_iota(jnp.int32, (8, 128), 0)
     boundary = (plane == 0) | (plane == 7)
     lane = lanes()
@@ -193,6 +205,8 @@
                 i = 2 * (3 * (a + 1) + b + 1)
                 sums[i, x] = out[qi(a, b, 0)] + (low + high)
                 sums[i + 1, x] = high - low
+    for copy in copies[2 + PIECES:]:
+        copy.wait()
     pieces = [jnp.zeros((8, 128), F32) for _ in range(3)]
     for key, (g, i, kind) in table.items():
         if key[0] == "v":
@@ -228,16 +242,16 @@
         halo.append(jnp.where(takes_left, from_left[g], from_right[g]))
         merged[g] = halo[g]
 
-    def outer(key):
+    def outer(key, b=0):
         g, i, kind = table[key]
-        return incoming(halo[g], i, kind)
+        return incoming(halo[g], i, kind, b)
 
     def both(a, x):
         parts = {}
         for b in SIGNS:
             for s in range(2):
                 i = 2 * (3 * (a + 1) + b + 1) + s
-                parts[b, s] = shift_y(sums[i, x], outer(("s", a, b, s, x)), -b, lane)
+                parts[b, s] = shift_y(sums[i, x], outer(("s", a, b, s, x), -b), -b, lane)
         result = []
         for n in range(2):
             result.append((
@@ -286,28 +300,32 @@
 
 
 def third_kernel(rows, rates, cot, speed, solid_in, own, merged, from_low, from_high, out, v1, g1, extra):
-    scale = scales(rates)
+    scale = [rates[i] for i in range(27)]
     lane = lanes()
     table, used = slots(rows)
     ring = rows + 2
     remote = {}
-    for side, message in ((1, from_high), (-1, from_low)):
+    for side, message, group in ((1, from_high, "high"), (-1, from_low, "low")):
         for k, (q, x) in enumerate(edge_rows(rows, side)):
-            g, i, kind = table["v", q, x]
-            remote[q, x + side * rows] = (message, k, i, kind)
+            _, i, kind = table["v", q, x]
+            remote[q, x + side * rows] = (message, group, k, i, kind)
+    turned = {}
+    for c in SIGNS:
+        for g in range(2):
+            turned[g, c] = turn(merged[g], -c, 0)
+        turned["low", c] = turn(from_low[35], -c, 0)
+        turned["high", c] = turn(from_high[35], -c, 0)
     for q, (a, b, c) in enumerate(Q):
         for x in range(-1, rows + 1):
             source = x + a
             if 0 <= source < rows:
                 main = cot[q, pl.ds(source, 8, stride=rows), :]
-                g, i, kind = table["v", q, source]
-                outer = incoming(merged[g], i, kind)
+                group, i, kind = table["v", q, source]
             else:
-                message, k, i, kind = remote[q, source]
+                message, group, k, i, kind = remote[q, source]
                 main = message[k]
-                outer = incoming(message[35], i, kind)
-            main, outer = turn(main, -c, 0), turn(outer, -c, 0)
-            main, outer = shift_y(main, outer, b, lane)
+            outer = incoming(turned[group, c], i, kind, b)
+            main, outer = shift_y(turn(main, -c, 0), outer, b, lane)
             v1[q, 2 * (x + 1)] = main
             v1[q, 2 * (x + 1) + 1] = outer
     for x in range(-1, rows + 1):
@@ -353,24 +371,20 @@
             r = 2 * (x + a + 1)
             main = g1[q, r]
             if b:
-                main = shift_y(main, g1[q, r + 1], b, lane)[0]
+                main = shift_y(main, turn(g1[q, r + 1], -b, 1), b, lane)[0]
             v.append(turn(main, -c, 0))
         result = pull_back(v, [speed[k, x] for k in range(3)], solid_in[x] > 0.5, scale)
         for q in range(27):
             out[q, pl.ds(x, 8, stride=rows), :] = result[q]
 
 
-def call(kernel, name, out_shapes, scratch, operands, smem_first):
-    vmem = pl.BlockSpec(memory_space=pltpu.VMEM)
-    specs = [vmem] * len(operands)
-    if smem_first:
-        specs[0] = pl.BlockSpec(memory_space=pltpu.SMEM)
+def call(kernel, name, out_shapes, scratch, operands, space=pltpu.VMEM):
     return pl.pallas_call(
         kernel,
         out_shape=[jax.ShapeDtypeStruct(s, F32) for s in out_shapes],
-        in_specs=specs,
-        out_specs=[vmem] * len(out_shapes),
-        scratch_shapes=[pltpu.VMEM(s, F32) for s in scratch],
+        in_specs=[pl.BlockSpec(memory_space=space)] * len(operands),
+        out_specs=[pl.BlockSpec(memory_space=pltpu.VMEM)] * len(out_shapes),
+        scratch_shapes=scratch,
         compiler_params=pltpu.CompilerParams(vmem_limit_bytes=32 * 1024 * 1024),
         name=name,
     )(*operands)
@@ -387,23 +401,27 @@
     cot = cotangent.reshape(27, planes * rows, width)
     wall = wall_mask.reshape(planes * rows, width)
     tile = (planes, width)
-    sums, speed, solid, packed = call(
+    lattice = (27, planes * rows, width)
+    cot, scale, sums, speed, solid, packed = call(
         functools.partial(first_kernel, rows), "collide",
-        [(18, rows) + tile, (3, rows) + tile, (rows,) + tile, (3,) + tile], [],
-        (rates, f, wall, cot), True)
+        [lattice, (27,) + tile, (18, rows) + tile, (3, rows) + tile, (rows,) + tile, (3,) + tile],
+        [pltpu.SMEM((27,), F32), pltpu.VMEM(lattice, F32), pltpu.VMEM(lattice[1:], jnp.int32),
+         pltpu.SemaphoreType.DMA((2 + 2 * PIECES,))],
+        (rates, f, wall, cot), pltpu.HBM)
     from_right = ring(packed, "gy", -1)
     from_left = ring(packed, "gy", 1)
     to_left, to_right, own, merged = call(
         functools.partial(second_kernel, rows), "pack",
         [(36,) + tile, (36,) + tile, (4, 2 * rows + 4) + tile, (3,) + tile], [],
-        (cot, sums, solid, from_left, from_right), False)
+        (cot, sums, solid, from_left, from_right))
     from_high = ring(to_left, "gx", -1)
     from_low = ring(to_right, "gx", 1)
     (out,) = call(
         functools.partial(third_kernel, rows), "gradient",
-        [(27, planes * rows, width)],
-        [(27, 2 * rows + 4) + tile, (27, 2 * rows + 4) + tile, (4, 2 * rows + 4) + tile],
-        (rates, cot, speed, solid, own, merged, from_low, from_high), True)
+        [lattice],
+        [pltpu.VMEM((27, 2 * rows + 4) + tile, F32), pltpu.VMEM((27, 2 * rows + 4) + tile, F32),
+         pltpu.VMEM((4, 2 * rows + 4) + tile, F32)],
+        (scale, cot, speed, solid, own, merged, from_low, from_high))
     return out.reshape(checkpoint.shape)
 
 

time: 25.2 us -> 22.5 us (0.89)
  Pallas kernels: 6.83 us -> 4.18 us
    pallas_call x3, Pallas kernels: 6.83 us -> 4.18 us  [call(): pl.pallas_call(kernel, out_shape=[jax.ShapeDtypeStruct(s, F32) for s in o...]
    unnamed x10 -> x8, local copies, waits for them, and re-layouts: 3.4 us -> 3.4 us
where the time goes in v2:
time: 22.5 us; the launch traced here: 22.3 us
  waiting for transfers between devices  7.46 us (33%)
  starting transfers between devices  7.24 us (32%)
  Pallas kernels  4.18 us (19%)
  local copies, waits for them, and re-layouts  3.4 us (15%)
    ppermute x4, waiting for transfers between devices, ring(): lax.ppermute(block, axis, [(i, (i + step) % size) for i in range(size)])  7.46 us
    ppermute x4, starting transfers between devices, ring(): lax.ppermute(block, axis, [(i, (i + step) % size) for i in range(size)])  7.24 us
    pallas_call x3, Pallas kernels, call(): pl.pallas_call(kernel, out_shape=[jax.ShapeDtypeStruct(s, F32) for s in o...  4.18 us
    unnamed x8, local copies, waits for them, and re-layouts  3.4 us
  transfers between devices with their start and end apart: 4, of which 4 were waited for; matrix products, arithmetic and copies ran while one was open for 0% of the time, Pallas kernels for 0%

profile of v2, /device:TPU:0, one launch (start us, length us, event | category | flops | bytes accessed | tf_op | source)
XLA Modules:
  0.0 22.3 jit_solution(1973398079766364491)
XLA Ops:
  0.0 0.0 copy-start.3
  0.0 0.7 %copy-done.3 = f32[27]{0:T(128)S(1)} copy-done((f32[27]{0:T(128)S(1)}, f32[27]{0:T(128)}, u32[]{:S(2)}) %copy-start.3) | copy-done | bytes 132
  0.7 0.0 copy-start
  0.7 1.0 %copy-done = f32[27,8,4,128]{3,2,1,0:T(4,128)S(1)} copy-done((f32[27,8,4,128]{3,2,1,0:T(4,128)S(1)}, f32[27,8,4,128]{3,2,1,0:T(4,128)}, u32[]{:S(2)}) %copy-start) | copy-done | bytes 442392
  1.7 0.0 copy-start.1
  1.7 1.0 %copy-done.1 = f32[27,8,4,128]{3,2,1,0:T(4,128)S(1)} copy-done((f32[27,8,4,128]{3,2,1,0:T(4,128)S(1)}, f32[27,8,4,128]{3,2,1,0:T(4,128)}, u32[]{:S(2)}) %copy-start.1) | copy-done | bytes 442392
  2.7 0.0 copy-start.2
  2.7 0.7 %copy-done.2 = s32[8,4,128]{2,1,0:T(4,128)S(1)} copy-done((s32[8,4,128]{2,1,0:T(4,128)S(1)}, s32[8,4,128]{2,1,0:T(4,128)}, u32[]{:S(2)}) %copy-start.2) | copy-done | bytes 16408
  3.4 1.7 %collide.1 = (f32[27,32,128]{2,1,0:T(8,128)S(1)}, f32[27,8,128]{2,1,0:T(8,128)S(1)}, f32[18,4,8,128]{3,2,1,0:T(8,128)S(1)}, f32[3,4,8,128]{3,2,1,0:T(8,128)S(1)}...) custom-call(f32[27]{0:T(128)S(1)} %copy-done.3, f32[27,32,128]{2,1,0:T(8,128)S(1)} %bitcast.4, ...), custom_call_target="tpu_custom_call" | custom-call | tf_op jit(solution)/shard_map/collide/pallas_call | solution.py:382
  5.1 2.5 %collective-permute-start.1 = (f32[3,8,128]{2,1,0:T(8,128)S(1)}, f32[3,8,128]{2,1,0:T(8,128)S(1)}, u32[]{:S(2)}, u32[]{:S(2)}) collective-permute-start(f32[3,8,128]{2,1,0:T(8,128)S(1)} %get-tuple-element.20), channel_id=1, source_target_pairs={{0,3},{1,0},{2,1},{3,2},{4,7},{5,4},{6,5},{7,6},{8,11},{9,8},{10,9... | collective-permute-start | bytes 36872 | tf_op jit(solution)/shard_map/ppermute | solution.py:395
  7.6 0.0 collective-permute-start
  7.6 1.4 %collective-permute-done.1.from_right = f32[3,8,128]{2,1,0:T(8,128)S(1)} collective-permute-done((f32[3,8,128]{2,1,0:T(8,128)S(1)}, f32[3,8,128]{2,1,0:T(8,128)S(1)}, u32[]{:S(2)}, u32[]{:S(2)}) %collective-permute-start.1) | collective-permute-done | bytes 12320 | tf_op jit(solution)/shard_map/ppermute | solution.py:395
  9.0 1.7 %collective-permute-done.from_left = f32[3,8,128]{2,1,0:T(8,128)S(1)} collective-permute-done((f32[3,8,128]{2,1,0:T(8,128)S(1)}, f32[3,8,128]{2,1,0:T(8,128)S(1)}, u32[]{:S(2)}, u32[]{:S(2)}) %collective-permute-start) | collective-permute-done | bytes 12320 | tf_op jit(solution)/shard_map/ppermute | solution.py:395
  10.7 0.3 %pack.1 = (f32[36,8,128]{2,1,0:T(8,128)S(1)}, f32[36,8,128]{2,1,0:T(8,128)S(1)}, f32[4,12,8,128]{3,2,1,0:T(8,128)S(1)}, f32[3,8,128]{2,1,0:T(8,128)S(1)}) custom-call(f32[27,32,128]{2,1,0:T(8,128)S(1)} %get-tuple-element.16.cot, f32[18,4,8,128]{3,2,1,0:T(8,128)S(1)} %get-tuple-element.19.sums, f32[4,8,128]{2,1,0:T(8,128)S(1)} %get-tuple-element.18.solid_in, ...), custom_call_target="tpu_custom_call" | custom-call | tf_op jit(solution)/shard_map/pack/pallas_call | solution.py:382
  11.0 1.5 %collective-permute-start.2 = (f32[36,8,128]{2,1,0:T(8,128)S(1)}, f32[36,8,128]{2,1,0:T(8,128)S(1)}, u32[]{:S(2)}, u32[]{:S(2)}) collective-permute-start(f32[36,8,128]{2,1,0:T(8,128)S(1)} %get-tuple-element.23), channel_id=1, source_target_pairs={{0,4},{4,8},{8,12},{12,16},{16,20},{20,24},{24,28},{28,0},{1,5},{5... | collective-permute-start | bytes 442376 | tf_op jit(solution)/shard_map/ppermute | solution.py:395
  12.5 3.2 %collective-permute-start.3 = (f32[36,8,128]{2,1,0:T(8,128)S(1)}, f32[36,8,128]{2,1,0:T(8,128)S(1)}, u32[]{:S(2)}, u32[]{:S(2)}) collective-permute-start(f32[36,8,128]{2,1,0:T(8,128)S(1)} %get-tuple-element.24), channel_id=1, source_target_pairs={{0,28},{4,0},{8,4},{12,8},{16,12},{20,16},{24,20},{28,24},{1,29},{... | collective-permute-start | bytes 442376 | tf_op jit(solution)/shard_map/ppermute | solution.py:395
  15.7 3.2 %collective-permute-done.2.from_low = f32[36,8,128]{2,1,0:T(8,128)S(1)} collective-permute-done((f32[36,8,128]{2,1,0:T(8,128)S(1)}, f32[36,8,128]{2,1,0:T(8,128)S(1)}, u32[]{:S(2)}, u32[]{:S(2)}) %collective-permute-start.2) | collective-permute-done | bytes 147488 | tf_op jit(solution)/shard_map/ppermute | solution.py:395
  18.9 1.2 %collective-permute-done.3.from_high = f32[36,8,128]{2,1,0:T(8,128)S(1)} collective-permute-done((f32[36,8,128]{2,1,0:T(8,128)S(1)}, f32[36,8,128]{2,1,0:T(8,128)S(1)}, u32[]{:S(2)}, u32[]{:S(2)}) %collective-permute-start.3) | collective-permute-done | bytes 147488 | tf_op jit(solution)/shard_map/ppermute | solution.py:395
  20.1 2.2 %gradient.1 = f32[27,32,128]{2,1,0:T(8,128)} custom-call(f32[27,8,128]{2,1,0:T(8,128)S(1)} %get-tuple-element.15.rates, f32[27,32,128]{2,1,0:T(8,128)S(1)} %get-tuple-element.16.cot, f32[3,4,8,128]{3,2,1,0:T(8,128)S(1)} %get-tuple-element.17.speed, f32[4,8,128]{2,1,0:T(8,128)S(1)} %get-tuple-element.18.solid_in, ...), custom_call_target="tpu_custom_call" | custom-call | tf_op jit(solution)/shard_map/gradient/pallas_call | solution.py:382
Async XLA Ops:
  0.0 0.7 %copy-start.3 = (f32[27]{0:T(128)S(1)}, f32[27]{0:T(128)}, u32[]{:S(2)}) copy-start(f32[27]{0:T(128)} %rates_in.1) | copy-start | bytes 328
  0.7 1.0 %copy-start = (f32[27,8,4,128]{3,2,1,0:T(4,128)S(1)}, f32[27,8,4,128]{3,2,1,0:T(4,128)}, u32[]{:S(2)}) copy-start(f32[27,8,4,128]{3,2,1,0:T(4,128)} %param.4) | copy-start | bytes 1327108
  1.7 1.0 %copy-start.1 = (f32[27,8,4,128]{3,2,1,0:T(4,128)S(1)}, f32[27,8,4,128]{3,2,1,0:T(4,128)}, u32[]{:S(2)}) copy-start(f32[27,8,4,128]{3,2,1,0:T(4,128)} %param.7) | copy-start | bytes 1327108
  2.7 0.7 %copy-start.2 = (s32[8,4,128]{2,1,0:T(4,128)S(1)}, s32[8,4,128]{2,1,0:T(4,128)}, u32[]{:S(2)}) copy-start(s32[8,4,128]{2,1,0:T(4,128)} %param.6) | copy-start | bytes 49156
  5.1 3.9 %collective-permute-start.1 = (f32[3,8,128]{2,1,0:T(8,128)S(1)}, f32[3,8,128]{2,1,0:T(8,128)S(1)}, u32[]{:S(2)}, u32[]{:S(2)}) collective-permute-start(f32[3,8,128]{2,1,0:T(8,128)S(1)} %get-tuple-element.20), channel_id=1, source_target_pairs={{0,3},{1,0},{2,1},{3,2},{4,7},{5,4},{6,5},{7,6},{8,11},{9,8},{10,9... | collective-permute-start | bytes 36872 | tf_op jit(solution)/shard_map/ppermute | solution.py:395
  7.6 3.1 %collective-permute-start = (f32[3,8,128]{2,1,0:T(8,128)S(1)}, f32[3,8,128]{2,1,0:T(8,128)S(1)}, u32[]{:S(2)}, u32[]{:S(2)}) collective-permute-start(f32[3,8,128]{2,1,0:T(8,128)S(1)} %get-tuple-element.20), channel_id=1, source_target_pairs={{0,1},{1,2},{2,3},{3,0},{4,5},{5,6},{6,7},{7,4},{8,9},{9,10},{10,1... | collective-permute-start | bytes 36872 | tf_op jit(solution)/shard_map/ppermute | solution.py:395
  11.0 7.9 %collective-permute-start.2 = (f32[36,8,128]{2,1,0:T(8,128)S(1)}, f32[36,8,128]{2,1,0:T(8,128)S(1)}, u32[]{:S(2)}, u32[]{:S(2)}) collective-permute-start(f32[36,8,128]{2,1,0:T(8,128)S(1)} %get-tuple-element.23), channel_id=1, source_target_pairs={{0,4},{4,8},{8,12},{12,16},{16,20},{20,24},{24,28},{28,0},{1,5},{5... | collective-permute-start | bytes 442376 | tf_op jit(solution)/shard_map/ppermute | solution.py:395
  12.5 7.6 %collective-permute-start.3 = (f32[36,8,128]{2,1,0:T(8,128)S(1)}, f32[36,8,128]{2,1,0:T(8,128)S(1)}, u32[]{:S(2)}, u32[]{:S(2)}) collective-permute-start(f32[36,8,128]{2,1,0:T(8,128)S(1)} %get-tuple-element.24), channel_id=1, source_target_pairs={{0,28},{4,0},{8,4},{12,8},{16,12},{20,16},{24,20},{28,24},{1,29},{... | collective-permute-start | bytes 442376 | tf_op jit(solution)/shard_map/ppermute | solution.py:395

commit v3 on v2

--- a/solution.py
+++ b/solution.py
@@ -407,7 +407,7 @@
         [lattice, (27,) + tile, (18, rows) + tile, (3, rows) + tile, (rows,) + tile, (3,) + tile],
         [pltpu.SMEM((27,), F32), pltpu.VMEM(lattice, F32), pltpu.VMEM(lattice[1:], jnp.int32),
          pltpu.SemaphoreType.DMA((2 + 2 * PIECES,))],
-        (rates, f, wall, cot), pltpu.HBM)
+        tuple(pltpu.with_memory_space_constraint(v, pltpu.HBM) for v in (rates, f, wall, cot)), pltpu.HBM)
     from_right = ring(packed, "gy", -1)
     from_left = ring(packed, "gy", 1)
     to_left, to_right, own, merged = call(

time: 22.5 us -> 19 us (0.84)
  local copies, waits for them, and re-layouts: 3.4 us -> 0 us
    unnamed x8 -> x0, local copies, waits for them, and re-layouts: 3.4 us -> none
where the time goes in v3:
time: 19 us; the launch traced here: 18.8 us
  waiting for transfers between devices  7.46 us (39%)
  starting transfers between devices  7.24 us (38%)
  Pallas kernels  4.11 us (22%)
    ppermute x4, waiting for transfers between devices, ring(): lax.ppermute(block, axis, [(i, (i + step) % size) for i in range(size)])  7.46 us
    ppermute x4, starting transfers between devices, ring(): lax.ppermute(block, axis, [(i, (i + step) % size) for i in range(size)])  7.24 us
    pallas_call x3, Pallas kernels, call(): pl.pallas_call(kernel, out_shape=[jax.ShapeDtypeStruct(s, F32) for s in o...  4.11 us
  transfers between devices with their start and end apart: 4, of which 4 were waited for; matrix products, arithmetic and copies ran while one was open for 0% of the time, Pallas kernels for 0%

profile of v3, /device:TPU:0, one launch (start us, length us, event | category | flops | bytes accessed | tf_op | source)
XLA Modules:
  0.0 18.8 jit_solution(9140260405927441855)
XLA Ops:
  0.0 1.6 %collide.1 = (f32[27,32,128]{2,1,0:T(8,128)S(1)}, f32[27,8,128]{2,1,0:T(8,128)S(1)}, f32[18,4,8,128]{3,2,1,0:T(8,128)S(1)}, f32[3,4,8,128]{3,2,1,0:T(8,128)S(1)}...) custom-call(f32[27]{0:T(128)} %rates_in.1, f32[27,32,128]{2,1,0:T(8,128)} %bitcast.4, s32[32,128]{1,0:T(8,128)} %bitcast.6, ...), custom_call_target="tpu_custom_call" | custom-call | tf_op jit(solution)/shard_map/collide/pallas_call | solution.py:382
  1.6 2.5 %collective-permute-start.1 = (f32[3,8,128]{2,1,0:T(8,128)S(1)}, f32[3,8,128]{2,1,0:T(8,128)S(1)}, u32[]{:S(2)}, u32[]{:S(2)}) collective-permute-start(f32[3,8,128]{2,1,0:T(8,128)S(1)} %get-tuple-element.20), channel_id=1, source_target_pairs={{0,3},{1,0},{2,1},{3,2},{4,7},{5,4},{6,5},{7,6},{8,11},{9,8},{10,9... | collective-permute-start | bytes 36872 | tf_op jit(solution)/shard_map/ppermute | solution.py:395
  4.1 0.0 collective-permute-start
  4.1 1.4 %collective-permute-done.1.from_right = f32[3,8,128]{2,1,0:T(8,128)S(1)} collective-permute-done((f32[3,8,128]{2,1,0:T(8,128)S(1)}, f32[3,8,128]{2,1,0:T(8,128)S(1)}, u32[]{:S(2)}, u32[]{:S(2)}) %collective-permute-start.1) | collective-permute-done | bytes 12320 | tf_op jit(solution)/shard_map/ppermute | solution.py:395
  5.5 1.7 %collective-permute-done.from_left = f32[3,8,128]{2,1,0:T(8,128)S(1)} collective-permute-done((f32[3,8,128]{2,1,0:T(8,128)S(1)}, f32[3,8,128]{2,1,0:T(8,128)S(1)}, u32[]{:S(2)}, u32[]{:S(2)}) %collective-permute-start) | collective-permute-done | bytes 12320 | tf_op jit(solution)/shard_map/ppermute | solution.py:395
  7.2 0.3 %pack.1 = (f32[36,8,128]{2,1,0:T(8,128)S(1)}, f32[36,8,128]{2,1,0:T(8,128)S(1)}, f32[4,12,8,128]{3,2,1,0:T(8,128)S(1)}, f32[3,8,128]{2,1,0:T(8,128)S(1)}) custom-call(f32[27,32,128]{2,1,0:T(8,128)S(1)} %get-tuple-element.16.cot, f32[18,4,8,128]{3,2,1,0:T(8,128)S(1)} %get-tuple-element.19.sums, f32[4,8,128]{2,1,0:T(8,128)S(1)} %get-tuple-element.18.solid_in, ...), custom_call_target="tpu_custom_call" | custom-call | tf_op jit(solution)/shard_map/pack/pallas_call | solution.py:382
  7.5 1.5 %collective-permute-start.2 = (f32[36,8,128]{2,1,0:T(8,128)S(1)}, f32[36,8,128]{2,1,0:T(8,128)S(1)}, u32[]{:S(2)}, u32[]{:S(2)}) collective-permute-start(f32[36,8,128]{2,1,0:T(8,128)S(1)} %get-tuple-element.23), channel_id=1, source_target_pairs={{0,4},{4,8},{8,12},{12,16},{16,20},{20,24},{24,28},{28,0},{1,5},{5... | collective-permute-start | bytes 442376 | tf_op jit(solution)/shard_map/ppermute | solution.py:395
  9.0 3.2 %collective-permute-start.3 = (f32[36,8,128]{2,1,0:T(8,128)S(1)}, f32[36,8,128]{2,1,0:T(8,128)S(1)}, u32[]{:S(2)}, u32[]{:S(2)}) collective-permute-start(f32[36,8,128]{2,1,0:T(8,128)S(1)} %get-tuple-element.24), channel_id=1, source_target_pairs={{0,28},{4,0},{8,4},{12,8},{16,12},{20,16},{24,20},{28,24},{1,29},{... | collective-permute-start | bytes 442376 | tf_op jit(solution)/shard_map/ppermute | solution.py:395
  12.3 3.2 %collective-permute-done.2.from_low = f32[36,8,128]{2,1,0:T(8,128)S(1)} collective-permute-done((f32[36,8,128]{2,1,0:T(8,128)S(1)}, f32[36,8,128]{2,1,0:T(8,128)S(1)}, u32[]{:S(2)}, u32[]{:S(2)}) %collective-permute-start.2) | collective-permute-done | bytes 147488 | tf_op jit(solution)/shard_map/ppermute | solution.py:395
  15.4 1.2 %collective-permute-done.3.from_high = f32[36,8,128]{2,1,0:T(8,128)S(1)} collective-permute-done((f32[36,8,128]{2,1,0:T(8,128)S(1)}, f32[36,8,128]{2,1,0:T(8,128)S(1)}, u32[]{:S(2)}, u32[]{:S(2)}) %collective-permute-start.3) | collective-permute-done | bytes 147488 | tf_op jit(solution)/shard_map/ppermute | solution.py:395
  16.6 2.2 %gradient.1 = f32[27,32,128]{2,1,0:T(8,128)} custom-call(f32[27,8,128]{2,1,0:T(8,128)S(1)} %get-tuple-element.15.rates, f32[27,32,128]{2,1,0:T(8,128)S(1)} %get-tuple-element.16.cot, f32[3,4,8,128]{3,2,1,0:T(8,128)S(1)} %get-tuple-element.17.speed, f32[4,8,128]{2,1,0:T(8,128)S(1)} %get-tuple-element.18.solid_in, ...), custom_call_target="tpu_custom_call" | custom-call | tf_op jit(solution)/shard_map/gradient/pallas_call | solution.py:382
Async XLA Ops:
  1.6 3.9 %collective-permute-start.1 = (f32[3,8,128]{2,1,0:T(8,128)S(1)}, f32[3,8,128]{2,1,0:T(8,128)S(1)}, u32[]{:S(2)}, u32[]{:S(2)}) collective-permute-start(f32[3,8,128]{2,1,0:T(8,128)S(1)} %get-tuple-element.20), channel_id=1, source_target_pairs={{0,3},{1,0},{2,1},{3,2},{4,7},{5,4},{6,5},{7,6},{8,11},{9,8},{10,9... | collective-permute-start | bytes 36872 | tf_op jit(solution)/shard_map/ppermute | solution.py:395
  4.1 3.1 %collective-permute-start = (f32[3,8,128]{2,1,0:T(8,128)S(1)}, f32[3,8,128]{2,1,0:T(8,128)S(1)}, u32[]{:S(2)}, u32[]{:S(2)}) collective-permute-start(f32[3,8,128]{2,1,0:T(8,128)S(1)} %get-tuple-element.20), channel_id=1, source_target_pairs={{0,1},{1,2},{2,3},{3,0},{4,5},{5,6},{6,7},{7,4},{8,9},{9,10},{10,1... | collective-permute-start | bytes 36872 | tf_op jit(solution)/shard_map/ppermute | solution.py:395
  7.5 7.9 %collective-permute-start.2 = (f32[36,8,128]{2,1,0:T(8,128)S(1)}, f32[36,8,128]{2,1,0:T(8,128)S(1)}, u32[]{:S(2)}, u32[]{:S(2)}) collective-permute-start(f32[36,8,128]{2,1,0:T(8,128)S(1)} %get-tuple-element.23), channel_id=1, source_target_pairs={{0,4},{4,8},{8,12},{12,16},{16,20},{20,24},{24,28},{28,0},{1,5},{5... | collective-permute-start | bytes 442376 | tf_op jit(solution)/shard_map/ppermute | solution.py:395
  9.0 7.6 %collective-permute-start.3 = (f32[36,8,128]{2,1,0:T(8,128)S(1)}, f32[36,8,128]{2,1,0:T(8,128)S(1)}, u32[]{:S(2)}, u32[]{:S(2)}) collective-permute-start(f32[36,8,128]{2,1,0:T(8,128)S(1)} %get-tuple-element.24), channel_id=1, source_target_pairs={{0,28},{4,0},{8,4},{12,8},{16,12},{20,16},{24,20},{28,24},{1,29},{... | collective-permute-start | bytes 442376 | tf_op jit(solution)/shard_map/ppermute | solution.py:395

commit v4 on v3

--- a/solution.py
+++ b/solution.py
@@ -173,6 +173,7 @@
 
 
 def first_kernel(rows, rates_in, f_in, wall_in, cot_in, cot, scale_out, sums, speed, solid_out, packed,
+                 raw_right,
                  rates, f, wall, sems):
     copies = [pltpu.make_async_copy(rates_in, rates, sems.at[0]), pltpu.make_async_copy(wall_in, wall, sems.at[1])]
     for array, (source, target) in enumerate(((f_in, f), (cot_in, cot))):
@@ -207,6 +208,7 @@
                 sums[i + 1, x] = high - low
     for copy in copies[2 + PIECES:]:
         copy.wait()
+    raw_rows(rows, -1, cot, raw_right)
     pieces = [jnp.zeros((8, 128), F32) for _ in range(3)]
     for key, (g, i, kind) in table.items():
         if key[0] == "v":
@@ -226,6 +228,11 @@
     keys = [(q, near) for q, c in enumerate(Q) if c[0] == 0]
     keys += [(q, near) for q, c in enumerate(Q) if c[0] == side]
     return keys + [(q, far) for q, c in enumerate(Q) if c[0] == side]
+
+
+def raw_rows(rows, side, cot, message):
+    for k, (q, x) in enumerate(edge_rows(rows, side)):
+        message[k] = cot[q, pl.ds(x, 8, stride=rows), :]
 
 
 def second_kernel(rows, cot, sums, solid_in, from_left, from_right, to_left, to_right, own, merged):
@@ -281,8 +288,9 @@
 
     for side, message in ((1, to_left), (-1, to_right)):
         near, far = (0, 1) if side == 1 else (rows - 1, rows - 2)
-        for k, (q, x) in enumerate(edge_rows(rows, side)):
-            message[k] = cot[q, pl.ds(x, 8, stride=rows), :]
+        first = message.shape[0] - 9
+        if first:
+            raw_rows(rows, side, cot, message)
         extra = []
         for n in range(2):
             row = list(t[-side, near][n])
@@ -293,99 +301,154 @@
             extra.append(row)
         columns = halo[0]
         for k in range(8):
-            message[27 + k] = extra[0][k]
+            message[first + k] = extra[0][k]
             i = used + 2 * k
             columns = jnp.where((lane == i) | (lane == i + 1), turn(extra[1][k], i + 1, 1), columns)
-        message[35] = columns
-
-
-def third_kernel(rows, rates, cot, speed, solid_in, own, merged, from_low, from_high, out, v1, g1, extra):
-    scale = [rates[i] for i in range(27)]
+        message[first + 8] = columns
+
+
+def outer_rows(rows):
+    return [x for x in range(-1, rows + 1) if not 0 < x < rows - 1]
+
+
+def gathered(rows, x, q, cot, turned, lane, remote=None):
+    table, _ = slots(rows)
+    a, b, c = Q[q]
+    source = x + a
+    if 0 <= source < rows:
+        main = cot[q, pl.ds(source, 8, stride=rows), :]
+        group, i, kind = table["v", q, source]
+    else:
+        message, group, k, i, kind = remote[q, source]
+        main = message[k]
+    outer = incoming(turned[group, c], i, kind, b)
+    return shift_y(turn(main, -c, 0), outer, b, lane)
+
+
+def middle_kernel(rows, scale_in, cot, solid_in, own, merged, inner, known):
+    scale = [scale_in[i] for i in range(27)]
+    lane = lanes()
+    table, _ = slots(rows)
+    turned = {(g, c): turn(merged[g], -c, 0) for g in range(2) for c in SIGNS}
+    for x in range(1, rows - 1):
+        v = [gathered(rows, x, q, cot, turned, lane) for q in range(27)]
+        for n in range(2):
+            total = [own[k, 2 * (x + 1) + n] for k in range(4)]
+            inverse = 1.0 / total[0]
+            if n == 0:
+                wall = solid_in[x]
+            else:
+                g, i, kind = table["w", x]
+                wall = incoming(merged[g], i, kind)
+            out = pull_back([t[n] for t in v], [t * inverse for t in total[1:]], wall > 0.5, scale)
+            for q in range(27):
+                inner[q, 2 * (x - 1) + n] = out[q]
+    for j, x in enumerate(outer_rows(rows)):
+        for q in range(27):
+            if 0 <= x + Q[q][0] < rows:
+                known[q, 2 * j], known[q, 2 * j + 1] = gathered(rows, x, q, cot, turned, lane)
+
+
+def outer_gradient(rows, side, scale, solid_in, own, merged, known, raw, extra, g1):
     lane = lanes()
     table, used = slots(rows)
-    ring = rows + 2
     remote = {}
-    for side, message, group in ((1, from_high, "high"), (-1, from_low, "low")):
-        for k, (q, x) in enumerate(edge_rows(rows, side)):
-            _, i, kind = table["v", q, x]
-            remote[q, x + side * rows] = (message, group, k, i, kind)
-    turned = {}
-    for c in SIGNS:
-        for g in range(2):
-            turned[g, c] = turn(merged[g], -c, 0)
-        turned["low", c] = turn(from_low[35], -c, 0)
-        turned["high", c] = turn(from_high[35], -c, 0)
-    for q, (a, b, c) in enumerate(Q):
-        for x in range(-1, rows + 1):
-            source = x + a
-            if 0 <= source < rows:
-                main = cot[q, pl.ds(source, 8, stride=rows), :]
-                group, i, kind = table["v", q, source]
+    for k, (q, x) in enumerate(edge_rows(rows, side)):
+        _, i, kind = table["v", q, x]
+        remote[q, x + side * rows] = (raw, "far", k, i, kind)
+    turned = {("far", c): turn(extra[8], -c, 0) for c in SIGNS}
+    near = rows - 1 if side == 1 else 0
+    for j, x in enumerate(outer_rows(rows)):
+        if x not in (near, near + side):
+            continue
+        v = []
+        for q in range(27):
+            if 0 <= x + Q[q][0] < rows:
+                v.append((known[q, 2 * j], known[q, 2 * j + 1]))
             else:
-                message, group, k, i, kind = remote[q, source]
-                main = message[k]
-            outer = incoming(turned[group, c], i, kind, b)
-            main, outer = shift_y(turn(main, -c, 0), outer, b, lane)
-            v1[q, 2 * (x + 1)] = main
-            v1[q, 2 * (x + 1) + 1] = outer
-    for x in range(-1, rows + 1):
+                v.append(gathered(rows, x, q, None, turned, lane, remote))
         for n in range(2):
+            def got(k):
+                return extra[k] if n == 0 else incoming(extra[8], used + 2 * k, 0)
+
             total = [own[k, 2 * (x + 1) + n] for k in range(4)]
-            for side, message in ((1, from_high), (-1, from_low)):
-                near = rows - 1 if side == 1 else 0
-
-                def got(k):
-                    if n == 0:
-                        return message[27 + k]
-                    return incoming(message[35], used + 2 * k, 0)
-
-                if x == near:
-                    total = [total[0] + got(0), total[1] - got(0) if side == 1 else total[1] + got(0),
-                             total[2] + got(1), total[3] + got(2)]
-                if x == near + side:
-                    total = [total[k] + got(3 + k) for k in range(4)]
-                    wall = got(7)
-            if 0 <= x < rows:
+            if x == near:
+                total = [total[0] + got(0), total[1] - got(0) if side == 1 else total[1] + got(0),
+                         total[2] + got(1), total[3] + got(2)]
                 if n == 0:
                     wall = solid_in[x]
                 else:
                     g, i, kind = table["w", x]
                     wall = incoming(merged[g], i, kind)
+            else:
+                total = [total[k] + got(3 + k) for k in range(4)]
+                wall = got(7)
             inverse = 1.0 / total[0]
-            for k in range(3):
-                extra[k, 2 * (x + 1) + n] = total[k + 1] * inverse
-            extra[3, 2 * (x + 1) + n] = wall
-
-    def one(r, _):
-        v = [v1[q, r] for q in range(27)]
-        u = [extra[k, r] for k in range(3)]
-        g = pull_back(v, u, extra[3, r] > 0.5, scale)
+            g = pull_back([t[n] for t in v], [t * inverse for t in total[1:]], wall > 0.5, scale)
+            for q in range(27):
+                if 0 <= x - Q[q][0] < rows:
+                    g1[q, 2 * (j % 2) + n] = g[q]
+
+
+def pulled_row(rows, x, arrays, speed, solid_in, scale, lane):
+    v = []
+    for q, (a, b, c) in enumerate(Q):
+        array, r = arrays(x + a)
+        main = array[q, r]
+        if b:
+            main = shift_y(main, turn(array[q, r + 1], -b, 1), b, lane)[0]
+        v.append(turn(main, -c, 0))
+    return pull_back(v, [speed[k, x] for k in range(3)], solid_in[x] > 0.5, scale)
+
+
+def low_kernel(rows, scale_in, speed, solid_in, own, merged, inner, known, raw, extra, done, g1):
+    scale = [scale_in[i] for i in range(27)]
+    lane = lanes()
+    outer_gradient(rows, -1, scale, solid_in, own, merged, known, raw, extra, g1)
+
+    def arrays(x):
+        return (g1, 2 * (x + 1)) if x < 1 else (inner, 2 * (x - 1))
+
+    for x in range(rows - 2):
+        result = pulled_row(rows, x, arrays, speed, solid_in, scale, lane)
         for q in range(27):
-            g1[q, r] = g[q]
-        return 0
-
-    lax.fori_loop(0, 2 * ring, one, 0)
+            done[q, x] = result[q]
+
+
+def last_kernel(rows, scale_in, speed, solid_in, own, merged, inner, known, done, from_high, out_hbm, high, out, sems):
+    scale = [scale_in[i] for i in range(27)]
+    lane = lanes()
+    outer_gradient(rows, 1, scale, solid_in, own, merged, known, from_high.at[0:27], from_high.at[27:36], high)
+
+    def arrays(x):
+        return (inner, 2 * (x - 1)) if x < rows - 1 else (high, 2 * (x - rows + 1))
+
     for x in range(rows):
-        v = []
-        for q, (a, b, c) in enumerate(Q):
-            r = 2 * (x + a + 1)
-            main = g1[q, r]
-            if b:
-                main = shift_y(main, turn(g1[q, r + 1], -b, 1), b, lane)[0]
-            v.append(turn(main, -c, 0))
-        result = pull_back(v, [speed[k, x] for k in range(3)], solid_in[x] > 0.5, scale)
+        if x < rows - 2:
+            result = [done[q, x] for q in range(27)]
+        else:
+            result = pulled_row(rows, x, arrays, speed, solid_in, scale, lane)
         for q in range(27):
             out[q, pl.ds(x, 8, stride=rows), :] = result[q]
-
-
-def call(kernel, name, out_shapes, scratch, operands, space=pltpu.VMEM):
+    copies = []
+    for piece in range(PIECES):
+        part = pl.ds(27 // PIECES * piece, 27 // PIECES)
+        copies.append(pltpu.make_async_copy(out.at[part], out_hbm.at[part], sems.at[piece]))
+    for copy in copies:
+        copy.start()
+    for copy in copies:
+        copy.wait()
+
+
+def call(kernel, name, out_shapes, scratch, operands, space=pltpu.VMEM, work=0, out_space=pltpu.VMEM):
     return pl.pallas_call(
         kernel,
         out_shape=[jax.ShapeDtypeStruct(s, F32) for s in out_shapes],
         in_specs=[pl.BlockSpec(memory_space=space)] * len(operands),
-        out_specs=[pl.BlockSpec(memory_space=pltpu.VMEM)] * len(out_shapes),
+        out_specs=[pl.BlockSpec(memory_space=out_space)] * len(out_shapes),
         scratch_shapes=scratch,
         compiler_params=pltpu.CompilerParams(vmem_limit_bytes=32 * 1024 * 1024),
+        cost_estimate=pl.CostEstimate(flops=work, bytes_accessed=0 if work else 0, transcendentals=0) if work else None,
         name=name,
     )(*operands)
 
@@ -393,6 +456,14 @@
 def ring(block, axis, step):
     size = lax.axis_size(axis)
     return lax.ppermute(block, axis, [(i, (i + step) % size) for i in range(size)])
+
+
+def swap(block, axis, first):
+    size = lax.axis_size(axis)
+    route = []
+    for i in range(first, size + first, 2):
+        route += [(i % size, (i + 1) % size), ((i + 1) % size, i % size)]
+    return lax.ppermute(block, axis, route)
 
 
 def shards(checkpoint, rates, wall_mask, cotangent):
@@ -402,26 +473,36 @@
     wall = wall_mask.reshape(planes * rows, width)
     tile = (planes, width)
     lattice = (27, planes * rows, width)
-    cot, scale, sums, speed, solid, packed = call(
+    cot, scale, sums, speed, solid, packed, raw_right = call(
         functools.partial(first_kernel, rows), "collide",
-        [lattice, (27,) + tile, (18, rows) + tile, (3, rows) + tile, (rows,) + tile, (3,) + tile],
+        [lattice, (27,) + tile, (18, rows) + tile, (3, rows) + tile, (rows,) + tile, (3,) + tile, (27,) + tile],
         [pltpu.SMEM((27,), F32), pltpu.VMEM(lattice, F32), pltpu.VMEM(lattice[1:], jnp.int32),
          pltpu.SemaphoreType.DMA((2 + 2 * PIECES,))],
         tuple(pltpu.with_memory_space_constraint(v, pltpu.HBM) for v in (rates, f, wall, cot)), pltpu.HBM)
-    from_right = ring(packed, "gy", -1)
-    from_left = ring(packed, "gy", 1)
-    to_left, to_right, own, merged = call(
+    raw_low = ring(raw_right, "gx", 1)
+    pairs = [swap(packed, "gy", first) for first in (0, 1)]
+    even = lax.axis_index("gy") % 2 == 0
+    from_right = jnp.where(even, pairs[0], pairs[1])
+    from_left = jnp.where(even, pairs[1], pairs[0])
+    to_left, small_right, own, merged = call(
         functools.partial(second_kernel, rows), "pack",
-        [(36,) + tile, (36,) + tile, (4, 2 * rows + 4) + tile, (3,) + tile], [],
+        [(36,) + tile, (9,) + tile, (4, 2 * rows + 4) + tile, (3,) + tile], [],
         (cot, sums, solid, from_left, from_right))
+    small_low = ring(small_right, "gx", 1)
     from_high = ring(to_left, "gx", -1)
-    from_low = ring(to_right, "gx", 1)
+    inner, known = call(
+        functools.partial(middle_kernel, rows), "inner_rows",
+        [(27, 2 * rows - 4) + tile, (27, 8) + tile], [],
+        (scale, cot, solid, own, merged))
+    (done,) = call(
+        functools.partial(low_kernel, rows), "low_rows",
+        [(27, rows - 2) + tile], [pltpu.VMEM((27, 4) + tile, F32)],
+        (scale, speed, solid, own, merged, inner, known, raw_low, small_low), work=2000000000)
     (out,) = call(
-        functools.partial(third_kernel, rows), "gradient",
+        functools.partial(last_kernel, rows), "gradient",
         [lattice],
-        [pltpu.VMEM((27, 2 * rows + 4) + tile, F32), pltpu.VMEM((27, 2 * rows + 4) + tile, F32),
-         pltpu.VMEM((4, 2 * rows + 4) + tile, F32)],
-        (scale, cot, speed, solid, own, merged, from_low, from_high))
+        [pltpu.VMEM((27, 4) + tile, F32), pltpu.VMEM(lattice, F32), pltpu.SemaphoreType.DMA((PIECES,))],
+        (scale, speed, solid, own, merged, inner, known, done, from_high), out_space=pltpu.HBM)
     return out.reshape(checkpoint.shape)
 
 

time: 19 us -> 17.9 us (0.942)
  waiting for transfers between devices: 7.46 us -> 4.4 us
  starting transfers between devices: 7.24 us -> 9.44 us
  Pallas kernels: 4.11 us -> 3.91 us
    ppermute x0 -> x2, starting transfers between devices: none -> 3.16 us  [swap(): return lax.ppermute(block, axis, route)]
    ppermute x4 -> x3, waiting for transfers between devices: 7.46 us -> 4.39 us  [ring(): lax.ppermute(block, axis, [(i, (i + step) % size) for i in range(size)])]
    ppermute x4 -> x3, starting transfers between devices: 7.24 us -> 6.28 us  [ring(): lax.ppermute(block, axis, [(i, (i + step) % size) for i in range(size)])]
    pallas_call x3 -> x5, Pallas kernels: 4.11 us -> 3.91 us  [call(): pl.pallas_call(kernel, out_shape=[jax.ShapeDtypeStruct(s, F32) for s in o...]
  transfers between devices with their start and end apart: 4 -> 5, of which waited for: 4 -> 2; matrix products, arithmetic and copies ran while one was open for 0% -> 0% of each run, Pallas kernels for 0% -> 6%
where the time goes in v4:
time: 17.9 us; the launch traced here: 17.8 us
  starting transfers between devices  9.44 us (53%)
  waiting for transfers between devices  4.4 us (25%)
  Pallas kernels  3.91 us (22%)
    ppermute x3, starting transfers between devices, ring(): lax.ppermute(block, axis, [(i, (i + step) % size) for i in range(size)])  6.28 us
    ppermute x3, waiting for transfers between devices, ring(): lax.ppermute(block, axis, [(i, (i + step) % size) for i in range(size)])  4.39 us
    pallas_call x5, Pallas kernels, call(): pl.pallas_call(kernel, out_shape=[jax.ShapeDtypeStruct(s, F32) for s in o...  3.91 us
    ppermute x2, starting transfers between devices, swap(): return lax.ppermute(block, axis, route)  3.16 us
  transfers between devices with their start and end apart: 5, of which 2 were waited for; matrix products, arithmetic and copies ran while one was open for 0% of the time, Pallas kernels for 6%

profile of v4, /device:TPU:0, one launch (start us, length us, event | category | flops | bytes accessed | tf_op | source)
XLA Modules:
  0.0 17.8 jit_solution(15706965544485075509)
XLA Ops:
  0.0 1.6 %collide.1 = (f32[27,32,128]{2,1,0:T(8,128)S(1)}, f32[27,8,128]{2,1,0:T(8,128)S(1)}, f32[18,4,8,128]{3,2,1,0:T(8,128)S(1)}, f32[3,4,8,128]{3,2,1,0:T(8,128)S(1)}...) custom-call(f32[27]{0:T(128)} %rates_in.1, f32[27,32,128]{2,1,0:T(8,128)} %bitcast.4, ...), custom_call_target="tpu_custom_call" | custom-call | tf_op jit(solution)/shard_map/collide/pallas_call | solution.py:444
  1.6 0.5 %collective-permute-start.1 = (f32[3,8,128]{2,1,0:T(8,128)S(1)}, f32[3,8,128]{2,1,0:T(8,128)S(1)}, u32[]{:S(2)}, u32[]{:S(2)}) collective-permute-start(f32[3,8,128]{2,1,0:T(8,128)S(1)} %get-tuple-element.23), channel_id=1, source_target_pairs={{0,1},{1,0},{2,3},{3,2},{4,5},{5,4},{6,7},{7,6},{8,9},{9,8},{10,11... | collective-permute-start | bytes 36872 | tf_op jit(solution)/shard_map/ppermute | solution.py:466
  2.2 2.6 %collective-permute-start = (f32[3,8,128]{2,1,0:T(8,128)S(1)}, f32[3,8,128]{2,1,0:T(8,128)S(1)}, u32[]{:S(2)}, u32[]{:S(2)}) collective-permute-start(f32[3,8,128]{2,1,0:T(8,128)S(1)} %get-tuple-element.23), channel_id=1, source_target_pairs={{1,2},{2,1},{3,0},{0,3},{5,6},{6,5},{7,4},{4,7},{9,10},{10,9},{11,... | collective-permute-start | bytes 36872 | tf_op jit(solution)/shard_map/ppermute | solution.py:466
  4.8 1.5 %collective-permute-start.2 = (f32[27,8,128]{2,1,0:T(8,128)S(1)}, f32[27,8,128]{2,1,0:T(8,128)S(1)}, u32[]{:S(2)}, u32[]{:S(2)}) collective-permute-start(f32[27,8,128]{2,1,0:T(8,128)S(1)} %get-tuple-element.28), channel_id=1, source_target_pairs={{0,4},{4,8},{8,12},{12,16},{16,20},{20,24},{24,28},{28,0},{1,5},{5... | collective-permute-start | bytes 331784 | tf_op jit(solution)/shard_map/ppermute | solution.py:458
  6.3 0.0 collective-permute-done.1
  6.3 0.0 collective-permute-done
  6.3 0.3 %pack.1 = (f32[36,8,128]{2,1,0:T(8,128)S(1)}, f32[9,8,128]{2,1,0:T(8,128)S(1)}, f32[4,12,8,128]{3,2,1,0:T(8,128)S(1)}, f32[3,8,128]{2,1,0:T(8,128)S(1)}) custom-call(f32[27,32,128]{2,1,0:T(8,128)S(1)} %get-tuple-element.21.cot, f32[18,4,8,128]{3,2,1,0:T(8,128)S(1)} %get-tuple-element.22.sums, f32[4,8,128]{2,1,0:T(8,128)S(1)} %get-tuple-element.20.solid_in, ...), custom_call_target="tpu_custom_call" | custom-call | tf_op jit(solution)/shard_map/pack/pallas_call | solution.py:444
  6.6 1.6 %collective-permute-start.3 = (f32[9,8,128]{2,1,0:T(8,128)S(1)}, f32[9,8,128]{2,1,0:T(8,128)S(1)}, u32[]{:S(2)}, u32[]{:S(2)}) collective-permute-start(f32[9,8,128]{2,1,0:T(8,128)S(1)} %get-tuple-element.29), channel_id=1, source_target_pairs={{0,4},{4,8},{8,12},{12,16},{16,20},{20,24},{24,28},{28,0},{1,5},{5... | collective-permute-start | bytes 110600 | tf_op jit(solution)/shard_map/ppermute | solution.py:458
  8.2 3.2 %collective-permute-start.4 = (f32[36,8,128]{2,1,0:T(8,128)S(1)}, f32[36,8,128]{2,1,0:T(8,128)S(1)}, u32[]{:S(2)}, u32[]{:S(2)}) collective-permute-start(f32[36,8,128]{2,1,0:T(8,128)S(1)} %get-tuple-element.30), channel_id=1, source_target_pairs={{0,28},{4,0},{8,4},{12,8},{16,12},{20,16},{24,20},{28,24},{1,29},{... | collective-permute-start | bytes 442376 | tf_op jit(solution)/shard_map/ppermute | solution.py:458
  11.4 0.4 %inner_rows.1 = (f32[27,4,8,128]{3,2,1,0:T(8,128)S(1)}, f32[27,8,8,128]{3,2,1,0:T(8,128)S(1)}) custom-call(f32[27,8,128]{2,1,0:T(8,128)S(1)} %get-tuple-element.18.scale_in, f32[27,32,128]{2,1,0:T(8,128)S(1)} %get-tuple-element.21.cot, f32[4,8,128]{2,1,0:T(8,128)S(1)} %get-tuple-element.20.solid_in, f32[4,12,8,128]{3,2,1,0:T(8,128)S(1)} %get-tuple-element.24.own, ...), custom_call_target="tpu_custom_call" | custom-call | tf_op jit(solution)/shard_map/inner_rows/pallas_call | solution.py:444
  11.8 1.7 %collective-permute-done.3.extra = f32[9,8,128]{2,1,0:T(8,128)S(1)} collective-permute-done((f32[9,8,128]{2,1,0:T(8,128)S(1)}, f32[9,8,128]{2,1,0:T(8,128)S(1)}, u32[]{:S(2)}, u32[]{:S(2)}) %collective-permute-start.3) | collective-permute-done | bytes 36896 | tf_op jit(solution)/shard_map/ppermute | solution.py:458
  13.5 0.0 collective-permute-done.2.raw
  13.5 0.4 %low_rows.1.done = f32[27,2,8,128]{3,2,1,0:T(8,128)S(1)} custom-call(f32[27,8,128]{2,1,0:T(8,128)S(1)} %get-tuple-element.18.scale_in, f32[3,4,8,128]{3,2,1,0:T(8,128)S(1)} %get-tuple-element.19.speed, f32[4,8,128]{2,1,0:T(8,128)S(1)} %get-tuple-element.20.solid_in, f32[4,12,8,128]{3,2,1,0:T(8,128)S(1)} %get-tuple-element.24.own, ...), custom_call_target="tpu_custom_call" | custom-call | flops 2000000000 | tf_op jit(solution)/shard_map/low_rows/pallas_call | solution.py:444
  13.9 2.7 %collective-permute-done.4.from_high = f32[36,8,128]{2,1,0:T(8,128)S(1)} collective-permute-done((f32[36,8,128]{2,1,0:T(8,128)S(1)}, f32[36,8,128]{2,1,0:T(8,128)S(1)}, u32[]{:S(2)}, u32[]{:S(2)}) %collective-permute-start.4) | collective-permute-done | bytes 147488 | tf_op jit(solution)/shard_map/ppermute | solution.py:458
  16.6 1.2 %gradient.1 = f32[27,32,128]{2,1,0:T(8,128)} custom-call(f32[27,8,128]{2,1,0:T(8,128)S(1)} %get-tuple-element.18.scale_in, f32[3,4,8,128]{3,2,1,0:T(8,128)S(1)} %get-tuple-element.19.speed, f32[4,8,128]{2,1,0:T(8,128)S(1)} %get-tuple-element.20.solid_in, f32[4,12,8,128]{3,2,1,0:T(8,128)S(1)} %get-tuple-element.24.own, ...), custom_call_target="tpu_custom_call" | custom-call | tf_op jit(solution)/shard_map/gradient/pallas_call | solution.py:444
  (1 shorter events, 0.0 us)
Async XLA Ops:
  1.6 4.7 %collective-permute-start.1 = (f32[3,8,128]{2,1,0:T(8,128)S(1)}, f32[3,8,128]{2,1,0:T(8,128)S(1)}, u32[]{:S(2)}, u32[]{:S(2)}) collective-permute-start(f32[3,8,128]{2,1,0:T(8,128)S(1)} %get-tuple-element.23), channel_id=1, source_target_pairs={{0,1},{1,0},{2,3},{3,2},{4,5},{5,4},{6,7},{7,6},{8,9},{9,8},{10,11... | collective-permute-start | bytes 36872 | tf_op jit(solution)/shard_map/ppermute | solution.py:466
  2.2 4.1 %collective-permute-start = (f32[3,8,128]{2,1,0:T(8,128)S(1)}, f32[3,8,128]{2,1,0:T(8,128)S(1)}, u32[]{:S(2)}, u32[]{:S(2)}) collective-permute-start(f32[3,8,128]{2,1,0:T(8,128)S(1)} %get-tuple-element.23), channel_id=1, source_target_pairs={{1,2},{2,1},{3,0},{0,3},{5,6},{6,5},{7,4},{4,7},{9,10},{10,9},{11,... | collective-permute-start | bytes 36872 | tf_op jit(solution)/shard_map/ppermute | solution.py:466
  4.8 8.7 %collective-permute-start.2 = (f32[27,8,128]{2,1,0:T(8,128)S(1)}, f32[27,8,128]{2,1,0:T(8,128)S(1)}, u32[]{:S(2)}, u32[]{:S(2)}) collective-permute-start(f32[27,8,128]{2,1,0:T(8,128)S(1)} %get-tuple-element.28), channel_id=1, source_target_pairs={{0,4},{4,8},{8,12},{12,16},{16,20},{20,24},{24,28},{28,0},{1,5},{5... | collective-permute-start | bytes 331784 | tf_op jit(solution)/shard_map/ppermute | solution.py:458
  6.6 6.9 %collective-permute-start.3 = (f32[9,8,128]{2,1,0:T(8,128)S(1)}, f32[9,8,128]{2,1,0:T(8,128)S(1)}, u32[]{:S(2)}, u32[]{:S(2)}) collective-permute-start(f32[9,8,128]{2,1,0:T(8,128)S(1)} %get-tuple-element.29), channel_id=1, source_target_pairs={{0,4},{4,8},{8,12},{12,16},{16,20},{20,24},{24,28},{28,0},{1,5},{5... | collective-permute-start | bytes 110600 | tf_op jit(solution)/shard_map/ppermute | solution.py:458
  8.2 8.4 %collective-permute-start.4 = (f32[36,8,128]{2,1,0:T(8,128)S(1)}, f32[36,8,128]{2,1,0:T(8,128)S(1)}, u32[]{:S(2)}, u32[]{:S(2)}) collective-permute-start(f32[36,8,128]{2,1,0:T(8,128)S(1)} %get-tuple-element.30), channel_id=1, source_target_pairs={{0,28},{4,0},{8,4},{12,8},{16,12},{20,16},{24,20},{28,24},{1,29},{... | collective-permute-start | bytes 442376 | tf_op jit(solution)/shard_map/ppermute | solution.py:458

commit v5 on v4

--- a/solution.py
+++ b/solution.py
@@ -208,7 +208,8 @@
                 sums[i + 1, x] = high - low
     for copy in copies[2 + PIECES:]:
         copy.wait()
-    raw_rows(rows, -1, cot, raw_right)
+    raw_rows(rows, -1, cot, raw_right, 0)
+    raw_right[RAW_ROWS:] = jnp.zeros((padded(RAW_ROWS) - RAW_ROWS, 128), F32)
     pieces = [jnp.zeros((8, 128), F32) for _ in range(3)]
     for key, (g, i, kind) in table.items():
         if key[0] == "v":
@@ -223,16 +224,40 @@
         packed[g] = pieces[g]
 
 
+FULL = 9
+
+
 def edge_rows(rows, side):
     near, far = (0, 1) if side == 1 else (rows - 1, rows - 2)
-    keys = [(q, near) for q, c in enumerate(Q) if c[0] == 0]
-    keys += [(q, near) for q, c in enumerate(Q) if c[0] == side]
+    keys = [(q, near) for q, c in enumerate(Q) if c[0] == side]
+    keys += [(q, near) for q, c in enumerate(Q) if c[0] == 0]
     return keys + [(q, far) for q, c in enumerate(Q) if c[0] == side]
 
 
-def raw_rows(rows, side, cot, message):
+def raw_at(k, gap):
+    return 8 * k if k < FULL else 8 * FULL + gap + 6 * (k - FULL)
+
+
+RAW_ROWS = 8 * FULL + 6 * 18
+SMALL_ROWS = 8 + 6 * 8
+
+
+def padded(count):
+    return (count + 7) // 8 * 8
+
+
+def raw_rows(rows, side, cot, message, gap):
     for k, (q, x) in enumerate(edge_rows(rows, side)):
-        message[k] = cot[q, pl.ds(x, 8, stride=rows), :]
+        at = raw_at(k, gap)
+        if k < FULL:
+            message[at:at + 8] = cot[q, pl.ds(x, 8, stride=rows), :]
+        else:
+            message[at:at + 6] = cot[q, pl.ds(x + rows * (1 + Q[q][2]), 6, stride=rows), :]
+
+
+def planes(ref, at):
+    start = min(at - 1, ref.shape[0] - 8)
+    return turn(ref[start:start + 8], 1 - (at - start), 0)
 
 
 def second_kernel(rows, cot, sums, solid_in, from_left, from_right, to_left, to_right, own, merged):
@@ -288,9 +313,13 @@
 
     for side, message in ((1, to_left), (-1, to_right)):
         near, far = (0, 1) if side == 1 else (rows - 1, rows - 2)
-        first = message.shape[0] - 9
-        if first:
-            raw_rows(rows, side, cot, message)
+        both_parts = message.shape[0] > SMALL_ROWS
+        at = 8 * FULL if both_parts else 0
+        items = RAW_ROWS + 8 if both_parts else 8
+        if both_parts:
+            raw_rows(rows, side, cot, message, 8)
+            end = RAW_ROWS + SMALL_ROWS
+            message[end:] = jnp.zeros((padded(end) - end, 128), F32)
         extra = []
         for n in range(2):
             row = list(t[-side, near][n])
@@ -301,10 +330,10 @@
             extra.append(row)
         columns = halo[0]
         for k in range(8):
-            message[first + k] = extra[0][k]
+            message[items + 6 * k:items + 6 * k + 6] = extra[0][k][1:7]
             i = used + 2 * k
             columns = jnp.where((lane == i) | (lane == i + 1), turn(extra[1][k], i + 1, 1), columns)
-        message[first + 8] = columns
+        message[at:at + 8] = columns
 
 
 def outer_rows(rows):
@@ -316,13 +345,13 @@
     a, b, c = Q[q]
     source = x + a
     if 0 <= source < rows:
-        main = cot[q, pl.ds(source, 8, stride=rows), :]
+        main = turn(cot[q, pl.ds(source, 8, stride=rows), :], -c, 0)
         group, i, kind = table["v", q, source]
     else:
-        message, group, k, i, kind = remote[q, source]
-        main = message[k]
+        load, group, i, kind = remote[q, source]
+        main = load()
     outer = incoming(turned[group, c], i, kind, b)
-    return shift_y(turn(main, -c, 0), outer, b, lane)
+    return shift_y(main, outer, b, lane)
 
 
 def middle_kernel(rows, scale_in, cot, solid_in, own, merged, inner, known):
@@ -349,14 +378,21 @@
                 known[q, 2 * j], known[q, 2 * j + 1] = gathered(rows, x, q, cot, turned, lane)
 
 
-def outer_gradient(rows, side, scale, solid_in, own, merged, known, raw, extra, g1):
+def outer_gradient(rows, side, scale, solid_in, own, merged, known, raw, gap, extra, columns_at, items_at, g1):
     lane = lanes()
     table, used = slots(rows)
     remote = {}
+    def load(k, c):
+        at = raw_at(k, gap)
+        return turn(raw[at:at + 8], -c, 0) if k < FULL else planes(raw, at)
+
     for k, (q, x) in enumerate(edge_rows(rows, side)):
         _, i, kind = table["v", q, x]
-        remote[q, x + side * rows] = (raw, "far", k, i, kind)
-    turned = {("far", c): turn(extra[8], -c, 0) for c in SIGNS}
+        remote[q, x + side * rows] = (functools.partial(load, k, Q[q][2]), "far", i, kind)
+    columns = extra[columns_at:columns_at + 8]
+    turned = {("far", c): turn(columns, -c, 0) for c in SIGNS}
+    plane = lax.broadcasted_iota(jnp.int32, (8, 128), 0)
+    boundary = (plane == 0) | (plane == 7)
     near = rows - 1 if side == 1 else 0
     for j, x in enumerate(outer_rows(rows)):
         if x not in (near, near + side):
@@ -369,7 +405,7 @@
                 v.append(gathered(rows, x, q, None, turned, lane, remote))
         for n in range(2):
             def got(k):
-                return extra[k] if n == 0 else incoming(extra[8], used + 2 * k, 0)
+                return planes(extra, items_at + 6 * k) if n == 0 else incoming(columns, used + 2 * k, 0)
 
             total = [own[k, 2 * (x + 1) + n] for k in range(4)]
             if x == near:
@@ -384,7 +420,7 @@
                 total = [total[k] + got(3 + k) for k in range(4)]
                 wall = got(7)
             inverse = 1.0 / total[0]
-            g = pull_back([t[n] for t in v], [t * inverse for t in total[1:]], wall > 0.5, scale)
+            g = pull_back([t[n] for t in v], [t * inverse for t in total[1:]], boundary | (wall > 0.5), scale)
             for q in range(27):
                 if 0 <= x - Q[q][0] < rows:
                     g1[q, 2 * (j % 2) + n] = g[q]
@@ -404,7 +440,7 @@
 def low_kernel(rows, scale_in, speed, solid_in, own, merged, inner, known, raw, extra, done, g1):
     scale = [scale_in[i] for i in range(27)]
     lane = lanes()
-    outer_gradient(rows, -1, scale, solid_in, own, merged, known, raw, extra, g1)
+    outer_gradient(rows, -1, scale, solid_in, own, merged, known, raw, 0, extra, 0, 8, g1)
 
     def arrays(x):
         return (g1, 2 * (x + 1)) if x < 1 else (inner, 2 * (x - 1))
@@ -418,7 +454,7 @@
 def last_kernel(rows, scale_in, speed, solid_in, own, merged, inner, known, done, from_high, out_hbm, high, out, sems):
     scale = [scale_in[i] for i in range(27)]
     lane = lanes()
-    outer_gradient(rows, 1, scale, solid_in, own, merged, known, from_high.at[0:27], from_high.at[27:36], high)
+    outer_gradient(rows, 1, scale, solid_in, own, merged, known, from_high, 8, from_high, 8 * FULL, RAW_ROWS + 8, high)
 
     def arrays(x):
         return (inner, 2 * (x - 1)) if x < rows - 1 else (high, 2 * (x - rows + 1))
@@ -475,7 +511,8 @@
     lattice = (27, planes * rows, width)
     cot, scale, sums, speed, solid, packed, raw_right = call(
         functools.partial(first_kernel, rows), "collide",
-        [lattice, (27,) + tile, (18, rows) + tile, (3, rows) + tile, (rows,) + tile, (3,) + tile, (27,) + tile],
+        [lattice, (27,) + tile, (18, rows) + tile, (3, rows) + tile, (rows,) + tile, (3,) + tile,
+         (padded(RAW_ROWS), width)],
         [pltpu.SMEM((27,), F32), pltpu.VMEM(lattice, F32), pltpu.VMEM(lattice[1:], jnp.int32),
          pltpu.SemaphoreType.DMA((2 + 2 * PIECES,))],
         tuple(pltpu.with_memory_space_constraint(v, pltpu.HBM) for v in (rates, f, wall, cot)), pltpu.HBM)
@@ -486,7 +523,7 @@
     from_left = jnp.where(even, pairs[1], pairs[0])
     to_left, small_right, own, merged = call(
         functools.partial(second_kernel, rows), "pack",
-        [(36,) + tile, (9,) + tile, (4, 2 * rows + 4) + tile, (3,) + tile], [],
+        [(padded(RAW_ROWS + SMALL_ROWS), width), (SMALL_ROWS, width), (4, 2 * rows + 4) + tile, (3,) + tile], [],
         (cot, sums, solid, from_left, from_right))
     small_low = ring(small_right, "gx", 1)
     from_high = ring(to_left, "gx", -1)

time: 17.9 us -> 16.9 us (0.944)
  waiting for transfers between devices: 4.4 us -> 3.33 us
    ppermute x3, waiting for transfers between devices: 4.39 us -> 3.33 us  [ring(): lax.ppermute(block, axis, [(i, (i + step) % size) for i in range(size)])]
where the time goes in v5:
time: 16.9 us; the launch traced here: 16.7 us
  starting transfers between devices  9.44 us (56%)
  Pallas kernels  3.94 us (23%)
  waiting for transfers between devices  3.33 us (20%)
    ppermute x3, starting transfers between devices, ring(): lax.ppermute(block, axis, [(i, (i + step) % size) for i in range(size)])  6.28 us
    pallas_call x5, Pallas kernels, call(): pl.pallas_call(kernel, out_shape=[jax.ShapeDtypeStruct(s, F32) for s in o...  3.94 us
    ppermute x3, waiting for transfers between devices, ring(): lax.ppermute(block, axis, [(i, (i + step) % size) for i in range(size)])  3.33 us
    ppermute x2, starting transfers between devices, swap(): return lax.ppermute(block, axis, route)  3.16 us
  transfers between devices with their start and end apart: 5, of which 2 were waited for; matrix products, arithmetic and copies ran while one was open for 0% of the time, Pallas kernels for 6%

profile of v5, /device:TPU:0, one launch (start us, length us, event | category | flops | bytes accessed | tf_op | source)
XLA Modules:
  0.0 16.7 jit_solution(1292787662123515126)
XLA Ops:
  0.0 1.6 %collide.1 = (f32[27,32,128]{2,1,0:T(8,128)S(1)}, f32[27,8,128]{2,1,0:T(8,128)S(1)}, f32[18,4,8,128]{3,2,1,0:T(8,128)S(1)}, f32[3,4,8,128]{3,2,1,0:T(8,128)S(1)}...) custom-call(f32[27]{0:T(128)} %rates_in.1, f32[27,32,128]{2,1,0:T(8,128)} %bitcast.4, ...), custom_call_target="tpu_custom_call" | custom-call | tf_op jit(solution)/shard_map/collide/pallas_call | solution.py:480
  1.6 0.5 %collective-permute-start.1 = (f32[3,8,128]{2,1,0:T(8,128)S(1)}, f32[3,8,128]{2,1,0:T(8,128)S(1)}, u32[]{:S(2)}, u32[]{:S(2)}) collective-permute-start(f32[3,8,128]{2,1,0:T(8,128)S(1)} %get-tuple-element.23), channel_id=1, source_target_pairs={{0,1},{1,0},{2,3},{3,2},{4,5},{5,4},{6,7},{7,6},{8,9},{9,8},{10,11... | collective-permute-start | bytes 36872 | tf_op jit(solution)/shard_map/ppermute | solution.py:502
  2.2 2.6 %collective-permute-start = (f32[3,8,128]{2,1,0:T(8,128)S(1)}, f32[3,8,128]{2,1,0:T(8,128)S(1)}, u32[]{:S(2)}, u32[]{:S(2)}) collective-permute-start(f32[3,8,128]{2,1,0:T(8,128)S(1)} %get-tuple-element.23), channel_id=1, source_target_pairs={{1,2},{2,1},{3,0},{0,3},{5,6},{6,5},{7,4},{4,7},{9,10},{10,9},{11,... | collective-permute-start | bytes 36872 | tf_op jit(solution)/shard_map/ppermute | solution.py:502
  4.8 1.5 %collective-permute-start.2 = (f32[184,128]{1,0:T(8,128)S(1)}, f32[184,128]{1,0:T(8,128)S(1)}, u32[]{:S(2)}, u32[]{:S(2)}) collective-permute-start(f32[184,128]{1,0:T(8,128)S(1)} %get-tuple-element.28), channel_id=1, source_target_pairs={{0,4},{4,8},{8,12},{12,16},{16,20},{20,24},{24,28},{28,0},{1,5},{5... | collective-permute-start | bytes 282632 | tf_op jit(solution)/shard_map/ppermute | solution.py:494
  6.3 0.0 collective-permute-done.1
  6.3 0.0 collective-permute-done
  6.3 0.3 %pack.1 = (f32[240,128]{1,0:T(8,128)S(1)}, f32[56,128]{1,0:T(8,128)S(1)}, f32[4,12,8,128]{3,2,1,0:T(8,128)S(1)}, f32[3,8,128]{2,1,0:T(8,128)S(1)}) custom-call(f32[27,32,128]{2,1,0:T(8,128)S(1)} %get-tuple-element.21.cot, f32[18,4,8,128]{3,2,1,0:T(8,128)S(1)} %get-tuple-element.22.sums, f32[4,8,128]{2,1,0:T(8,128)S(1)} %get-tuple-element.20.solid_in, ...), custom_call_target="tpu_custom_call" | custom-call | tf_op jit(solution)/shard_map/pack/pallas_call | solution.py:480
  6.6 1.6 %collective-permute-start.3 = (f32[56,128]{1,0:T(8,128)S(1)}, f32[56,128]{1,0:T(8,128)S(1)}, u32[]{:S(2)}, u32[]{:S(2)}) collective-permute-start(f32[56,128]{1,0:T(8,128)S(1)} %get-tuple-element.29), channel_id=1, source_target_pairs={{0,4},{4,8},{8,12},{12,16},{16,20},{20,24},{24,28},{28,0},{1,5},{5... | collective-permute-start | bytes 86024 | tf_op jit(solution)/shard_map/ppermute | solution.py:494
  8.2 3.2 %collective-permute-start.4 = (f32[240,128]{1,0:T(8,128)S(1)}, f32[240,128]{1,0:T(8,128)S(1)}, u32[]{:S(2)}, u32[]{:S(2)}) collective-permute-start(f32[240,128]{1,0:T(8,128)S(1)} %get-tuple-element.30), channel_id=1, source_target_pairs={{0,28},{4,0},{8,4},{12,8},{16,12},{20,16},{24,20},{28,24},{1,29},{... | collective-permute-start | bytes 368648 | tf_op jit(solution)/shard_map/ppermute | solution.py:494
  11.4 0.4 %inner_rows.1 = (f32[27,4,8,128]{3,2,1,0:T(8,128)S(1)}, f32[27,8,8,128]{3,2,1,0:T(8,128)S(1)}) custom-call(f32[27,8,128]{2,1,0:T(8,128)S(1)} %get-tuple-element.18.scale_in, f32[27,32,128]{2,1,0:T(8,128)S(1)} %get-tuple-element.21.cot, f32[4,8,128]{2,1,0:T(8,128)S(1)} %get-tuple-element.20.solid_in, f32[4,12,8,128]{3,2,1,0:T(8,128)S(1)} %get-tuple-element.24.own, ...), custom_call_target="tpu_custom_call" | custom-call | tf_op jit(solution)/shard_map/inner_rows/pallas_call | solution.py:480
  11.8 1.5 %collective-permute-done.3.extra = f32[56,128]{1,0:T(8,128)S(1)} collective-permute-done((f32[56,128]{1,0:T(8,128)S(1)}, f32[56,128]{1,0:T(8,128)S(1)}, u32[]{:S(2)}, u32[]{:S(2)}) %collective-permute-start.3) | collective-permute-done | bytes 28704 | tf_op jit(solution)/shard_map/ppermute | solution.py:494
  13.3 0.0 collective-permute-done.2.raw
  13.3 0.4 %low_rows.1.done = f32[27,2,8,128]{3,2,1,0:T(8,128)S(1)} custom-call(f32[27,8,128]{2,1,0:T(8,128)S(1)} %get-tuple-element.18.scale_in, f32[3,4,8,128]{3,2,1,0:T(8,128)S(1)} %get-tuple-element.19.speed, f32[4,8,128]{2,1,0:T(8,128)S(1)} %get-tuple-element.20.solid_in, f32[4,12,8,128]{3,2,1,0:T(8,128)S(1)} %get-tuple-element.24.own, ...), custom_call_target="tpu_custom_call" | custom-call | flops 2000000000 | tf_op jit(solution)/shard_map/low_rows/pallas_call | solution.py:480
  13.7 1.9 %collective-permute-done.4.from_high = f32[240,128]{1,0:T(8,128)S(1)} collective-permute-done((f32[240,128]{1,0:T(8,128)S(1)}, f32[240,128]{1,0:T(8,128)S(1)}, u32[]{:S(2)}, u32[]{:S(2)}) %collective-permute-start.4) | collective-permute-done | bytes 122912 | tf_op jit(solution)/shard_map/ppermute | solution.py:494
  15.5 1.2 %gradient.1 = f32[27,32,128]{2,1,0:T(8,128)} custom-call(f32[27,8,128]{2,1,0:T(8,128)S(1)} %get-tuple-element.18.scale_in, f32[3,4,8,128]{3,2,1,0:T(8,128)S(1)} %get-tuple-element.19.speed, f32[4,8,128]{2,1,0:T(8,128)S(1)} %get-tuple-element.20.solid_in, f32[4,12,8,128]{3,2,1,0:T(8,128)S(1)} %get-tuple-element.24.own, ...), custom_call_target="tpu_custom_call" | custom-call | tf_op jit(solution)/shard_map/gradient/pallas_call | solution.py:480
  (1 shorter events, 0.0 us)
Async XLA Ops:
  1.6 4.7 %collective-permute-start.1 = (f32[3,8,128]{2,1,0:T(8,128)S(1)}, f32[3,8,128]{2,1,0:T(8,128)S(1)}, u32[]{:S(2)}, u32[]{:S(2)}) collective-permute-start(f32[3,8,128]{2,1,0:T(8,128)S(1)} %get-tuple-element.23), channel_id=1, source_target_pairs={{0,1},{1,0},{2,3},{3,2},{4,5},{5,4},{6,7},{7,6},{8,9},{9,8},{10,11... | collective-permute-start | bytes 36872 | tf_op jit(solution)/shard_map/ppermute | solution.py:502
  2.2 4.1 %collective-permute-start = (f32[3,8,128]{2,1,0:T(8,128)S(1)}, f32[3,8,128]{2,1,0:T(8,128)S(1)}, u32[]{:S(2)}, u32[]{:S(2)}) collective-permute-start(f32[3,8,128]{2,1,0:T(8,128)S(1)} %get-tuple-element.23), channel_id=1, source_target_pairs={{1,2},{2,1},{3,0},{0,3},{5,6},{6,5},{7,4},{4,7},{9,10},{10,9},{11,... | collective-permute-start | bytes 36872 | tf_op jit(solution)/shard_map/ppermute | solution.py:502
  4.8 8.4 %collective-permute-start.2 = (f32[184,128]{1,0:T(8,128)S(1)}, f32[184,128]{1,0:T(8,128)S(1)}, u32[]{:S(2)}, u32[]{:S(2)}) collective-permute-start(f32[184,128]{1,0:T(8,128)S(1)} %get-tuple-element.28), channel_id=1, source_target_pairs={{0,4},{4,8},{8,12},{12,16},{16,20},{20,24},{24,28},{28,0},{1,5},{5... | collective-permute-start | bytes 282632 | tf_op jit(solution)/shard_map/ppermute | solution.py:494
  6.6 6.7 %collective-permute-start.3 = (f32[56,128]{1,0:T(8,128)S(1)}, f32[56,128]{1,0:T(8,128)S(1)}, u32[]{:S(2)}, u32[]{:S(2)}) collective-permute-start(f32[56,128]{1,0:T(8,128)S(1)} %get-tuple-element.29), channel_id=1, source_target_pairs={{0,4},{4,8},{8,12},{12,16},{16,20},{20,24},{24,28},{28,0},{1,5},{5... | collective-permute-start | bytes 86024 | tf_op jit(solution)/shard_map/ppermute | solution.py:494
  8.2 7.3 %collective-permute-start.4 = (f32[240,128]{1,0:T(8,128)S(1)}, f32[240,128]{1,0:T(8,128)S(1)}, u32[]{:S(2)}, u32[]{:S(2)}) collective-permute-start(f32[240,128]{1,0:T(8,128)S(1)} %get-tuple-element.30), channel_id=1, source_target_pairs={{0,28},{4,0},{8,4},{12,8},{16,12},{20,16},{24,20},{28,24},{1,29},{... | collective-permute-start | bytes 368648 | tf_op jit(solution)/shard_map/ppermute | solution.py:494

commit v6 on v5

--- a/solution.py
+++ b/solution.py
@@ -169,7 +169,7 @@
     return [jnp.where(solid, v[26 - q], v[q] - h[q]) for q in range(27)]
 
 
-PIECES = 3
+PIECES = 1
 
 
 def first_kernel(rows, rates_in, f_in, wall_in, cot_in, cot, scale_out, sums, speed, solid_out, packed,
@@ -517,10 +517,10 @@
          pltpu.SemaphoreType.DMA((2 + 2 * PIECES,))],
         tuple(pltpu.with_memory_space_constraint(v, pltpu.HBM) for v in (rates, f, wall, cot)), pltpu.HBM)
     raw_low = ring(raw_right, "gx", 1)
-    pairs = [swap(packed, "gy", first) for first in (0, 1)]
-    even = lax.axis_index("gy") % 2 == 0
-    from_right = jnp.where(even, pairs[0], pairs[1])
-    from_left = jnp.where(even, pairs[1], pairs[0])
+    across, inside = swap(packed, "gy", 1), swap(packed, "gy", 0)
+    odd = lax.axis_index("gy") % 2 == 1
+    from_left = jnp.where(odd, inside, across)
+    from_right = jnp.where(odd, across, inside)
     to_left, small_right, own, merged = call(
         functools.partial(second_kernel, rows), "pack",
         [(padded(RAW_ROWS + SMALL_ROWS), width), (SMALL_ROWS, width), (4, 2 * rows + 4) + tile, (3,) + tile], [],

time: 16.9 us -> 16.7 us (0.988)
  no operation moved by 1% of the time
where the time goes in v6:
time: 16.7 us; the launch traced here: 16.6 us
  starting transfers between devices  9.41 us (56%)
  Pallas kernels  3.85 us (23%)
  waiting for transfers between devices  3.29 us (20%)
    ppermute x3, starting transfers between devices, ring(): lax.ppermute(block, axis, [(i, (i + step) % size) for i in range(size)])  6.27 us
    pallas_call x5, Pallas kernels, call(): pl.pallas_call(kernel, out_shape=[jax.ShapeDtypeStruct(s, F32) for s in o...  3.85 us
    ppermute x3, waiting for transfers between devices, ring(): lax.ppermute(block, axis, [(i, (i + step) % size) for i in range(size)])  3.28 us
    ppermute x2, starting transfers between devices, swap(): return lax.ppermute(block, axis, route)  3.15 us
  transfers between devices with their start and end apart: 5, of which 2 were waited for; matrix products, arithmetic and copies ran while one was open for 0% of the time, Pallas kernels for 6%

profile of v6, /device:TPU:0, one launch (start us, length us, event | category | flops | bytes accessed | tf_op | source)
XLA Modules:
  0.0 16.6 jit_solution(6170380278006567056)
XLA Ops:
  0.0 1.6 %collide.1 = (f32[27,32,128]{2,1,0:T(8,128)S(1)}, f32[27,8,128]{2,1,0:T(8,128)S(1)}, f32[18,4,8,128]{3,2,1,0:T(8,128)S(1)}, f32[3,4,8,128]{3,2,1,0:T(8,128)S(1)}...) custom-call(f32[27]{0:T(128)} %rates_in.1, f32[27,32,128]{2,1,0:T(8,128)} %bitcast.4, ...), custom_call_target="tpu_custom_call" | custom-call | tf_op jit(solution)/shard_map/collide/pallas_call | solution.py:480
  1.6 2.5 %collective-permute-start.1 = (f32[3,8,128]{2,1,0:T(8,128)S(1)}, f32[3,8,128]{2,1,0:T(8,128)S(1)}, u32[]{:S(2)}, u32[]{:S(2)}) collective-permute-start(f32[3,8,128]{2,1,0:T(8,128)S(1)} %get-tuple-element.23), channel_id=1, source_target_pairs={{1,2},{2,1},{3,0},{0,3},{5,6},{6,5},{7,4},{4,7},{9,10},{10,9},{11,... | collective-permute-start | bytes 36872 | tf_op jit(solution)/shard_map/ppermute | solution.py:502
  4.0 0.7 %collective-permute-start = (f32[3,8,128]{2,1,0:T(8,128)S(1)}, f32[3,8,128]{2,1,0:T(8,128)S(1)}, u32[]{:S(2)}, u32[]{:S(2)}) collective-permute-start(f32[3,8,128]{2,1,0:T(8,128)S(1)} %get-tuple-element.23), channel_id=1, source_target_pairs={{0,1},{1,0},{2,3},{3,2},{4,5},{5,4},{6,7},{7,6},{8,9},{9,8},{10,11... | collective-permute-start | bytes 36872 | tf_op jit(solution)/shard_map/ppermute | solution.py:502
  4.7 1.5 %collective-permute-start.2 = (f32[184,128]{1,0:T(8,128)S(1)}, f32[184,128]{1,0:T(8,128)S(1)}, u32[]{:S(2)}, u32[]{:S(2)}) collective-permute-start(f32[184,128]{1,0:T(8,128)S(1)} %get-tuple-element.28), channel_id=1, source_target_pairs={{0,4},{4,8},{8,12},{12,16},{16,20},{20,24},{24,28},{28,0},{1,5},{5... | collective-permute-start | bytes 282632 | tf_op jit(solution)/shard_map/ppermute | solution.py:494
  6.2 0.0 collective-permute-done.1
  6.2 0.0 collective-permute-done
  6.2 0.3 %pack.1 = (f32[240,128]{1,0:T(8,128)S(1)}, f32[56,128]{1,0:T(8,128)S(1)}, f32[4,12,8,128]{3,2,1,0:T(8,128)S(1)}, f32[3,8,128]{2,1,0:T(8,128)S(1)}) custom-call(f32[27,32,128]{2,1,0:T(8,128)S(1)} %get-tuple-element.21.cot, f32[18,4,8,128]{3,2,1,0:T(8,128)S(1)} %get-tuple-element.22.sums, f32[4,8,128]{2,1,0:T(8,128)S(1)} %get-tuple-element.20.solid_in, ...), custom_call_target="tpu_custom_call" | custom-call | tf_op jit(solution)/shard_map/pack/pallas_call | solution.py:480
  6.5 1.6 %collective-permute-start.3 = (f32[56,128]{1,0:T(8,128)S(1)}, f32[56,128]{1,0:T(8,128)S(1)}, u32[]{:S(2)}, u32[]{:S(2)}) collective-permute-start(f32[56,128]{1,0:T(8,128)S(1)} %get-tuple-element.29), channel_id=1, source_target_pairs={{0,4},{4,8},{8,12},{12,16},{16,20},{20,24},{24,28},{28,0},{1,5},{5... | collective-permute-start | bytes 86024 | tf_op jit(solution)/shard_map/ppermute | solution.py:494
  8.1 3.2 %collective-permute-start.4 = (f32[240,128]{1,0:T(8,128)S(1)}, f32[240,128]{1,0:T(8,128)S(1)}, u32[]{:S(2)}, u32[]{:S(2)}) collective-permute-start(f32[240,128]{1,0:T(8,128)S(1)} %get-tuple-element.30), channel_id=1, source_target_pairs={{0,28},{4,0},{8,4},{12,8},{16,12},{20,16},{24,20},{28,24},{1,29},{... | collective-permute-start | bytes 368648 | tf_op jit(solution)/shard_map/ppermute | solution.py:494
  11.3 0.4 %inner_rows.1 = (f32[27,4,8,128]{3,2,1,0:T(8,128)S(1)}, f32[27,8,8,128]{3,2,1,0:T(8,128)S(1)}) custom-call(f32[27,8,128]{2,1,0:T(8,128)S(1)} %get-tuple-element.18.scale_in, f32[27,32,128]{2,1,0:T(8,128)S(1)} %get-tuple-element.21.cot, f32[4,8,128]{2,1,0:T(8,128)S(1)} %get-tuple-element.20.solid_in, f32[4,12,8,128]{3,2,1,0:T(8,128)S(1)} %get-tuple-element.24.own, ...), custom_call_target="tpu_custom_call" | custom-call | tf_op jit(solution)/shard_map/inner_rows/pallas_call | solution.py:480
  11.7 1.5 %collective-permute-done.3.extra = f32[56,128]{1,0:T(8,128)S(1)} collective-permute-done((f32[56,128]{1,0:T(8,128)S(1)}, f32[56,128]{1,0:T(8,128)S(1)}, u32[]{:S(2)}, u32[]{:S(2)}) %collective-permute-start.3) | collective-permute-done | bytes 28704 | tf_op jit(solution)/shard_map/ppermute | solution.py:494
  13.2 0.0 collective-permute-done.2.raw
  13.2 0.4 %low_rows.1.done = f32[27,2,8,128]{3,2,1,0:T(8,128)S(1)} custom-call(f32[27,8,128]{2,1,0:T(8,128)S(1)} %get-tuple-element.18.scale_in, f32[3,4,8,128]{3,2,1,0:T(8,128)S(1)} %get-tuple-element.19.speed, f32[4,8,128]{2,1,0:T(8,128)S(1)} %get-tuple-element.20.solid_in, f32[4,12,8,128]{3,2,1,0:T(8,128)S(1)} %get-tuple-element.24.own, ...), custom_call_target="tpu_custom_call" | custom-call | flops 2000000000 | tf_op jit(solution)/shard_map/low_rows/pallas_call | solution.py:480
  13.6 1.8 %collective-permute-done.4.from_high = f32[240,128]{1,0:T(8,128)S(1)} collective-permute-done((f32[240,128]{1,0:T(8,128)S(1)}, f32[240,128]{1,0:T(8,128)S(1)}, u32[]{:S(2)}, u32[]{:S(2)}) %collective-permute-start.4) | collective-permute-done | bytes 122912 | tf_op jit(solution)/shard_map/ppermute | solution.py:494
  15.4 1.2 %gradient.1 = f32[27,32,128]{2,1,0:T(8,128)} custom-call(f32[27,8,128]{2,1,0:T(8,128)S(1)} %get-tuple-element.18.scale_in, f32[3,4,8,128]{3,2,1,0:T(8,128)S(1)} %get-tuple-element.19.speed, f32[4,8,128]{2,1,0:T(8,128)S(1)} %get-tuple-element.20.solid_in, f32[4,12,8,128]{3,2,1,0:T(8,128)S(1)} %get-tuple-element.24.own, ...), custom_call_target="tpu_custom_call" | custom-call | tf_op jit(solution)/shard_map/gradient/pallas_call | solution.py:480
  (1 shorter events, 0.0 us)
Async XLA Ops:
  1.6 4.6 %collective-permute-start.1 = (f32[3,8,128]{2,1,0:T(8,128)S(1)}, f32[3,8,128]{2,1,0:T(8,128)S(1)}, u32[]{:S(2)}, u32[]{:S(2)}) collective-permute-start(f32[3,8,128]{2,1,0:T(8,128)S(1)} %get-tuple-element.23), channel_id=1, source_target_pairs={{1,2},{2,1},{3,0},{0,3},{5,6},{6,5},{7,4},{4,7},{9,10},{10,9},{11,... | collective-permute-start | bytes 36872 | tf_op jit(solution)/shard_map/ppermute | solution.py:502
  4.0 2.2 %collective-permute-start = (f32[3,8,128]{2,1,0:T(8,128)S(1)}, f32[3,8,128]{2,1,0:T(8,128)S(1)}, u32[]{:S(2)}, u32[]{:S(2)}) collective-permute-start(f32[3,8,128]{2,1,0:T(8,128)S(1)} %get-tuple-element.23), channel_id=1, source_target_pairs={{0,1},{1,0},{2,3},{3,2},{4,5},{5,4},{6,7},{7,6},{8,9},{9,8},{10,11... | collective-permute-start | bytes 36872 | tf_op jit(solution)/shard_map/ppermute | solution.py:502
  4.7 8.4 %collective-permute-start.2 = (f32[184,128]{1,0:T(8,128)S(1)}, f32[184,128]{1,0:T(8,128)S(1)}, u32[]{:S(2)}, u32[]{:S(2)}) collective-permute-start(f32[184,128]{1,0:T(8,128)S(1)} %get-tuple-element.28), channel_id=1, source_target_pairs={{0,4},{4,8},{8,12},{12,16},{16,20},{20,24},{24,28},{28,0},{1,5},{5... | collective-permute-start | bytes 282632 | tf_op jit(solution)/shard_map/ppermute | solution.py:494
  6.5 6.7 %collective-permute-start.3 = (f32[56,128]{1,0:T(8,128)S(1)}, f32[56,128]{1,0:T(8,128)S(1)}, u32[]{:S(2)}, u32[]{:S(2)}) collective-permute-start(f32[56,128]{1,0:T(8,128)S(1)} %get-tuple-element.29), channel_id=1, source_target_pairs={{0,4},{4,8},{8,12},{12,16},{16,20},{20,24},{24,28},{28,0},{1,5},{5... | collective-permute-start | bytes 86024 | tf_op jit(solution)/shard_map/ppermute | solution.py:494
  8.1 7.3 %collective-permute-start.4 = (f32[240,128]{1,0:T(8,128)S(1)}, f32[240,128]{1,0:T(8,128)S(1)}, u32[]{:S(2)}, u32[]{:S(2)}) collective-permute-start(f32[240,128]{1,0:T(8,128)S(1)} %get-tuple-element.30), channel_id=1, source_target_pairs={{0,28},{4,0},{8,4},{12,8},{16,12},{20,16},{24,20},{28,24},{1,29},{... | collective-permute-start | bytes 368648 | tf_op jit(solution)/shard_map/ppermute | solution.py:494

commit v7 on v6

--- a/solution.py
+++ b/solution.py
@@ -69,10 +69,10 @@
     return jnp.where(edge, rolled_outer, rolled), jnp.where(edge, rolled, rolled_outer)
 
 
-def along(values, pass_):
+def along(values, pass_, steps=(1, 3, 9)):
     values = list(values)
-    for step in (1, 3, 9):
-        for start in range(27):
+    for step in steps:
+        for start in range(len(values)):
             if (start // step) % 3 == 0:
                 at = (start, start + step, start + 2 * step)
                 for i, new in zip(at, pass_(*[values[j] for j in at])):
@@ -95,11 +95,9 @@
     return along(values, lambda m0, m1, m2: (m2 - m1, m0 - (m2 + m2), m2 + m1))
 
 
-def from_dual(values):
-    def pass_(z0, z1, z2):
-        both = z0 + z2
-        return both - z1, z0, both + z1
-    return along(values, pass_)
+def dual_back(z0, z1, z2):
+    both = z0 + z2
+    return both - z1, z0, both + z1
 
 
 def collide(f, solid, scale):
@@ -137,10 +135,7 @@
     return out, (ux, uy, uz)
 
 
-def pull_back(v, u, solid, scale):
-    ux, uy, uz = u
-    z = [y * s for y, s in zip(dual_moments(v), scale)]
-
+def low_rank(z):
     def at(i, j, k):
         return z[mi(i, j, k)]
 
@@ -157,33 +152,71 @@
     q_xy = at(1, 1, 0) + at(1, 1, 2) * third
     q_xz = at(1, 0, 1) + at(1, 2, 1) * third
     q_yz = at(0, 1, 1) + at(2, 1, 1) * third
+    return base, (b_x, b_y, b_z), (q_xx, q_yy, q_zz, q_xy, q_xz, q_yz)
+
+
+def form(coefficients, u):
+    q_xx, q_yy, q_zz, q_xy, q_xz, q_yz = coefficients
+    ux, uy, uz = u
     p_x = (q_xx + q_xx) * ux + q_xy * uy + q_xz * uz
     p_y = q_xy * ux + (q_yy + q_yy) * uy + q_yz * uz
     p_z = q_xz * ux + q_yz * uy + (q_zz + q_zz) * uz
-    quad = (p_x * ux + p_y * uy + p_z * uz) * 0.5
+    return p_x, p_y, p_z, (p_x * ux + p_y * uy + p_z * uz) * 0.5
+
+
+def pull_back_parts(v, u, solid, scale):
+    z = [y * s for y, s in zip(dual_moments(v), scale)]
+    base, (b_x, b_y, b_z), coefficients = low_rank(z)
+    p_x, p_y, p_z, quad = form(coefficients, u)
     z[0] = z[0] - (base - quad)
     z[mi(1, 0, 0)] = z[mi(1, 0, 0)] - (b_x + p_x)
     z[mi(0, 1, 0)] = z[mi(0, 1, 0)] - (b_y + p_y)
     z[mi(0, 0, 1)] = z[mi(0, 0, 1)] - (b_z + p_z)
-    h = from_dual(z)
-    return [jnp.where(solid, v[26 - q], v[q] - h[q]) for q in range(27)]
-
-
-PIECES = 1
+    h = along(z, dual_back, (9, 3))
+    for a in range(3):
+        part = along(h[9 * a:9 * a + 9], dual_back, (1,))
+        yield [jnp.where(solid, v[26 - q], v[q] - part[q - 9 * a]) for q in range(9 * a, 9 * a + 9)]
+
+
+def pull_back(v, u, solid, scale):
+    return sum(pull_back_parts(v, u, solid, scale), [])
+
+
+def side_pull_back(groups, side, scale):
+    def pass_(lo, mid, hi):
+        return mid, hi - lo, (hi - mid) + (lo - mid)
+
+    t = {a: along(values, pass_, (1, 3)) for a, values in groups.items()}
+    if side in t:
+        still, moved = t[0], t[side]
+        first = moved if side == 1 else [-v for v in moved]
+        second = [(v - m) - m for v, m in zip(moved, still)]
+    else:
+        moved = t[-side]
+        still = [jnp.zeros_like(v) for v in moved]
+        first = moved if side == -1 else [-v for v in moved]
+        second = moved
+    z = [y * s for y, s in zip(list(still) + list(first) + list(second), scale)]
+    base, (b_x, b_y, b_z), coefficients = low_rank(z)
+    z[0] = z[0] - base
+    z[mi(1, 0, 0)] = z[mi(1, 0, 0)] - b_x
+    z[mi(0, 1, 0)] = z[mi(0, 1, 0)] - b_y
+    z[mi(0, 0, 1)] = z[mi(0, 0, 1)] - b_z
+    h = [(z[i] + z[18 + i]) + z[9 + i] if side == 1 else (z[i] + z[18 + i]) - z[9 + i] for i in range(9)]
+    h = along(h, dual_back, (1, 3))
+    if side in groups:
+        return [v - w for v, w in zip(groups[side], h)], coefficients
+    return [-w for w in h], coefficients
 
 
 def first_kernel(rows, rates_in, f_in, wall_in, cot_in, cot, scale_out, sums, speed, solid_out, packed,
                  raw_right,
                  rates, f, wall, sems):
-    copies = [pltpu.make_async_copy(rates_in, rates, sems.at[0]), pltpu.make_async_copy(wall_in, wall, sems.at[1])]
-    for array, (source, target) in enumerate(((f_in, f), (cot_in, cot))):
-        for piece in range(PIECES):
-            part = pl.ds(27 // PIECES * piece, 27 // PIECES)
-            copies.append(pltpu.make_async_copy(
-                source.at[part], target.at[part], sems.at[2 + PIECES * array + piece]))
+    pairs = ((f_in, f), (rates_in, rates), (wall_in, wall), (cot_in, cot))
+    copies = [pltpu.make_async_copy(source, target, sems.at[i]) for i, (source, target) in enumerate(pairs)]
     for copy in copies:
         copy.start()
-    for copy in copies[:2 + PIECES]:
+    for copy in copies[:3]:
         copy.wait()
     for i in range(27):
         scale_out[i] = jnp.full((8, 128), rates[i] * (0.5 ** NNZ[i]), F32)
@@ -206,10 +239,10 @@
                 i = 2 * (3 * (a + 1) + b + 1)
                 sums[i, x] = out[qi(a, b, 0)] + (low + high)
                 sums[i + 1, x] = high - low
-    for copy in copies[2 + PIECES:]:
+    for copy in copies[3:]:
         copy.wait()
     raw_rows(rows, -1, cot, raw_right, 0)
-    raw_right[RAW_ROWS:] = jnp.zeros((padded(RAW_ROWS) - RAW_ROWS, 128), F32)
+    clear_end(raw_right, raw_height(-1))
     pieces = [jnp.zeros((8, 128), F32) for _ in range(3)]
     for key, (g, i, kind) in table.items():
         if key[0] == "v":
@@ -234,12 +267,23 @@
     return keys + [(q, far) for q, c in enumerate(Q) if c[0] == side]
 
 
+REDUCED = (1,)
+
+
+def raw_count(side):
+    return FULL if side in REDUCED else 27
+
+
 def raw_at(k, gap):
     return 8 * k if k < FULL else 8 * FULL + gap + 6 * (k - FULL)
 
 
-RAW_ROWS = 8 * FULL + 6 * 18
-SMALL_ROWS = 8 + 6 * 8
+def raw_height(side):
+    return raw_at(raw_count(side), 0)
+
+
+def small_height(side):
+    return 8 + 6 * (23 if side in REDUCED else 8)
 
 
 def padded(count):
@@ -247,7 +291,7 @@
 
 
 def raw_rows(rows, side, cot, message, gap):
-    for k, (q, x) in enumerate(edge_rows(rows, side)):
+    for k, (q, x) in enumerate(edge_rows(rows, side)[:raw_count(side)]):
         at = raw_at(k, gap)
         if k < FULL:
             message[at:at + 8] = cot[q, pl.ds(x, 8, stride=rows), :]
@@ -255,12 +299,35 @@
             message[at:at + 6] = cot[q, pl.ds(x + rows * (1 + Q[q][2]), 6, stride=rows), :]
 
 
+def clear_end(message, count):
+    if message.shape[0] > count:
+        message[count:] = jnp.zeros((message.shape[0] - count, 128), F32)
+
+
 def planes(ref, at):
     start = min(at - 1, ref.shape[0] - 8)
     return turn(ref[start:start + 8], 1 - (at - start), 0)
 
 
-def second_kernel(rows, cot, sums, solid_in, from_left, from_right, to_left, to_right, own, merged):
+def sent_sums(rows):
+    return [(-1, 0), (-1, 1), (0, 0), (0, rows - 1), (1, rows - 1), (1, rows - 2)]
+
+
+def sums_over_y(a, x, sums, halo, table, lane):
+    parts = {}
+    for b in SIGNS:
+        for s in range(2):
+            i = 2 * (3 * (a + 1) + b + 1) + s
+            g, at, kind = table["s", a, b, s, x]
+            parts[b, s] = shift_y(sums[i, x], incoming(halo[g], at, kind, -b), -b, lane)
+    return [(
+        parts[0, 0][n] + (parts[-1, 0][n] + parts[1, 0][n]),
+        parts[1, 0][n] - parts[-1, 0][n],
+        parts[0, 1][n] + (parts[-1, 1][n] + parts[1, 1][n]),
+    ) for n in range(2)]
+
+
+def second_kernel(rows, scale_in, cot, sums, solid_in, from_left, from_right, to_left, to_right, sent, merged):
     lane = lanes()
     table, used = slots(rows)
     halo = []
@@ -274,63 +341,43 @@
         halo.append(jnp.where(takes_left, from_left[g], from_right[g]))
         merged[g] = halo[g]
 
-    def outer(key, b=0):
-        g, i, kind = table[key]
-        return incoming(halo[g], i, kind, b)
-
-    def both(a, x):
-        parts = {}
-        for b in SIGNS:
-            for s in range(2):
-                i = 2 * (3 * (a + 1) + b + 1) + s
-                parts[b, s] = shift_y(sums[i, x], outer(("s", a, b, s, x), -b), -b, lane)
-        result = []
+    t = {}
+    for i, (a, x) in enumerate(sent_sums(rows)):
+        t[a, x] = sums_over_y(a, x, sums, halo, table, lane)
         for n in range(2):
-            result.append((
-                parts[0, 0][n] + (parts[-1, 0][n] + parts[1, 0][n]),
-                parts[1, 0][n] - parts[-1, 0][n],
-                parts[0, 1][n] + (parts[-1, 1][n] + parts[1, 1][n]),
-            ))
-        return result
-
-    t = {(a, x): both(a, x) for a in SIGNS for x in range(rows)}
-
-    def total(x, n):
-        terms = [(a, t[a, x - a][n]) for a in SIGNS if 0 <= x - a < rows]
-        density = functools.reduce(jnp.add, [v[0] for _, v in terms])
-        along_y = functools.reduce(jnp.add, [v[1] for _, v in terms])
-        along_z = functools.reduce(jnp.add, [v[2] for _, v in terms])
-        moving = [(a, v[0]) for a, v in terms if a]
-        along_x = jnp.zeros((8, 128), F32)
-        for a, v in moving:
-            along_x = along_x + v if a == 1 else along_x - v
-        return density, along_x, along_y, along_z
-
-    for x in range(-1, rows + 1):
-        for n in range(2):
-            for k, v in enumerate(total(x, n)):
-                own[k, 2 * (x + 1) + n] = v
-
+            for k in range(3):
+                sent[i, 2 * k + n] = t[a, x][n][k]
+    turned = {(g, c): turn(halo[g], -c, 0) for g in range(2) for c in SIGNS}
     for side, message in ((1, to_left), (-1, to_right)):
         near, far = (0, 1) if side == 1 else (rows - 1, rows - 2)
-        both_parts = message.shape[0] > SMALL_ROWS
-        at = 8 * FULL if both_parts else 0
-        items = RAW_ROWS + 8 if both_parts else 8
-        if both_parts:
+        with_raw = side == 1
+        at = 8 * FULL if with_raw else 0
+        items = raw_height(side) + 8 if with_raw else 8
+        if with_raw:
             raw_rows(rows, side, cot, message, 8)
-            end = RAW_ROWS + SMALL_ROWS
-            message[end:] = jnp.zeros((padded(end) - end, 128), F32)
+        clear_end(message, (raw_height(side) if with_raw else 0) + small_height(side))
         extra = []
         for n in range(2):
             row = list(t[-side, near][n])
             still, moved = t[0, near][n], t[-side, far][n]
             row += [still[0] + moved[0], moved[0] if side == -1 else -moved[0]]
             row += [still[1] + moved[1], still[2] + moved[2]]
-            row.append(solid_in[near] if n == 0 else outer(("w", near)))
+            row.append(solid_in[near] if n == 0 else incoming(halo[table["w", near][0]], table["w", near][1], 0))
             extra.append(row)
         columns = halo[0]
+        if side in REDUCED:
+            groups = {0: [], side: []}
+            for q, x in edge_rows(rows, side)[FULL:]:
+                a, b, c = Q[q]
+                main, beyond = gathered(rows, x - a, q, cot, turned, lane)
+                groups[a].append(main)
+                i = table["v", q, x][1]
+                columns = jnp.where((lane == i) | (lane == i + 1), turn(beyond, i + 1, 1), columns)
+            part, coefficients = side_pull_back(groups, side, [scale_in[i] for i in range(27)])
+            extra[0] += list(part) + list(coefficients)
+        for k, value in enumerate(extra[0]):
+            message[items + 6 * k:items + 6 * k + 6] = value[1:7]
         for k in range(8):
-            message[items + 6 * k:items + 6 * k + 6] = extra[0][k][1:7]
             i = used + 2 * k
             columns = jnp.where((lane == i) | (lane == i + 1), turn(extra[1][k], i + 1, 1), columns)
         message[at:at + 8] = columns
@@ -354,10 +401,26 @@
     return shift_y(main, outer, b, lane)
 
 
-def middle_kernel(rows, scale_in, cot, solid_in, own, merged, inner, known):
+def middle_kernel(rows, scale_in, cot, sums, solid_in, sent, merged, inner, known, own):
     scale = [scale_in[i] for i in range(27)]
     lane = lanes()
     table, _ = slots(rows)
+    halo = [merged[g] for g in range(3)]
+    t = {key: [[sent[i, 2 * k + n] for k in range(3)] for n in range(2)] for i, key in enumerate(sent_sums(rows))}
+    for a in SIGNS:
+        for x in range(rows):
+            if (a, x) not in t:
+                t[a, x] = sums_over_y(a, x, sums, halo, table, lane)
+    for x in range(-1, rows + 1):
+        for n in range(2):
+            terms = [(a, t[a, x - a][n]) for a in SIGNS if 0 <= x - a < rows]
+            along_x = jnp.zeros((8, 128), F32)
+            for a, v in terms:
+                if a:
+                    along_x = along_x + v[0] if a == 1 else along_x - v[0]
+            moments_here = [functools.reduce(jnp.add, [v[k] for _, v in terms]) for k in range(3)]
+            for k, v in enumerate([moments_here[0], along_x] + moments_here[1:]):
+                own[k, 2 * (x + 1) + n] = v
     turned = {(g, c): turn(merged[g], -c, 0) for g in range(2) for c in SIGNS}
     for x in range(1, rows - 1):
         v = [gathered(rows, x, q, cot, turned, lane) for q in range(27)]
@@ -386,7 +449,7 @@
         at = raw_at(k, gap)
         return turn(raw[at:at + 8], -c, 0) if k < FULL else planes(raw, at)
 
-    for k, (q, x) in enumerate(edge_rows(rows, side)):
+    for k, (q, x) in enumerate(edge_rows(rows, side)[:raw_count(side)]):
         _, i, kind = table["v", q, x]
         remote[q, x + side * rows] = (functools.partial(load, k, Q[q][2]), "far", i, kind)
     columns = extra[columns_at:columns_at + 8]
@@ -398,11 +461,13 @@
         if x not in (near, near + side):
             continue
         v = []
-        for q in range(27):
-            if 0 <= x + Q[q][0] < rows:
+        for q, (a, b, c) in enumerate(Q):
+            if 0 <= x + a < rows:
                 v.append((known[q, 2 * j], known[q, 2 * j + 1]))
+            elif x == near or side not in REDUCED:
+                v.append(gathered(rows, x, q, None, turned, lane, remote))
             else:
-                v.append(gathered(rows, x, q, None, turned, lane, remote))
+                v.append((None, incoming(columns, table["v", q, x + a - side * rows][1], 0)))
         for n in range(2):
             def got(k):
                 return planes(extra, items_at + 6 * k) if n == 0 else incoming(columns, used + 2 * k, 0)
@@ -420,7 +485,21 @@
                 total = [total[k] + got(3 + k) for k in range(4)]
                 wall = got(7)
             inverse = 1.0 / total[0]
-            g = pull_back([t[n] for t in v], [t * inverse for t in total[1:]], boundary | (wall > 0.5), scale)
+            u = [t * inverse for t in total[1:]]
+            solid = boundary | (wall > 0.5)
+            if x != near and n == 0 and side in REDUCED:
+                mine = [t[0] for t in v[9 * (1 - side):9 * (1 - side) + 9]]
+                part, coefficients = side_pull_back({-side: mine}, side, scale)
+                p_x, p_y, p_z, quad = form([m + got(17 + k) for k, m in enumerate(coefficients)], u)
+                start = (p_x if side == 1 else -p_x) - quad
+                along_y = {-1: start - p_y, 0: start, 1: start + p_y}
+                for i in range(9):
+                    b, c = i // 3 - 1, i % 3 - 1
+                    rest = along_y[b] + p_z if c == 1 else along_y[b] - p_z if c == -1 else along_y[b]
+                    value = (part[i] + got(8 + i)) + rest
+                    g1[9 * (1 + side) + i, 2 * (j % 2)] = jnp.where(solid, mine[8 - i], value)
+                continue
+            g = pull_back([t[n] for t in v], u, solid, scale)
             for q in range(27):
                 if 0 <= x - Q[q][0] < rows:
                     g1[q, 2 * (j % 2) + n] = g[q]
@@ -434,7 +513,7 @@
         if b:
             main = shift_y(main, turn(array[q, r + 1], -b, 1), b, lane)[0]
         v.append(turn(main, -c, 0))
-    return pull_back(v, [speed[k, x] for k in range(3)], solid_in[x] > 0.5, scale)
+    return pull_back_parts(v, [speed[k, x] for k in range(3)], solid_in[x] > 0.5, scale)
 
 
 def low_kernel(rows, scale_in, speed, solid_in, own, merged, inner, known, raw, extra, done, g1):
@@ -446,32 +525,29 @@
         return (g1, 2 * (x + 1)) if x < 1 else (inner, 2 * (x - 1))
 
     for x in range(rows - 2):
-        result = pulled_row(rows, x, arrays, speed, solid_in, scale, lane)
-        for q in range(27):
-            done[q, x] = result[q]
+        for a, part in enumerate(pulled_row(rows, x, arrays, speed, solid_in, scale, lane)):
+            for i, value in enumerate(part):
+                done[9 * a + i, x] = value
 
 
 def last_kernel(rows, scale_in, speed, solid_in, own, merged, inner, known, done, from_high, out_hbm, high, out, sems):
     scale = [scale_in[i] for i in range(27)]
     lane = lanes()
-    outer_gradient(rows, 1, scale, solid_in, own, merged, known, from_high, 8, from_high, 8 * FULL, RAW_ROWS + 8, high)
+    outer_gradient(rows, 1, scale, solid_in, own, merged, known, from_high, 8, from_high, 8 * FULL, raw_height(1) + 8, high)
 
     def arrays(x):
         return (inner, 2 * (x - 1)) if x < rows - 1 else (high, 2 * (x - rows + 1))
 
-    for x in range(rows):
-        if x < rows - 2:
-            result = [done[q, x] for q in range(27)]
-        else:
-            result = pulled_row(rows, x, arrays, speed, solid_in, scale, lane)
-        for q in range(27):
-            out[q, pl.ds(x, 8, stride=rows), :] = result[q]
+    late = {x: pulled_row(rows, x, arrays, speed, solid_in, scale, lane) for x in range(rows - 2, rows)}
     copies = []
-    for piece in range(PIECES):
-        part = pl.ds(27 // PIECES * piece, 27 // PIECES)
-        copies.append(pltpu.make_async_copy(out.at[part], out_hbm.at[part], sems.at[piece]))
-    for copy in copies:
-        copy.start()
+    for a in range(3):
+        for x in range(rows):
+            part = next(late[x]) if x in late else [done[9 * a + i, x] for i in range(9)]
+            for i, value in enumerate(part):
+                out[9 * a + i, pl.ds(x, 8, stride=rows), :] = value
+        part = pl.ds(9 * a, 9)
+        copies.append(pltpu.make_async_copy(out.at[part], out_hbm.at[part], sems.at[a]))
+        copies[a].start()
     for copy in copies:
         copy.wait()
 
@@ -512,25 +588,25 @@
     cot, scale, sums, speed, solid, packed, raw_right = call(
         functools.partial(first_kernel, rows), "collide",
         [lattice, (27,) + tile, (18, rows) + tile, (3, rows) + tile, (rows,) + tile, (3,) + tile,
-         (padded(RAW_ROWS), width)],
+         (padded(raw_height(-1)), width)],
         [pltpu.SMEM((27,), F32), pltpu.VMEM(lattice, F32), pltpu.VMEM(lattice[1:], jnp.int32),
-         pltpu.SemaphoreType.DMA((2 + 2 * PIECES,))],
+         pltpu.SemaphoreType.DMA((4,))],
         tuple(pltpu.with_memory_space_constraint(v, pltpu.HBM) for v in (rates, f, wall, cot)), pltpu.HBM)
     raw_low = ring(raw_right, "gx", 1)
     across, inside = swap(packed, "gy", 1), swap(packed, "gy", 0)
     odd = lax.axis_index("gy") % 2 == 1
     from_left = jnp.where(odd, inside, across)
     from_right = jnp.where(odd, across, inside)
-    to_left, small_right, own, merged = call(
+    to_left, small_right, sent, merged = call(
         functools.partial(second_kernel, rows), "pack",
-        [(padded(RAW_ROWS + SMALL_ROWS), width), (SMALL_ROWS, width), (4, 2 * rows + 4) + tile, (3,) + tile], [],
-        (cot, sums, solid, from_left, from_right))
+        [(padded(raw_height(1) + small_height(1)), width), (padded(small_height(-1)), width), (6, 6) + tile, (3,) + tile], [],
+        (scale, cot, sums, solid, from_left, from_right))
     small_low = ring(small_right, "gx", 1)
     from_high = ring(to_left, "gx", -1)
-    inner, known = call(
+    inner, known, own = call(
         functools.partial(middle_kernel, rows), "inner_rows",
-        [(27, 2 * rows - 4) + tile, (27, 8) + tile], [],
-        (scale, cot, solid, own, merged))
+        [(27, 2 * rows - 4) + tile, (27, 8) + tile, (4, 2 * rows + 4) + tile], [],
+        (scale, cot, sums, solid, sent, merged))
     (done,) = call(
         functools.partial(low_kernel, rows), "low_rows",
         [(27, rows - 2) + tile], [pltpu.VMEM((27, 4) + tile, F32)],
@@ -538,7 +614,7 @@
     (out,) = call(
         functools.partial(last_kernel, rows), "gradient",
         [lattice],
-        [pltpu.VMEM((27, 4) + tile, F32), pltpu.VMEM(lattice, F32), pltpu.SemaphoreType.DMA((PIECES,))],
+        [pltpu.VMEM((27, 4) + tile, F32), pltpu.VMEM(lattice, F32), pltpu.SemaphoreType.DMA((3,))],
         (scale, speed, solid, own, merged, inner, known, done, from_high), out_space=pltpu.HBM)
     return out.reshape(checkpoint.shape)
 

time: 16.7 us -> 16.5 us (0.988)
  waiting for transfers between devices: 3.29 us -> 3.06 us
    ppermute x3, waiting for transfers between devices: 3.28 us -> 3.05 us  [ring(): lax.ppermute(block, axis, [(i, (i + step) % size) for i in range(size)])]
  transfers between devices with their start and end apart: 5 -> 5, of which waited for: 2 -> 2; matrix products, arithmetic and copies ran while one was open for 0% -> 0% of each run, Pallas kernels for 6% -> 7%
where the time goes in v7:
time: 16.5 us; the launch traced here: 16.3 us
  starting transfers between devices  9.41 us (57%)
  Pallas kernels  3.82 us (23%)
  waiting for transfers between devices  3.06 us (19%)
    ppermute x3, starting transfers between devices, ring(): lax.ppermute(block, axis, [(i, (i + step) % size) for i in range(size)])  6.27 us
    pallas_call x5, Pallas kernels, call(): pl.pallas_call(kernel, out_shape=[jax.ShapeDtypeStruct(s, F32) for s in o...  3.82 us
    ppermute x2, starting transfers between devices, swap(): return lax.ppermute(block, axis, route)  3.15 us
    ppermute x3, waiting for transfers between devices, ring(): lax.ppermute(block, axis, [(i, (i + step) % size) for i in range(size)])  3.05 us
  transfers between devices with their start and end apart: 5, of which 2 were waited for; matrix products, arithmetic and copies ran while one was open for 0% of the time, Pallas kernels for 7%

profile of v7, /device:TPU:0, one launch (start us, length us, event | category | flops | bytes accessed | tf_op | source)
XLA Modules:
  0.0 16.3 jit_solution(16482611887184392081)
XLA Ops:
  0.0 1.6 %collide.1 = (f32[27,32,128]{2,1,0:T(8,128)S(1)}, f32[27,8,128]{2,1,0:T(8,128)S(1)}, f32[18,4,8,128]{3,2,1,0:T(8,128)S(1)}, f32[3,4,8,128]{3,2,1,0:T(8,128)S(1)}...) custom-call(f32[27]{0:T(128)} %rates_in.1, f32[27,32,128]{2,1,0:T(8,128)} %bitcast.4, ...), custom_call_target="tpu_custom_call" | custom-call | tf_op jit(solution)/shard_map/collide/pallas_call | solution.py:556
  1.6 2.5 %collective-permute-start.1 = (f32[3,8,128]{2,1,0:T(8,128)S(1)}, f32[3,8,128]{2,1,0:T(8,128)S(1)}, u32[]{:S(2)}, u32[]{:S(2)}) collective-permute-start(f32[3,8,128]{2,1,0:T(8,128)S(1)} %get-tuple-element.24), channel_id=1, source_target_pairs={{1,2},{2,1},{3,0},{0,3},{5,6},{6,5},{7,4},{4,7},{9,10},{10,9},{11,... | collective-permute-start | bytes 36872 | tf_op jit(solution)/shard_map/ppermute | solution.py:578
  4.0 0.7 %collective-permute-start = (f32[3,8,128]{2,1,0:T(8,128)S(1)}, f32[3,8,128]{2,1,0:T(8,128)S(1)}, u32[]{:S(2)}, u32[]{:S(2)}) collective-permute-start(f32[3,8,128]{2,1,0:T(8,128)S(1)} %get-tuple-element.24), channel_id=1, source_target_pairs={{0,1},{1,0},{2,3},{3,2},{4,5},{5,4},{6,7},{7,6},{8,9},{9,8},{10,11... | collective-permute-start | bytes 36872 | tf_op jit(solution)/shard_map/ppermute | solution.py:578
  4.7 1.5 %collective-permute-start.2 = (f32[184,128]{1,0:T(8,128)S(1)}, f32[184,128]{1,0:T(8,128)S(1)}, u32[]{:S(2)}, u32[]{:S(2)}) collective-permute-start(f32[184,128]{1,0:T(8,128)S(1)} %get-tuple-element.30), channel_id=1, source_target_pairs={{0,4},{4,8},{8,12},{12,16},{16,20},{20,24},{24,28},{28,0},{1,5},{5... | collective-permute-start | bytes 282632 | tf_op jit(solution)/shard_map/ppermute | solution.py:570
  6.2 0.0 collective-permute-done.1
  6.2 0.0 collective-permute-done
  6.2 0.3 %pack.1 = (f32[224,128]{1,0:T(8,128)S(1)}, f32[56,128]{1,0:T(8,128)S(1)}, f32[6,6,8,128]{3,2,1,0:T(8,128)S(1)}, f32[3,8,128]{2,1,0:T(8,128)S(1)}) custom-call(f32[27,8,128]{2,1,0:T(8,128)S(1)} %get-tuple-element.19.scale_in, f32[27,32,128]{2,1,0:T(8,128)S(1)} %get-tuple-element.22.cot, f32[18,4,8,128]{3,2,1,0:T(8,128)S(1)} %get-tuple-element.23.sums, ...), custom_call_target="tpu_custom_call" | custom-call | tf_op jit(solution)/shard_map/pack/pallas_call | solution.py:556
  6.5 1.6 %collective-permute-start.3 = (f32[56,128]{1,0:T(8,128)S(1)}, f32[56,128]{1,0:T(8,128)S(1)}, u32[]{:S(2)}, u32[]{:S(2)}) collective-permute-start(f32[56,128]{1,0:T(8,128)S(1)} %get-tuple-element.31), channel_id=1, source_target_pairs={{0,4},{4,8},{8,12},{12,16},{16,20},{20,24},{24,28},{28,0},{1,5},{5... | collective-permute-start | bytes 86024 | tf_op jit(solution)/shard_map/ppermute | solution.py:570
  8.1 3.2 %collective-permute-start.4 = (f32[224,128]{1,0:T(8,128)S(1)}, f32[224,128]{1,0:T(8,128)S(1)}, u32[]{:S(2)}, u32[]{:S(2)}) collective-permute-start(f32[224,128]{1,0:T(8,128)S(1)} %get-tuple-element.32), channel_id=1, source_target_pairs={{0,28},{4,0},{8,4},{12,8},{16,12},{20,16},{24,20},{28,24},{1,29},{... | collective-permute-start | bytes 344072 | tf_op jit(solution)/shard_map/ppermute | solution.py:570
  11.3 0.5 %inner_rows.1 = (f32[27,4,8,128]{3,2,1,0:T(8,128)S(1)}, f32[27,8,8,128]{3,2,1,0:T(8,128)S(1)}, f32[4,12,8,128]{3,2,1,0:T(8,128)S(1)}) custom-call(f32[27,8,128]{2,1,0:T(8,128)S(1)} %get-tuple-element.19.scale_in, f32[27,32,128]{2,1,0:T(8,128)S(1)} %get-tuple-element.22.cot, f32[18,4,8,128]{3,2,1,0:T(8,128)S(1)} %get-tuple-element.23.sums, ...), custom_call_target="tpu_custom_call" | custom-call | tf_op jit(solution)/shard_map/inner_rows/pallas_call | solution.py:556
  11.7 1.4 %collective-permute-done.3.extra = f32[56,128]{1,0:T(8,128)S(1)} collective-permute-done((f32[56,128]{1,0:T(8,128)S(1)}, f32[56,128]{1,0:T(8,128)S(1)}, u32[]{:S(2)}, u32[]{:S(2)}) %collective-permute-start.3) | collective-permute-done | bytes 28704 | tf_op jit(solution)/shard_map/ppermute | solution.py:570
  13.2 0.0 collective-permute-done.2.raw
  13.2 0.4 %low_rows.1.done = f32[27,2,8,128]{3,2,1,0:T(8,128)S(1)} custom-call(f32[27,8,128]{2,1,0:T(8,128)S(1)} %get-tuple-element.19.scale_in, f32[3,4,8,128]{3,2,1,0:T(8,128)S(1)} %get-tuple-element.20.speed, f32[4,8,128]{2,1,0:T(8,128)S(1)} %get-tuple-element.21.solid_in, f32[4,12,8,128]{3,2,1,0:T(8,128)S(1)} %get-tuple-element.27.own, ...), custom_call_target="tpu_custom_call" | custom-call | flops 2000000000 | tf_op jit(solution)/shard_map/low_rows/pallas_call | solution.py:556
  13.6 1.6 %collective-permute-done.4.from_high = f32[224,128]{1,0:T(8,128)S(1)} collective-permute-done((f32[224,128]{1,0:T(8,128)S(1)}, f32[224,128]{1,0:T(8,128)S(1)}, u32[]{:S(2)}, u32[]{:S(2)}) %collective-permute-start.4) | collective-permute-done | bytes 114720 | tf_op jit(solution)/shard_map/ppermute | solution.py:570
  15.2 1.1 %gradient.1 = f32[27,32,128]{2,1,0:T(8,128)} custom-call(f32[27,8,128]{2,1,0:T(8,128)S(1)} %get-tuple-element.19.scale_in, f32[3,4,8,128]{3,2,1,0:T(8,128)S(1)} %get-tuple-element.20.speed, f32[4,8,128]{2,1,0:T(8,128)S(1)} %get-tuple-element.21.solid_in, f32[4,12,8,128]{3,2,1,0:T(8,128)S(1)} %get-tuple-element.27.own, ...), custom_call_target="tpu_custom_call" | custom-call | tf_op jit(solution)/shard_map/gradient/pallas_call | solution.py:556
  (1 shorter events, 0.0 us)
Async XLA Ops:
  1.6 4.6 %collective-permute-start.1 = (f32[3,8,128]{2,1,0:T(8,128)S(1)}, f32[3,8,128]{2,1,0:T(8,128)S(1)}, u32[]{:S(2)}, u32[]{:S(2)}) collective-permute-start(f32[3,8,128]{2,1,0:T(8,128)S(1)} %get-tuple-element.24), channel_id=1, source_target_pairs={{1,2},{2,1},{3,0},{0,3},{5,6},{6,5},{7,4},{4,7},{9,10},{10,9},{11,... | collective-permute-start | bytes 36872 | tf_op jit(solution)/shard_map/ppermute | solution.py:578
  4.0 2.2 %collective-permute-start = (f32[3,8,128]{2,1,0:T(8,128)S(1)}, f32[3,8,128]{2,1,0:T(8,128)S(1)}, u32[]{:S(2)}, u32[]{:S(2)}) collective-permute-start(f32[3,8,128]{2,1,0:T(8,128)S(1)} %get-tuple-element.24), channel_id=1, source_target_pairs={{0,1},{1,0},{2,3},{3,2},{4,5},{5,4},{6,7},{7,6},{8,9},{9,8},{10,11... | collective-permute-start | bytes 36872 | tf_op jit(solution)/shard_map/ppermute | solution.py:578
  4.7 8.4 %collective-permute-start.2 = (f32[184,128]{1,0:T(8,128)S(1)}, f32[184,128]{1,0:T(8,128)S(1)}, u32[]{:S(2)}, u32[]{:S(2)}) collective-permute-start(f32[184,128]{1,0:T(8,128)S(1)} %get-tuple-element.30), channel_id=1, source_target_pairs={{0,4},{4,8},{8,12},{12,16},{16,20},{20,24},{24,28},{28,0},{1,5},{5... | collective-permute-start | bytes 282632 | tf_op jit(solution)/shard_map/ppermute | solution.py:570
  6.5 6.7 %collective-permute-start.3 = (f32[56,128]{1,0:T(8,128)S(1)}, f32[56,128]{1,0:T(8,128)S(1)}, u32[]{:S(2)}, u32[]{:S(2)}) collective-permute-start(f32[56,128]{1,0:T(8,128)S(1)} %get-tuple-element.31), channel_id=1, source_target_pairs={{0,4},{4,8},{8,12},{12,16},{16,20},{20,24},{24,28},{28,0},{1,5},{5... | collective-permute-start | bytes 86024 | tf_op jit(solution)/shard_map/ppermute | solution.py:570
  8.1 7.1 %collective-permute-start.4 = (f32[224,128]{1,0:T(8,128)S(1)}, f32[224,128]{1,0:T(8,128)S(1)}, u32[]{:S(2)}, u32[]{:S(2)}) collective-permute-start(f32[224,128]{1,0:T(8,128)S(1)} %get-tuple-element.32), channel_id=1, source_target_pairs={{0,28},{4,0},{8,4},{12,8},{16,12},{20,16},{24,20},{28,24},{1,29},{... | collective-permute-start | bytes 344072 | tf_op jit(solution)/shard_map/ppermute | solution.py:570

commit v8 on v7

--- a/solution.py
+++ b/solution.py
@@ -22,26 +22,38 @@
 NNZ = [(i > 0) + (j > 0) + (k > 0) for i in range(3) for j in range(3) for k in range(3)]
 
 
+def layout(rows):
+    quads, singles = [[], [], []], [[], [], []]
+    for a in SIGNS:
+        for c in SIGNS:
+            for x in range(rows):
+                left = (a >= 0 and x == 0) or (a == 1 and x == 1)
+                right = (a <= 0 and x == rows - 1) or (a == -1 and x == rows - 2)
+                g = 0 if left or right else 1
+                quads[g].append((("v", qi(a, -1, c), x), ("v", qi(a, 1, c), x)))
+                singles[g].append(("v", qi(a, 0, c), x))
+    used = 4 * len(quads[0]) + 2 * len(singles[0])
+    singles[1] += [("w", x) for x in range(rows)]
+    for a in SIGNS:
+        for s in range(2):
+            for x in range(rows):
+                quads[2].append((("s", a, 1, s, x), ("s", a, -1, s, x)))
+                singles[2].append(("s", a, 0, s, x))
+    room = 64 - 2 * len(quads[2])
+    singles[0] += singles[2][room:]
+    singles[2] = singles[2][:room]
+    return quads, singles, used
+
+
 def slots(rows):
-    first, second, sums = [], [], []
-    for q, (a, b, c) in enumerate(Q):
-        for x in range(rows):
-            left = (a >= 0 and x == 0) or (a == 1 and x == 1)
-            right = (a <= 0 and x == rows - 1) or (a == -1 and x == rows - 2)
-            (first if left or right else second).append((("v", q, x), b))
-    for x in range(rows):
-        second.append((("w", x), 0))
-    for a in SIGNS:
-        for b in SIGNS:
-            for s in range(2):
-                for x in range(rows):
-                    sums.append((("s", a, b, s, x), -b))
+    quads, singles, used = layout(rows)
     table = {}
-    groups = [first + sums[64:], second, sums[:64]]
-    for g, group in enumerate(groups):
-        for i, (key, kind) in enumerate(group):
-            table[key] = (g, 2 * i, kind)
-    return table, 2 * len(first)
+    for g in range(3):
+        for n, (low, high) in enumerate(quads[g]):
+            table[low], table[high] = (g, 4 * n, -1), (g, 4 * n + 2, 1)
+        for n, key in enumerate(singles[g]):
+            table[key] = (g, 4 * len(quads[g]) + 2 * n, 0)
+    return table, used
 
 
 def turn(v, shift, axis):
@@ -51,10 +63,6 @@
 
 def lanes():
     return lax.broadcasted_iota(jnp.int32, (8, 128), 1)
-
-
-def outgoing(block, lane, kind):
-    return turn(block, {0: lane + 1, 1: lane, -1: lane + 2}[kind], 1)
 
 
 def incoming(packed, lane, kind, b=0):
@@ -243,18 +251,25 @@
         copy.wait()
     raw_rows(rows, -1, cot, raw_right, 0)
     clear_end(raw_right, raw_height(-1))
-    pieces = [jnp.zeros((8, 128), F32) for _ in range(3)]
-    for key, (g, i, kind) in table.items():
+    def block(key):
         if key[0] == "v":
-            block = cot[key[1], pl.ds(key[2], 8, stride=rows), :]
-        elif key[0] == "w":
-            block = solid_out[key[1]]
-        else:
-            block = sums[2 * (3 * (key[1] + 1) + key[2] + 1) + key[3], key[4]]
-        mine = (lane == i) | (lane == i + 1)
-        pieces[g] = jnp.where(mine, outgoing(block, i, kind), pieces[g])
+            return cot[key[1], pl.ds(key[2], 8, stride=rows), :]
+        if key[0] == "w":
+            return solid_out[key[1]]
+        return sums[2 * (3 * (key[1] + 1) + key[2] + 1) + key[3], key[4]]
+
+    quads, singles, _ = layout(rows)
+    by_two, by_four = lane >> 1, lane >> 2
+    high_lanes = lane >= 64
     for g in range(3):
-        packed[g] = pieces[g]
+        piece = jnp.zeros((8, 128), F32)
+        for n, (low, high) in enumerate(quads[g]):
+            both = jnp.where(high_lanes, block(low), block(high))
+            piece = jnp.where(by_four == n, turn(both, 4 * n + 2, 1), piece)
+        for n, key in enumerate(singles[g]):
+            i = 4 * len(quads[g]) + 2 * n
+            piece = jnp.where(by_two == i // 2, turn(block(key), i + 1, 1), piece)
+        packed[g] = piece
 
 
 FULL = 9
@@ -330,14 +345,11 @@
 def second_kernel(rows, scale_in, cot, sums, solid_in, from_left, from_right, to_left, to_right, sent, merged):
     lane = lanes()
     table, used = slots(rows)
+    by_two = lane >> 1
     halo = []
     for g in range(3):
-        takes_left = jnp.zeros((8, 128), jnp.bool_)
-        for key, (h, i, kind) in table.items():
-            if h == g and kind <= 0:
-                takes_left = takes_left | (lane == i)
-            if h == g and kind == -1:
-                takes_left = takes_left | (lane == i + 1)
+        end = 4 * len(layout(rows)[0][g])
+        takes_left = ((lane < end) & ((lane & 2) == 0)) | ((lane >= end) & ((lane & 1) == 0))
         halo.append(jnp.where(takes_left, from_left[g], from_right[g]))
         merged[g] = halo[g]
 
@@ -372,14 +384,14 @@
                 main, beyond = gathered(rows, x - a, q, cot, turned, lane)
                 groups[a].append(main)
                 i = table["v", q, x][1]
-                columns = jnp.where((lane == i) | (lane == i + 1), turn(beyond, i + 1, 1), columns)
+                columns = jnp.where(by_two == i // 2, turn(beyond, i + 1, 1), columns)
             part, coefficients = side_pull_back(groups, side, [scale_in[i] for i in range(27)])
             extra[0] += list(part) + list(coefficients)
         for k, value in enumerate(extra[0]):
             message[items + 6 * k:items + 6 * k + 6] = value[1:7]
         for k in range(8):
             i = used + 2 * k
-            columns = jnp.where((lane == i) | (lane == i + 1), turn(extra[1][k], i + 1, 1), columns)
+            columns = jnp.where(by_two == i // 2, turn(extra[1][k], i + 1, 1), columns)
         message[at:at + 8] = columns
 
 

time: 16.5 us -> 16.4 us (level)
  no operation moved by 1% of the time
where the time goes in v8:
time: 16.4 us; the launch traced here: 16.3 us
  starting transfers between devices  9.41 us (57%)
  Pallas kernels  3.73 us (23%)
  waiting for transfers between devices  3.08 us (19%)
    ppermute x3, starting transfers between devices, ring(): lax.ppermute(block, axis, [(i, (i + step) % size) for i in range(size)])  6.27 us
    pallas_call x5, Pallas kernels, call(): pl.pallas_call(kernel, out_shape=[jax.ShapeDtypeStruct(s, F32) for s in o...  3.73 us
    ppermute x2, starting transfers between devices, swap(): return lax.ppermute(block, axis, route)  3.15 us
    ppermute x3, waiting for transfers between devices, ring(): lax.ppermute(block, axis, [(i, (i + step) % size) for i in range(size)])  3.08 us
  transfers between devices with their start and end apart: 5, of which 2 were waited for; matrix products, arithmetic and copies ran while one was open for 0% of the time, Pallas kernels for 7%

profile of v8, /device:TPU:0, one launch (start us, length us, event | category | flops | bytes accessed | tf_op | source)
XLA Modules:
  0.0 16.3 jit_solution(17245889874979538843)
XLA Ops:
  0.0 1.5 %collide.1 = (f32[27,32,128]{2,1,0:T(8,128)S(1)}, f32[27,8,128]{2,1,0:T(8,128)S(1)}, f32[18,4,8,128]{3,2,1,0:T(8,128)S(1)}, f32[3,4,8,128]{3,2,1,0:T(8,128)S(1)}...) custom-call(f32[27]{0:T(128)} %rates_in.1, f32[27,32,128]{2,1,0:T(8,128)} %bitcast.4, ...), custom_call_target="tpu_custom_call" | custom-call | tf_op jit(solution)/shard_map/collide/pallas_call | solution.py:568
  1.5 2.5 %collective-permute-start.1 = (f32[3,8,128]{2,1,0:T(8,128)S(1)}, f32[3,8,128]{2,1,0:T(8,128)S(1)}, u32[]{:S(2)}, u32[]{:S(2)}) collective-permute-start(f32[3,8,128]{2,1,0:T(8,128)S(1)} %get-tuple-element.24), channel_id=1, source_target_pairs={{1,2},{2,1},{3,0},{0,3},{5,6},{6,5},{7,4},{4,7},{9,10},{10,9},{11,... | collective-permute-start | bytes 36872 | tf_op jit(solution)/shard_map/ppermute | solution.py:590
  4.0 0.7 %collective-permute-start = (f32[3,8,128]{2,1,0:T(8,128)S(1)}, f32[3,8,128]{2,1,0:T(8,128)S(1)}, u32[]{:S(2)}, u32[]{:S(2)}) collective-permute-start(f32[3,8,128]{2,1,0:T(8,128)S(1)} %get-tuple-element.24), channel_id=1, source_target_pairs={{0,1},{1,0},{2,3},{3,2},{4,5},{5,4},{6,7},{7,6},{8,9},{9,8},{10,11... | collective-permute-start | bytes 36872 | tf_op jit(solution)/shard_map/ppermute | solution.py:590
  4.7 1.5 %collective-permute-start.2 = (f32[184,128]{1,0:T(8,128)S(1)}, f32[184,128]{1,0:T(8,128)S(1)}, u32[]{:S(2)}, u32[]{:S(2)}) collective-permute-start(f32[184,128]{1,0:T(8,128)S(1)} %get-tuple-element.30), channel_id=1, source_target_pairs={{0,4},{4,8},{8,12},{12,16},{16,20},{20,24},{24,28},{28,0},{1,5},{5... | collective-permute-start | bytes 282632 | tf_op jit(solution)/shard_map/ppermute | solution.py:582
  6.1 0.0 collective-permute-done.1
  6.1 0.0 collective-permute-done
  6.2 0.2 %pack.1 = (f32[224,128]{1,0:T(8,128)S(1)}, f32[56,128]{1,0:T(8,128)S(1)}, f32[6,6,8,128]{3,2,1,0:T(8,128)S(1)}, f32[3,8,128]{2,1,0:T(8,128)S(1)}) custom-call(f32[27,8,128]{2,1,0:T(8,128)S(1)} %get-tuple-element.19.scale_in, f32[27,32,128]{2,1,0:T(8,128)S(1)} %get-tuple-element.22.cot, f32[18,4,8,128]{3,2,1,0:T(8,128)S(1)} %get-tuple-element.23.sums, ...), custom_call_target="tpu_custom_call" | custom-call | tf_op jit(solution)/shard_map/pack/pallas_call | solution.py:568
  6.4 1.6 %collective-permute-start.3 = (f32[56,128]{1,0:T(8,128)S(1)}, f32[56,128]{1,0:T(8,128)S(1)}, u32[]{:S(2)}, u32[]{:S(2)}) collective-permute-start(f32[56,128]{1,0:T(8,128)S(1)} %get-tuple-element.31), channel_id=1, source_target_pairs={{0,4},{4,8},{8,12},{12,16},{16,20},{20,24},{24,28},{28,0},{1,5},{5... | collective-permute-start | bytes 86024 | tf_op jit(solution)/shard_map/ppermute | solution.py:582
  8.0 3.2 %collective-permute-start.4 = (f32[224,128]{1,0:T(8,128)S(1)}, f32[224,128]{1,0:T(8,128)S(1)}, u32[]{:S(2)}, u32[]{:S(2)}) collective-permute-start(f32[224,128]{1,0:T(8,128)S(1)} %get-tuple-element.32), channel_id=1, source_target_pairs={{0,28},{4,0},{8,4},{12,8},{16,12},{20,16},{24,20},{28,24},{1,29},{... | collective-permute-start | bytes 344072 | tf_op jit(solution)/shard_map/ppermute | solution.py:582
  11.2 0.5 %inner_rows.1 = (f32[27,4,8,128]{3,2,1,0:T(8,128)S(1)}, f32[27,8,8,128]{3,2,1,0:T(8,128)S(1)}, f32[4,12,8,128]{3,2,1,0:T(8,128)S(1)}) custom-call(f32[27,8,128]{2,1,0:T(8,128)S(1)} %get-tuple-element.19.scale_in, f32[27,32,128]{2,1,0:T(8,128)S(1)} %get-tuple-element.22.cot, f32[18,4,8,128]{3,2,1,0:T(8,128)S(1)} %get-tuple-element.23.sums, ...), custom_call_target="tpu_custom_call" | custom-call | tf_op jit(solution)/shard_map/inner_rows/pallas_call | solution.py:568
  11.6 1.4 %collective-permute-done.3.extra = f32[56,128]{1,0:T(8,128)S(1)} collective-permute-done((f32[56,128]{1,0:T(8,128)S(1)}, f32[56,128]{1,0:T(8,128)S(1)}, u32[]{:S(2)}, u32[]{:S(2)}) %collective-permute-start.3) | collective-permute-done | bytes 28704 | tf_op jit(solution)/shard_map/ppermute | solution.py:582
  13.1 0.0 collective-permute-done.2.raw
  13.1 0.4 %low_rows.1.done = f32[27,2,8,128]{3,2,1,0:T(8,128)S(1)} custom-call(f32[27,8,128]{2,1,0:T(8,128)S(1)} %get-tuple-element.19.scale_in, f32[3,4,8,128]{3,2,1,0:T(8,128)S(1)} %get-tuple-element.20.speed, f32[4,8,128]{2,1,0:T(8,128)S(1)} %get-tuple-element.21.solid_in, f32[4,12,8,128]{3,2,1,0:T(8,128)S(1)} %get-tuple-element.27.own, ...), custom_call_target="tpu_custom_call" | custom-call | flops 2000000000 | tf_op jit(solution)/shard_map/low_rows/pallas_call | solution.py:568
  13.5 1.7 %collective-permute-done.4.from_high = f32[224,128]{1,0:T(8,128)S(1)} collective-permute-done((f32[224,128]{1,0:T(8,128)S(1)}, f32[224,128]{1,0:T(8,128)S(1)}, u32[]{:S(2)}, u32[]{:S(2)}) %collective-permute-start.4) | collective-permute-done | bytes 114720 | tf_op jit(solution)/shard_map/ppermute | solution.py:582
  15.1 1.1 %gradient.1 = f32[27,32,128]{2,1,0:T(8,128)} custom-call(f32[27,8,128]{2,1,0:T(8,128)S(1)} %get-tuple-element.19.scale_in, f32[3,4,8,128]{3,2,1,0:T(8,128)S(1)} %get-tuple-element.20.speed, f32[4,8,128]{2,1,0:T(8,128)S(1)} %get-tuple-element.21.solid_in, f32[4,12,8,128]{3,2,1,0:T(8,128)S(1)} %get-tuple-element.27.own, ...), custom_call_target="tpu_custom_call" | custom-call | tf_op jit(solution)/shard_map/gradient/pallas_call | solution.py:568
  (1 shorter events, 0.0 us)
Async XLA Ops:
  1.5 4.6 %collective-permute-start.1 = (f32[3,8,128]{2,1,0:T(8,128)S(1)}, f32[3,8,128]{2,1,0:T(8,128)S(1)}, u32[]{:S(2)}, u32[]{:S(2)}) collective-permute-start(f32[3,8,128]{2,1,0:T(8,128)S(1)} %get-tuple-element.24), channel_id=1, source_target_pairs={{1,2},{2,1},{3,0},{0,3},{5,6},{6,5},{7,4},{4,7},{9,10},{10,9},{11,... | collective-permute-start | bytes 36872 | tf_op jit(solution)/shard_map/ppermute | solution.py:590
  4.0 2.2 %collective-permute-start = (f32[3,8,128]{2,1,0:T(8,128)S(1)}, f32[3,8,128]{2,1,0:T(8,128)S(1)}, u32[]{:S(2)}, u32[]{:S(2)}) collective-permute-start(f32[3,8,128]{2,1,0:T(8,128)S(1)} %get-tuple-element.24), channel_id=1, source_target_pairs={{0,1},{1,0},{2,3},{3,2},{4,5},{5,4},{6,7},{7,6},{8,9},{9,8},{10,11... | collective-permute-start | bytes 36872 | tf_op jit(solution)/shard_map/ppermute | solution.py:590
  4.7 8.4 %collective-permute-start.2 = (f32[184,128]{1,0:T(8,128)S(1)}, f32[184,128]{1,0:T(8,128)S(1)}, u32[]{:S(2)}, u32[]{:S(2)}) collective-permute-start(f32[184,128]{1,0:T(8,128)S(1)} %get-tuple-element.30), channel_id=1, source_target_pairs={{0,4},{4,8},{8,12},{12,16},{16,20},{20,24},{24,28},{28,0},{1,5},{5... | collective-permute-start | bytes 282632 | tf_op jit(solution)/shard_map/ppermute | solution.py:582
  6.4 6.7 %collective-permute-start.3 = (f32[56,128]{1,0:T(8,128)S(1)}, f32[56,128]{1,0:T(8,128)S(1)}, u32[]{:S(2)}, u32[]{:S(2)}) collective-permute-start(f32[56,128]{1,0:T(8,128)S(1)} %get-tuple-element.31), channel_id=1, source_target_pairs={{0,4},{4,8},{8,12},{12,16},{16,20},{20,24},{24,28},{28,0},{1,5},{5... | collective-permute-start | bytes 86024 | tf_op jit(solution)/shard_map/ppermute | solution.py:582
  8.0 7.1 %collective-permute-start.4 = (f32[224,128]{1,0:T(8,128)S(1)}, f32[224,128]{1,0:T(8,128)S(1)}, u32[]{:S(2)}, u32[]{:S(2)}) collective-permute-start(f32[224,128]{1,0:T(8,128)S(1)} %get-tuple-element.32), channel_id=1, source_target_pairs={{0,28},{4,0},{8,4},{12,8},{16,12},{20,16},{24,20},{28,24},{1,29},{... | collective-permute-start | bytes 344072 | tf_op jit(solution)/shard_map/ppermute | solution.py:582

commit v9 on v8

--- a/solution.py
+++ b/solution.py
@@ -282,7 +282,7 @@
     return keys + [(q, far) for q, c in enumerate(Q) if c[0] == side]
 
 
-REDUCED = (1,)
+REDUCED = (1, -1)
 
 
 def raw_count(side):
@@ -360,7 +360,12 @@
             for k in range(3):
                 sent[i, 2 * k + n] = t[a, x][n][k]
     turned = {(g, c): turn(halo[g], -c, 0) for g in range(2) for c in SIGNS}
-    for side, message in ((1, to_left), (-1, to_right)):
+    keys = sent_sums(rows)
+
+    def both(a, x, n):
+        return [sent[keys.index((a, x)), 2 * k + n] for k in range(3)]
+
+    def one_side(side, message):
         near, far = (0, 1) if side == 1 else (rows - 1, rows - 2)
         with_raw = side == 1
         at = 8 * FULL if with_raw else 0
@@ -370,8 +375,8 @@
         clear_end(message, (raw_height(side) if with_raw else 0) + small_height(side))
         extra = []
         for n in range(2):
-            row = list(t[-side, near][n])
-            still, moved = t[0, near][n], t[-side, far][n]
+            row = both(-side, near, n)
+            still, moved = both(0, near, n), both(-side, far, n)
             row += [still[0] + moved[0], moved[0] if side == -1 else -moved[0]]
             row += [still[1] + moved[1], still[2] + moved[2]]
             row.append(solid_in[near] if n == 0 else incoming(halo[table["w", near][0]], table["w", near][1], 0))
@@ -393,6 +398,9 @@
             i = used + 2 * k
             columns = jnp.where(by_two == i // 2, turn(extra[1][k], i + 1, 1), columns)
         message[at:at + 8] = columns
+
+    one_side(-1, to_right)
+    pl.when(lax.axis_index("gx") >= 0)(functools.partial(one_side, 1, to_left))
 
 
 def outer_rows(rows):
@@ -619,6 +627,10 @@
         functools.partial(middle_kernel, rows), "inner_rows",
         [(27, 2 * rows - 4) + tile, (27, 8) + tile, (4, 2 * rows + 4) + tile], [],
         (scale, cot, sums, solid, sent, merged))
+    def hold(source, target):
+        target[...] = source[...]
+
+    (raw_low,) = call(hold, "near_rows", [(padded(raw_height(-1)), width)], [], (raw_low,), work=1000000000)
     (done,) = call(
         functools.partial(low_kernel, rows), "low_rows",
         [(27, rows - 2) + tile], [pltpu.VMEM((27, 4) + tile, F32)],

time: 16.4 us -> 16.4 us (level)
    pallas_call x5 -> x6, Pallas kernels: 3.73 us -> 3.86 us  [call(): pl.pallas_call(kernel, out_shape=[jax.ShapeDtypeStruct(s, F32) for s in o...]
  transfers between devices with their start and end apart: 5 -> 5, of which waited for: 2 -> 2; matrix products, arithmetic and copies ran while one was open for 0% -> 0% of each run, Pallas kernels for 7% -> 8%
where the time goes in v9:
time: 16.4 us; the launch traced here: 16.3 us
  starting transfers between devices  9.41 us (57%)
  Pallas kernels  3.86 us (24%)
  waiting for transfers between devices  2.94 us (18%)
    ppermute x3, starting transfers between devices, ring(): lax.ppermute(block, axis, [(i, (i + step) % size) for i in range(size)])  6.27 us
    pallas_call x6, Pallas kernels, call(): pl.pallas_call(kernel, out_shape=[jax.ShapeDtypeStruct(s, F32) for s in o...  3.86 us
    ppermute x2, starting transfers between devices, swap(): return lax.ppermute(block, axis, route)  3.15 us
    ppermute x3, waiting for transfers between devices, ring(): lax.ppermute(block, axis, [(i, (i + step) % size) for i in range(size)])  2.93 us
  transfers between devices with their start and end apart: 5, of which 2 were waited for; matrix products, arithmetic and copies ran while one was open for 0% of the time, Pallas kernels for 8%

profile of v9, /device:TPU:0, one launch (start us, length us, event | category | flops | bytes accessed | tf_op | source)
XLA Modules:
  0.0 16.3 jit_solution(12185410801831200813)
XLA Ops:
  0.0 1.5 %collide.1 = (f32[27,32,128]{2,1,0:T(8,128)S(1)}, f32[27,8,128]{2,1,0:T(8,128)S(1)}, f32[18,4,8,128]{3,2,1,0:T(8,128)S(1)}, f32[3,4,8,128]{3,2,1,0:T(8,128)S(1)}...) custom-call(f32[27]{0:T(128)} %rates_in.1, f32[27,32,128]{2,1,0:T(8,128)} %bitcast.4, ...), custom_call_target="tpu_custom_call" | custom-call | tf_op jit(solution)/shard_map/collide/pallas_call | solution.py:576
  1.5 2.5 %collective-permute-start.1 = (f32[3,8,128]{2,1,0:T(8,128)S(1)}, f32[3,8,128]{2,1,0:T(8,128)S(1)}, u32[]{:S(2)}, u32[]{:S(2)}) collective-permute-start(f32[3,8,128]{2,1,0:T(8,128)S(1)} %get-tuple-element.24), channel_id=1, source_target_pairs={{1,2},{2,1},{3,0},{0,3},{5,6},{6,5},{7,4},{4,7},{9,10},{10,9},{11,... | collective-permute-start | bytes 36872 | tf_op jit(solution)/shard_map/ppermute | solution.py:598
  4.0 0.7 %collective-permute-start = (f32[3,8,128]{2,1,0:T(8,128)S(1)}, f32[3,8,128]{2,1,0:T(8,128)S(1)}, u32[]{:S(2)}, u32[]{:S(2)}) collective-permute-start(f32[3,8,128]{2,1,0:T(8,128)S(1)} %get-tuple-element.24), channel_id=1, source_target_pairs={{0,1},{1,0},{2,3},{3,2},{4,5},{5,4},{6,7},{7,6},{8,9},{9,8},{10,11... | collective-permute-start | bytes 36872 | tf_op jit(solution)/shard_map/ppermute | solution.py:598
  4.6 1.5 %collective-permute-start.2 = (f32[72,128]{1,0:T(8,128)S(1)}, f32[72,128]{1,0:T(8,128)S(1)}, u32[]{:S(2)}, u32[]{:S(2)}) collective-permute-start(f32[72,128]{1,0:T(8,128)S(1)} %get-tuple-element.30), channel_id=1, source_target_pairs={{0,4},{4,8},{8,12},{12,16},{16,20},{20,24},{24,28},{28,0},{1,5},{5... | collective-permute-start | bytes 110600 | tf_op jit(solution)/shard_map/ppermute | solution.py:590
  6.1 0.0 collective-permute-done.1
  6.1 0.0 collective-permute-done
  6.1 0.4 %pack.1 = (f32[224,128]{1,0:T(8,128)S(1)}, f32[152,128]{1,0:T(8,128)S(1)}, f32[6,6,8,128]{3,2,1,0:T(8,128)S(1)}, f32[3,8,128]{2,1,0:T(8,128)S(1)}) custom-call(f32[27,8,128]{2,1,0:T(8,128)S(1)} %get-tuple-element.19.scale_in, f32[27,32,128]{2,1,0:T(8,128)S(1)} %get-tuple-element.22.cot, f32[18,4,8,128]{3,2,1,0:T(8,128)S(1)} %get-tuple-element.23.sums, ...), custom_call_target="tpu_custom_call" | custom-call | tf_op jit(solution)/shard_map/pack/pallas_call | solution.py:576
  6.6 1.6 %collective-permute-start.3 = (f32[152,128]{1,0:T(8,128)S(1)}, f32[152,128]{1,0:T(8,128)S(1)}, u32[]{:S(2)}, u32[]{:S(2)}) collective-permute-start(f32[152,128]{1,0:T(8,128)S(1)} %get-tuple-element.31), channel_id=1, source_target_pairs={{0,4},{4,8},{8,12},{12,16},{16,20},{20,24},{24,28},{28,0},{1,5},{5... | collective-permute-start | bytes 233480 | tf_op jit(solution)/shard_map/ppermute | solution.py:590
  8.2 3.2 %collective-permute-start.4 = (f32[224,128]{1,0:T(8,128)S(1)}, f32[224,128]{1,0:T(8,128)S(1)}, u32[]{:S(2)}, u32[]{:S(2)}) collective-permute-start(f32[224,128]{1,0:T(8,128)S(1)} %get-tuple-element.32), channel_id=1, source_target_pairs={{0,28},{4,0},{8,4},{12,8},{16,12},{20,16},{24,20},{28,24},{1,29},{... | collective-permute-start | bytes 344072 | tf_op jit(solution)/shard_map/ppermute | solution.py:590
  11.4 0.5 %inner_rows.1 = (f32[27,4,8,128]{3,2,1,0:T(8,128)S(1)}, f32[27,8,8,128]{3,2,1,0:T(8,128)S(1)}, f32[4,12,8,128]{3,2,1,0:T(8,128)S(1)}) custom-call(f32[27,8,128]{2,1,0:T(8,128)S(1)} %get-tuple-element.19.scale_in, f32[27,32,128]{2,1,0:T(8,128)S(1)} %get-tuple-element.22.cot, f32[18,4,8,128]{3,2,1,0:T(8,128)S(1)} %get-tuple-element.23.sums, ...), custom_call_target="tpu_custom_call" | custom-call | tf_op jit(solution)/shard_map/inner_rows/pallas_call | solution.py:576
  11.8 0.0 collective-permute-done.2.source
  11.8 2.1 %collective-permute-done.3.extra = f32[152,128]{1,0:T(8,128)S(1)} collective-permute-done((f32[152,128]{1,0:T(8,128)S(1)}, f32[152,128]{1,0:T(8,128)S(1)}, u32[]{:S(2)}, u32[]{:S(2)}) %collective-permute-start.3) | collective-permute-done | bytes 77856 | tf_op jit(solution)/shard_map/ppermute | solution.py:590
  14.0 0.4 %low_rows.1.done = f32[27,2,8,128]{3,2,1,0:T(8,128)S(1)} custom-call(f32[27,8,128]{2,1,0:T(8,128)S(1)} %get-tuple-element.19.scale_in, f32[3,4,8,128]{3,2,1,0:T(8,128)S(1)} %get-tuple-element.20.speed, f32[4,8,128]{2,1,0:T(8,128)S(1)} %get-tuple-element.21.solid_in, f32[4,12,8,128]{3,2,1,0:T(8,128)S(1)} %get-tuple-element.27.own, ...), custom_call_target="tpu_custom_call" | custom-call | flops 2000000000 | tf_op jit(solution)/shard_map/low_rows/pallas_call | solution.py:576
  14.3 0.8 %collective-permute-done.4.from_high = f32[224,128]{1,0:T(8,128)S(1)} collective-permute-done((f32[224,128]{1,0:T(8,128)S(1)}, f32[224,128]{1,0:T(8,128)S(1)}, u32[]{:S(2)}, u32[]{:S(2)}) %collective-permute-start.4) | collective-permute-done | bytes 114720 | tf_op jit(solution)/shard_map/ppermute | solution.py:590
  15.1 1.1 %gradient.1 = f32[27,32,128]{2,1,0:T(8,128)} custom-call(f32[27,8,128]{2,1,0:T(8,128)S(1)} %get-tuple-element.19.scale_in, f32[3,4,8,128]{3,2,1,0:T(8,128)S(1)} %get-tuple-element.20.speed, f32[4,8,128]{2,1,0:T(8,128)S(1)} %get-tuple-element.21.solid_in, f32[4,12,8,128]{3,2,1,0:T(8,128)S(1)} %get-tuple-element.27.own, ...), custom_call_target="tpu_custom_call" | custom-call | tf_op jit(solution)/shard_map/gradient/pallas_call | solution.py:576
  (2 shorter events, 0.0 us)
Async XLA Ops:
  1.5 4.6 %collective-permute-start.1 = (f32[3,8,128]{2,1,0:T(8,128)S(1)}, f32[3,8,128]{2,1,0:T(8,128)S(1)}, u32[]{:S(2)}, u32[]{:S(2)}) collective-permute-start(f32[3,8,128]{2,1,0:T(8,128)S(1)} %get-tuple-element.24), channel_id=1, source_target_pairs={{1,2},{2,1},{3,0},{0,3},{5,6},{6,5},{7,4},{4,7},{9,10},{10,9},{11,... | collective-permute-start | bytes 36872 | tf_op jit(solution)/shard_map/ppermute | solution.py:598
  4.0 2.2 %collective-permute-start = (f32[3,8,128]{2,1,0:T(8,128)S(1)}, f32[3,8,128]{2,1,0:T(8,128)S(1)}, u32[]{:S(2)}, u32[]{:S(2)}) collective-permute-start(f32[3,8,128]{2,1,0:T(8,128)S(1)} %get-tuple-element.24), channel_id=1, source_target_pairs={{0,1},{1,0},{2,3},{3,2},{4,5},{5,4},{6,7},{7,6},{8,9},{9,8},{10,11... | collective-permute-start | bytes 36872 | tf_op jit(solution)/shard_map/ppermute | solution.py:598
  4.6 7.2 %collective-permute-start.2 = (f32[72,128]{1,0:T(8,128)S(1)}, f32[72,128]{1,0:T(8,128)S(1)}, u32[]{:S(2)}, u32[]{:S(2)}) collective-permute-start(f32[72,128]{1,0:T(8,128)S(1)} %get-tuple-element.30), channel_id=1, source_target_pairs={{0,4},{4,8},{8,12},{12,16},{16,20},{20,24},{24,28},{28,0},{1,5},{5... | collective-permute-start | bytes 110600 | tf_op jit(solution)/shard_map/ppermute | solution.py:590
  6.6 7.4 %collective-permute-start.3 = (f32[152,128]{1,0:T(8,128)S(1)}, f32[152,128]{1,0:T(8,128)S(1)}, u32[]{:S(2)}, u32[]{:S(2)}) collective-permute-start(f32[152,128]{1,0:T(8,128)S(1)} %get-tuple-element.31), channel_id=1, source_target_pairs={{0,4},{4,8},{8,12},{12,16},{16,20},{20,24},{24,28},{28,0},{1,5},{5... | collective-permute-start | bytes 233480 | tf_op jit(solution)/shard_map/ppermute | solution.py:590
  8.2 6.9 %collective-permute-start.4 = (f32[224,128]{1,0:T(8,128)S(1)}, f32[224,128]{1,0:T(8,128)S(1)}, u32[]{:S(2)}, u32[]{:S(2)}) collective-permute-start(f32[224,128]{1,0:T(8,128)S(1)} %get-tuple-element.32), channel_id=1, source_target_pairs={{0,28},{4,0},{8,4},{12,8},{16,12},{20,16},{24,20},{28,24},{1,29},{... | collective-permute-start | bytes 344072 | tf_op jit(solution)/shard_map/ppermute | solution.py:590

commit v10 on v8

--- a/solution.py
+++ b/solution.py
@@ -59,6 +59,10 @@
 def turn(v, shift, axis):
     shift = shift % v.shape[axis]
     return v if shift == 0 else pltpu.roll(v, shift, axis)
+
+
+def region(body):
+    pl.when(lax.axis_index("gx") >= 0)(body)
 
 
 def lanes():
@@ -261,7 +265,7 @@
     quads, singles, _ = layout(rows)
     by_two, by_four = lane >> 1, lane >> 2
     high_lanes = lane >= 64
-    for g in range(3):
+    def pack(g):
         piece = jnp.zeros((8, 128), F32)
         for n, (low, high) in enumerate(quads[g]):
             both = jnp.where(high_lanes, block(low), block(high))
@@ -270,6 +274,9 @@
             i = 4 * len(quads[g]) + 2 * n
             piece = jnp.where(by_two == i // 2, turn(block(key), i + 1, 1), piece)
         packed[g] = piece
+
+    for g in range(3):
+        region(functools.partial(pack, g))
 
 
 FULL = 9
@@ -517,18 +524,20 @@
                     g1[q, 2 * (j % 2) + n] = g[q]
 
 
-def pulled_row(rows, x, arrays, speed, solid_in, scale, lane):
-    v = []
-    for q, (a, b, c) in enumerate(Q):
-        array, r = arrays(x + a)
-        main = array[q, r]
-        if b:
-            main = shift_y(main, turn(array[q, r + 1], -b, 1), b, lane)[0]
-        v.append(turn(main, -c, 0))
-    return pull_back_parts(v, [speed[k, x] for k in range(3)], solid_in[x] > 0.5, scale)
-
-
-def low_kernel(rows, scale_in, speed, solid_in, own, merged, inner, known, raw, extra, done, g1):
+def pulled(rows, x, q, arrays, lane):
+    a, b, c = Q[q]
+    array, r = arrays(x + a)
+    main = array[q, r]
+    if b:
+        main = shift_y(main, turn(array[q, r + 1], -b, 1), b, lane)[0]
+    return turn(main, -c, 0)
+
+
+def early_keys(rows):
+    return [(q, x) for x in range(rows - 2, rows) for q in range(27) if 0 < x + Q[q][0] < rows - 1]
+
+
+def low_kernel(rows, scale_in, speed, solid_in, own, merged, inner, known, raw, extra, done, ready, g1):
     scale = [scale_in[i] for i in range(27)]
     lane = lanes()
     outer_gradient(rows, -1, scale, solid_in, own, merged, known, raw, 0, extra, 0, 8, g1)
@@ -537,20 +546,26 @@
         return (g1, 2 * (x + 1)) if x < 1 else (inner, 2 * (x - 1))
 
     for x in range(rows - 2):
-        for a, part in enumerate(pulled_row(rows, x, arrays, speed, solid_in, scale, lane)):
-            for i, value in enumerate(part):
-                done[9 * a + i, x] = value
-
-
-def last_kernel(rows, scale_in, speed, solid_in, own, merged, inner, known, done, from_high, out_hbm, high, out, sems):
+        v = [pulled(rows, x, q, arrays, lane) for q in range(27)]
+        for q, value in enumerate(pull_back(v, [speed[k, x] for k in range(3)], solid_in[x] > 0.5, scale)):
+            done[q, x] = value
+    for i, (q, x) in enumerate(early_keys(rows)):
+        ready[i] = pulled(rows, x, q, arrays, lane)
+
+
+def last_kernel(rows, scale_in, speed, solid_in, own, merged, known, done, ready, from_high, out_hbm, high, out, sems):
     scale = [scale_in[i] for i in range(27)]
     lane = lanes()
     outer_gradient(rows, 1, scale, solid_in, own, merged, known, from_high, 8, from_high, 8 * FULL, raw_height(1) + 8, high)
 
     def arrays(x):
-        return (inner, 2 * (x - 1)) if x < rows - 1 else (high, 2 * (x - rows + 1))
-
-    late = {x: pulled_row(rows, x, arrays, speed, solid_in, scale, lane) for x in range(rows - 2, rows)}
+        return high, 2 * (x - rows + 1)
+
+    keys = early_keys(rows)
+    late = {}
+    for x in range(rows - 2, rows):
+        v = [ready[keys.index((q, x))] if (q, x) in keys else pulled(rows, x, q, arrays, lane) for q in range(27)]
+        late[x] = pull_back_parts(v, [speed[k, x] for k in range(3)], solid_in[x] > 0.5, scale)
     copies = []
     for a in range(3):
         for x in range(rows):
@@ -619,15 +634,15 @@
         functools.partial(middle_kernel, rows), "inner_rows",
         [(27, 2 * rows - 4) + tile, (27, 8) + tile, (4, 2 * rows + 4) + tile], [],
         (scale, cot, sums, solid, sent, merged))
-    (done,) = call(
+    done, ready = call(
         functools.partial(low_kernel, rows), "low_rows",
-        [(27, rows - 2) + tile], [pltpu.VMEM((27, 4) + tile, F32)],
+        [(27, rows - 2) + tile, (len(early_keys(rows)),) + tile], [pltpu.VMEM((27, 4) + tile, F32)],
         (scale, speed, solid, own, merged, inner, known, raw_low, small_low), work=2000000000)
     (out,) = call(
         functools.partial(last_kernel, rows), "gradient",
         [lattice],
         [pltpu.VMEM((27, 4) + tile, F32), pltpu.VMEM(lattice, F32), pltpu.SemaphoreType.DMA((3,))],
-        (scale, speed, solid, own, merged, inner, known, done, from_high), out_space=pltpu.HBM)
+        (scale, speed, solid, own, merged, known, done, ready, from_high), out_space=pltpu.HBM)
     return out.reshape(checkpoint.shape)
 
 

time: 16.4 us -> 16.4 us (level)
  no operation moved by 1% of the time
where the time goes in v10:
time: 16.4 us; the launch traced here: 16.3 us
  starting transfers between devices  9.41 us (57%)
  Pallas kernels  3.71 us (23%)
  waiting for transfers between devices  3.11 us (19%)
    ppermute x3, starting transfers between devices, ring(): lax.ppermute(block, axis, [(i, (i + step) % size) for i in range(size)])  6.27 us
    pallas_call x5, Pallas kernels, call(): pl.pallas_call(kernel, out_shape=[jax.ShapeDtypeStruct(s, F32) for s in o...  3.71 us
    ppermute x2, starting transfers between devices, swap(): return lax.ppermute(block, axis, route)  3.15 us
    ppermute x3, waiting for transfers between devices, ring(): lax.ppermute(block, axis, [(i, (i + step) % size) for i in range(size)])  3.1 us
  transfers between devices with their start and end apart: 5, of which 2 were waited for; matrix products, arithmetic and copies ran while one was open for 0% of the time, Pallas kernels for 7%

profile of v10, /device:TPU:0, one launch (start us, length us, event | category | flops | bytes accessed | tf_op | source)
XLA Modules:
  0.0 16.3 jit_solution(16678732764183476826)
XLA Ops:
  0.0 1.5 %collide.1 = (f32[27,32,128]{2,1,0:T(8,128)S(1)}, f32[27,8,128]{2,1,0:T(8,128)S(1)}, f32[18,4,8,128]{3,2,1,0:T(8,128)S(1)}, f32[3,4,8,128]{3,2,1,0:T(8,128)S(1)}...) custom-call(f32[27]{0:T(128)} %rates_in.1, f32[27,32,128]{2,1,0:T(8,128)} %bitcast.4, ...), custom_call_target="tpu_custom_call" | custom-call | tf_op jit(solution)/shard_map/collide/pallas_call | solution.py:583
  1.5 2.5 %collective-permute-start.1 = (f32[3,8,128]{2,1,0:T(8,128)S(1)}, f32[3,8,128]{2,1,0:T(8,128)S(1)}, u32[]{:S(2)}, u32[]{:S(2)}) collective-permute-start(f32[3,8,128]{2,1,0:T(8,128)S(1)} %get-tuple-element.26), channel_id=1, source_target_pairs={{1,2},{2,1},{3,0},{0,3},{5,6},{6,5},{7,4},{4,7},{9,10},{10,9},{11,... | collective-permute-start | bytes 36872 | tf_op jit(solution)/shard_map/ppermute | solution.py:605
  4.0 0.7 %collective-permute-start = (f32[3,8,128]{2,1,0:T(8,128)S(1)}, f32[3,8,128]{2,1,0:T(8,128)S(1)}, u32[]{:S(2)}, u32[]{:S(2)}) collective-permute-start(f32[3,8,128]{2,1,0:T(8,128)S(1)} %get-tuple-element.26), channel_id=1, source_target_pairs={{0,1},{1,0},{2,3},{3,2},{4,5},{5,4},{6,7},{7,6},{8,9},{9,8},{10,11... | collective-permute-start | bytes 36872 | tf_op jit(solution)/shard_map/ppermute | solution.py:605
  4.7 1.5 %collective-permute-start.2 = (f32[184,128]{1,0:T(8,128)S(1)}, f32[184,128]{1,0:T(8,128)S(1)}, u32[]{:S(2)}, u32[]{:S(2)}) collective-permute-start(f32[184,128]{1,0:T(8,128)S(1)} %get-tuple-element.32), channel_id=1, source_target_pairs={{0,4},{4,8},{8,12},{12,16},{16,20},{20,24},{24,28},{28,0},{1,5},{5... | collective-permute-start | bytes 282632 | tf_op jit(solution)/shard_map/ppermute | solution.py:597
  6.1 0.0 collective-permute-done.1
  6.1 0.0 collective-permute-done
  6.2 0.2 %pack.1 = (f32[224,128]{1,0:T(8,128)S(1)}, f32[56,128]{1,0:T(8,128)S(1)}, f32[6,6,8,128]{3,2,1,0:T(8,128)S(1)}, f32[3,8,128]{2,1,0:T(8,128)S(1)}) custom-call(f32[27,8,128]{2,1,0:T(8,128)S(1)} %get-tuple-element.21.scale_in, f32[27,32,128]{2,1,0:T(8,128)S(1)} %get-tuple-element.24.cot, f32[18,4,8,128]{3,2,1,0:T(8,128)S(1)} %get-tuple-element.25.sums, ...), custom_call_target="tpu_custom_call" | custom-call | tf_op jit(solution)/shard_map/pack/pallas_call | solution.py:583
  6.4 1.6 %collective-permute-start.3 = (f32[56,128]{1,0:T(8,128)S(1)}, f32[56,128]{1,0:T(8,128)S(1)}, u32[]{:S(2)}, u32[]{:S(2)}) collective-permute-start(f32[56,128]{1,0:T(8,128)S(1)} %get-tuple-element.33), channel_id=1, source_target_pairs={{0,4},{4,8},{8,12},{12,16},{16,20},{20,24},{24,28},{28,0},{1,5},{5... | collective-permute-start | bytes 86024 | tf_op jit(solution)/shard_map/ppermute | solution.py:597
  8.0 3.2 %collective-permute-start.4 = (f32[224,128]{1,0:T(8,128)S(1)}, f32[224,128]{1,0:T(8,128)S(1)}, u32[]{:S(2)}, u32[]{:S(2)}) collective-permute-start(f32[224,128]{1,0:T(8,128)S(1)} %get-tuple-element.36), channel_id=1, source_target_pairs={{0,28},{4,0},{8,4},{12,8},{16,12},{20,16},{24,20},{28,24},{1,29},{... | collective-permute-start | bytes 344072 | tf_op jit(solution)/shard_map/ppermute | solution.py:597
  11.2 0.5 %inner_rows.1 = (f32[27,4,8,128]{3,2,1,0:T(8,128)S(1)}, f32[27,8,8,128]{3,2,1,0:T(8,128)S(1)}, f32[4,12,8,128]{3,2,1,0:T(8,128)S(1)}) custom-call(f32[27,8,128]{2,1,0:T(8,128)S(1)} %get-tuple-element.21.scale_in, f32[27,32,128]{2,1,0:T(8,128)S(1)} %get-tuple-element.24.cot, f32[18,4,8,128]{3,2,1,0:T(8,128)S(1)} %get-tuple-element.25.sums, ...), custom_call_target="tpu_custom_call" | custom-call | tf_op jit(solution)/shard_map/inner_rows/pallas_call | solution.py:583
  11.6 1.4 %collective-permute-done.3.extra = f32[56,128]{1,0:T(8,128)S(1)} collective-permute-done((f32[56,128]{1,0:T(8,128)S(1)}, f32[56,128]{1,0:T(8,128)S(1)}, u32[]{:S(2)}, u32[]{:S(2)}) %collective-permute-start.3) | collective-permute-done | bytes 28704 | tf_op jit(solution)/shard_map/ppermute | solution.py:597
  13.1 0.0 collective-permute-done.2.raw
  13.1 0.4 %low_rows.1 = (f32[27,2,8,128]{3,2,1,0:T(8,128)S(1)}, f32[27,8,128]{2,1,0:T(8,128)S(1)}) custom-call(f32[27,8,128]{2,1,0:T(8,128)S(1)} %get-tuple-element.21.scale_in, f32[3,4,8,128]{3,2,1,0:T(8,128)S(1)} %get-tuple-element.22.speed, f32[4,8,128]{2,1,0:T(8,128)S(1)} %get-tuple-element.23.solid_in, f32[4,12,8,128]{3,2,1,0:T(8,128)S(1)} %get-tuple-element.29.own, ...), custom_call_target="tpu_custom_call" | custom-call | flops 2000000000 | tf_op jit(solution)/shard_map/low_rows/pallas_call | solution.py:583
  13.5 1.7 %collective-permute-done.4.from_high = f32[224,128]{1,0:T(8,128)S(1)} collective-permute-done((f32[224,128]{1,0:T(8,128)S(1)}, f32[224,128]{1,0:T(8,128)S(1)}, u32[]{:S(2)}, u32[]{:S(2)}) %collective-permute-start.4) | collective-permute-done | bytes 114720 | tf_op jit(solution)/shard_map/ppermute | solution.py:597
  15.1 1.1 %gradient.1 = f32[27,32,128]{2,1,0:T(8,128)} custom-call(f32[27,8,128]{2,1,0:T(8,128)S(1)} %get-tuple-element.21.scale_in, f32[3,4,8,128]{3,2,1,0:T(8,128)S(1)} %get-tuple-element.22.speed, f32[4,8,128]{2,1,0:T(8,128)S(1)} %get-tuple-element.23.solid_in, f32[4,12,8,128]{3,2,1,0:T(8,128)S(1)} %get-tuple-element.29.own, ...), custom_call_target="tpu_custom_call" | custom-call | tf_op jit(solution)/shard_map/gradient/pallas_call | solution.py:583
  (1 shorter events, 0.0 us)
Async XLA Ops:
  1.5 4.6 %collective-permute-start.1 = (f32[3,8,128]{2,1,0:T(8,128)S(1)}, f32[3,8,128]{2,1,0:T(8,128)S(1)}, u32[]{:S(2)}, u32[]{:S(2)}) collective-permute-start(f32[3,8,128]{2,1,0:T(8,128)S(1)} %get-tuple-element.26), channel_id=1, source_target_pairs={{1,2},{2,1},{3,0},{0,3},{5,6},{6,5},{7,4},{4,7},{9,10},{10,9},{11,... | collective-permute-start | bytes 36872 | tf_op jit(solution)/shard_map/ppermute | solution.py:605
  4.0 2.2 %collective-permute-start = (f32[3,8,128]{2,1,0:T(8,128)S(1)}, f32[3,8,128]{2,1,0:T(8,128)S(1)}, u32[]{:S(2)}, u32[]{:S(2)}) collective-permute-start(f32[3,8,128]{2,1,0:T(8,128)S(1)} %get-tuple-element.26), channel_id=1, source_target_pairs={{0,1},{1,0},{2,3},{3,2},{4,5},{5,4},{6,7},{7,6},{8,9},{9,8},{10,11... | collective-permute-start | bytes 36872 | tf_op jit(solution)/shard_map/ppermute | solution.py:605
  4.7 8.4 %collective-permute-start.2 = (f32[184,128]{1,0:T(8,128)S(1)}, f32[184,128]{1,0:T(8,128)S(1)}, u32[]{:S(2)}, u32[]{:S(2)}) collective-permute-start(f32[184,128]{1,0:T(8,128)S(1)} %get-tuple-element.32), channel_id=1, source_target_pairs={{0,4},{4,8},{8,12},{12,16},{16,20},{20,24},{24,28},{28,0},{1,5},{5... | collective-permute-start | bytes 282632 | tf_op jit(solution)/shard_map/ppermute | solution.py:597
  6.4 6.7 %collective-permute-start.3 = (f32[56,128]{1,0:T(8,128)S(1)}, f32[56,128]{1,0:T(8,128)S(1)}, u32[]{:S(2)}, u32[]{:S(2)}) collective-permute-start(f32[56,128]{1,0:T(8,128)S(1)} %get-tuple-element.33), channel_id=1, source_target_pairs={{0,4},{4,8},{8,12},{12,16},{16,20},{20,24},{24,28},{28,0},{1,5},{5... | collective-permute-start | bytes 86024 | tf_op jit(solution)/shard_map/ppermute | solution.py:597
  8.0 7.1 %collective-permute-start.4 = (f32[224,128]{1,0:T(8,128)S(1)}, f32[224,128]{1,0:T(8,128)S(1)}, u32[]{:S(2)}, u32[]{:S(2)}) collective-permute-start(f32[224,128]{1,0:T(8,128)S(1)} %get-tuple-element.36), channel_id=1, source_target_pairs={{0,28},{4,0},{8,4},{12,8},{16,12},{20,16},{24,20},{28,24},{1,29},{... | collective-permute-start | bytes 344072 | tf_op jit(solution)/shard_map/ppermute | solution.py:597

commit v11 on v8

--- a/solution.py
+++ b/solution.py
@@ -282,7 +282,7 @@
     return keys + [(q, far) for q, c in enumerate(Q) if c[0] == side]
 
 
-REDUCED = (1,)
+REDUCED = (-1,)
 
 
 def raw_count(side):
@@ -619,6 +619,10 @@
         functools.partial(middle_kernel, rows), "inner_rows",
         [(27, 2 * rows - 4) + tile, (27, 8) + tile, (4, 2 * rows + 4) + tile], [],
         (scale, cot, sums, solid, sent, merged))
+    def hold(source, target):
+        target[...] = source[...]
+
+    (raw_low,) = call(hold, "hold", [(padded(raw_height(-1)), width)], [], (raw_low,), work=1000000000)
     (done,) = call(
         functools.partial(low_kernel, rows), "low_rows",
         [(27, rows - 2) + tile], [pltpu.VMEM((27, 4) + tile, F32)],

time: 16.4 us -> 16.4 us (level)
    pallas_call x5 -> x6, Pallas kernels: 3.73 us -> 3.73 us  [call(): pl.pallas_call(kernel, out_shape=[jax.ShapeDtypeStruct(s, F32) for s in o...]
  transfers between devices with their start and end apart: 5 -> 5, of which waited for: 2 -> 2; matrix products, arithmetic and copies ran while one was open for 0% -> 0% of each run, Pallas kernels for 7% -> 6%
where the time goes in v11:
time: 16.4 us; the launch traced here: 16.3 us
  starting transfers between devices  9.41 us (57%)
  Pallas kernels  3.73 us (23%)
  waiting for transfers between devices  3.12 us (19%)
    ppermute x3, starting transfers between devices, ring(): lax.ppermute(block, axis, [(i, (i + step) % size) for i in range(size)])  6.27 us
    pallas_call x6, Pallas kernels, call(): pl.pallas_call(kernel, out_shape=[jax.ShapeDtypeStruct(s, F32) for s in o...  3.73 us
    ppermute x2, starting transfers between devices, swap(): return lax.ppermute(block, axis, route)  3.15 us
    ppermute x3, waiting for transfers between devices, ring(): lax.ppermute(block, axis, [(i, (i + step) % size) for i in range(size)])  3.11 us
  transfers between devices with their start and end apart: 5, of which 2 were waited for; matrix products, arithmetic and copies ran while one was open for 0% of the time, Pallas kernels for 6%

profile of v11, /device:TPU:0, one launch (start us, length us, event | category | flops | bytes accessed | tf_op | source)
XLA Modules:
  0.0 16.3 jit_solution(18129895003973106327)
XLA Ops:
  0.0 1.5 %collide.1 = (f32[27,32,128]{2,1,0:T(8,128)S(1)}, f32[27,8,128]{2,1,0:T(8,128)S(1)}, f32[18,4,8,128]{3,2,1,0:T(8,128)S(1)}, f32[3,4,8,128]{3,2,1,0:T(8,128)S(1)}...) custom-call(f32[27]{0:T(128)} %rates_in.1, f32[27,32,128]{2,1,0:T(8,128)} %bitcast.4, ...), custom_call_target="tpu_custom_call" | custom-call | tf_op jit(solution)/shard_map/collide/pallas_call | solution.py:568
  1.5 2.5 %collective-permute-start.1 = (f32[3,8,128]{2,1,0:T(8,128)S(1)}, f32[3,8,128]{2,1,0:T(8,128)S(1)}, u32[]{:S(2)}, u32[]{:S(2)}) collective-permute-start(f32[3,8,128]{2,1,0:T(8,128)S(1)} %get-tuple-element.24), channel_id=1, source_target_pairs={{1,2},{2,1},{3,0},{0,3},{5,6},{6,5},{7,4},{4,7},{9,10},{10,9},{11,... | collective-permute-start | bytes 36872 | tf_op jit(solution)/shard_map/ppermute | solution.py:590
  4.0 0.7 %collective-permute-start = (f32[3,8,128]{2,1,0:T(8,128)S(1)}, f32[3,8,128]{2,1,0:T(8,128)S(1)}, u32[]{:S(2)}, u32[]{:S(2)}) collective-permute-start(f32[3,8,128]{2,1,0:T(8,128)S(1)} %get-tuple-element.24), channel_id=1, source_target_pairs={{0,1},{1,0},{2,3},{3,2},{4,5},{5,4},{6,7},{7,6},{8,9},{9,8},{10,11... | collective-permute-start | bytes 36872 | tf_op jit(solution)/shard_map/ppermute | solution.py:590
  4.6 1.5 %collective-permute-start.2 = (f32[72,128]{1,0:T(8,128)S(1)}, f32[72,128]{1,0:T(8,128)S(1)}, u32[]{:S(2)}, u32[]{:S(2)}) collective-permute-start(f32[72,128]{1,0:T(8,128)S(1)} %get-tuple-element.30), channel_id=1, source_target_pairs={{0,4},{4,8},{8,12},{12,16},{16,20},{20,24},{24,28},{28,0},{1,5},{5... | collective-permute-start | bytes 110600 | tf_op jit(solution)/shard_map/ppermute | solution.py:582
  6.1 0.0 collective-permute-done.1
  6.1 0.0 collective-permute-done
  6.1 0.2 %pack.1 = (f32[240,128]{1,0:T(8,128)S(1)}, f32[152,128]{1,0:T(8,128)S(1)}, f32[6,6,8,128]{3,2,1,0:T(8,128)S(1)}, f32[3,8,128]{2,1,0:T(8,128)S(1)}) custom-call(f32[27,8,128]{2,1,0:T(8,128)S(1)} %get-tuple-element.19.scale_in, f32[27,32,128]{2,1,0:T(8,128)S(1)} %get-tuple-element.22.cot, f32[18,4,8,128]{3,2,1,0:T(8,128)S(1)} %get-tuple-element.23.sums, ...), custom_call_target="tpu_custom_call" | custom-call | tf_op jit(solution)/shard_map/pack/pallas_call | solution.py:568
  6.4 1.6 %collective-permute-start.3 = (f32[152,128]{1,0:T(8,128)S(1)}, f32[152,128]{1,0:T(8,128)S(1)}, u32[]{:S(2)}, u32[]{:S(2)}) collective-permute-start(f32[152,128]{1,0:T(8,128)S(1)} %get-tuple-element.31), channel_id=1, source_target_pairs={{0,4},{4,8},{8,12},{12,16},{16,20},{20,24},{24,28},{28,0},{1,5},{5... | collective-permute-start | bytes 233480 | tf_op jit(solution)/shard_map/ppermute | solution.py:582
  8.0 3.2 %collective-permute-start.4 = (f32[240,128]{1,0:T(8,128)S(1)}, f32[240,128]{1,0:T(8,128)S(1)}, u32[]{:S(2)}, u32[]{:S(2)}) collective-permute-start(f32[240,128]{1,0:T(8,128)S(1)} %get-tuple-element.32), channel_id=1, source_target_pairs={{0,28},{4,0},{8,4},{12,8},{16,12},{20,16},{24,20},{28,24},{1,29},{... | collective-permute-start | bytes 368648 | tf_op jit(solution)/shard_map/ppermute | solution.py:582
  11.2 0.5 %inner_rows.1 = (f32[27,4,8,128]{3,2,1,0:T(8,128)S(1)}, f32[27,8,8,128]{3,2,1,0:T(8,128)S(1)}, f32[4,12,8,128]{3,2,1,0:T(8,128)S(1)}) custom-call(f32[27,8,128]{2,1,0:T(8,128)S(1)} %get-tuple-element.19.scale_in, f32[27,32,128]{2,1,0:T(8,128)S(1)} %get-tuple-element.22.cot, f32[18,4,8,128]{3,2,1,0:T(8,128)S(1)} %get-tuple-element.23.sums, ...), custom_call_target="tpu_custom_call" | custom-call | tf_op jit(solution)/shard_map/inner_rows/pallas_call | solution.py:568
  11.6 0.0 collective-permute-done.2.source
  11.6 2.1 %collective-permute-done.3.extra = f32[152,128]{1,0:T(8,128)S(1)} collective-permute-done((f32[152,128]{1,0:T(8,128)S(1)}, f32[152,128]{1,0:T(8,128)S(1)}, u32[]{:S(2)}, u32[]{:S(2)}) %collective-permute-start.3) | collective-permute-done | bytes 77856 | tf_op jit(solution)/shard_map/ppermute | solution.py:582
  13.8 0.4 %low_rows.1.done = f32[27,2,8,128]{3,2,1,0:T(8,128)S(1)} custom-call(f32[27,8,128]{2,1,0:T(8,128)S(1)} %get-tuple-element.19.scale_in, f32[3,4,8,128]{3,2,1,0:T(8,128)S(1)} %get-tuple-element.20.speed, f32[4,8,128]{2,1,0:T(8,128)S(1)} %get-tuple-element.21.solid_in, f32[4,12,8,128]{3,2,1,0:T(8,128)S(1)} %get-tuple-element.27.own, ...), custom_call_target="tpu_custom_call" | custom-call | flops 2000000000 | tf_op jit(solution)/shard_map/low_rows/pallas_call | solution.py:568
  14.1 1.0 %collective-permute-done.4.from_high = f32[240,128]{1,0:T(8,128)S(1)} collective-permute-done((f32[240,128]{1,0:T(8,128)S(1)}, f32[240,128]{1,0:T(8,128)S(1)}, u32[]{:S(2)}, u32[]{:S(2)}) %collective-permute-start.4) | collective-permute-done | bytes 122912 | tf_op jit(solution)/shard_map/ppermute | solution.py:582
  15.1 1.2 %gradient.1 = f32[27,32,128]{2,1,0:T(8,128)} custom-call(f32[27,8,128]{2,1,0:T(8,128)S(1)} %get-tuple-element.19.scale_in, f32[3,4,8,128]{3,2,1,0:T(8,128)S(1)} %get-tuple-element.20.speed, f32[4,8,128]{2,1,0:T(8,128)S(1)} %get-tuple-element.21.solid_in, f32[4,12,8,128]{3,2,1,0:T(8,128)S(1)} %get-tuple-element.27.own, ...), custom_call_target="tpu_custom_call" | custom-call | tf_op jit(solution)/shard_map/gradient/pallas_call | solution.py:568
  (2 shorter events, 0.0 us)
Async XLA Ops:
  1.5 4.6 %collective-permute-start.1 = (f32[3,8,128]{2,1,0:T(8,128)S(1)}, f32[3,8,128]{2,1,0:T(8,128)S(1)}, u32[]{:S(2)}, u32[]{:S(2)}) collective-permute-start(f32[3,8,128]{2,1,0:T(8,128)S(1)} %get-tuple-element.24), channel_id=1, source_target_pairs={{1,2},{2,1},{3,0},{0,3},{5,6},{6,5},{7,4},{4,7},{9,10},{10,9},{11,... | collective-permute-start | bytes 36872 | tf_op jit(solution)/shard_map/ppermute | solution.py:590
  4.0 2.2 %collective-permute-start = (f32[3,8,128]{2,1,0:T(8,128)S(1)}, f32[3,8,128]{2,1,0:T(8,128)S(1)}, u32[]{:S(2)}, u32[]{:S(2)}) collective-permute-start(f32[3,8,128]{2,1,0:T(8,128)S(1)} %get-tuple-element.24), channel_id=1, source_target_pairs={{0,1},{1,0},{2,3},{3,2},{4,5},{5,4},{6,7},{7,6},{8,9},{9,8},{10,11... | collective-permute-start | bytes 36872 | tf_op jit(solution)/shard_map/ppermute | solution.py:590
  4.6 7.0 %collective-permute-start.2 = (f32[72,128]{1,0:T(8,128)S(1)}, f32[72,128]{1,0:T(8,128)S(1)}, u32[]{:S(2)}, u32[]{:S(2)}) collective-permute-start(f32[72,128]{1,0:T(8,128)S(1)} %get-tuple-element.30), channel_id=1, source_target_pairs={{0,4},{4,8},{8,12},{12,16},{16,20},{20,24},{24,28},{28,0},{1,5},{5... | collective-permute-start | bytes 110600 | tf_op jit(solution)/shard_map/ppermute | solution.py:582
  6.4 7.4 %collective-permute-start.3 = (f32[152,128]{1,0:T(8,128)S(1)}, f32[152,128]{1,0:T(8,128)S(1)}, u32[]{:S(2)}, u32[]{:S(2)}) collective-permute-start(f32[152,128]{1,0:T(8,128)S(1)} %get-tuple-element.31), channel_id=1, source_target_pairs={{0,4},{4,8},{8,12},{12,16},{16,20},{20,24},{24,28},{28,0},{1,5},{5... | collective-permute-start | bytes 233480 | tf_op jit(solution)/shard_map/ppermute | solution.py:582
  8.0 7.1 %collective-permute-start.4 = (f32[240,128]{1,0:T(8,128)S(1)}, f32[240,128]{1,0:T(8,128)S(1)}, u32[]{:S(2)}, u32[]{:S(2)}) collective-permute-start(f32[240,128]{1,0:T(8,128)S(1)} %get-tuple-element.32), channel_id=1, source_target_pairs={{0,28},{4,0},{8,4},{12,8},{16,12},{20,16},{24,20},{28,24},{1,29},{... | collective-permute-start | bytes 368648 | tf_op jit(solution)/shard_map/ppermute | solution.py:582
